TPU v7x, 512 devices: a whole 4x8x8 slice. The times are simulated.
512 devices in a mesh: seq: 32 (over x, z), tp: 16 (over y, core).
Axes of the slice: x: 4, y: 8, z: 8, core: 2. Of those that a mesh axis runs over, the one named last changes fastest.
Arguments:
- joined: bfloat16 [4096, 14336], P('seq', 'tp')
- gain: float32 [14336], P('tp'), may hold values from 0.25 to 1.75
- weight_codes: bfloat16 [7168, 14336], P('seq', 'tp'), may hold values from -0.046875 to 0.046875
- scale_exp: int32 [7168, 112], P('seq', 'tp'), may hold values from -2 to 1
- cotangent: bfloat16 [4096, 7168], P('tp', 'seq'), may hold values from -6 to 6
Outputs:
- projected: bfloat16 [4096, 7168], P('tp', 'seq')
- joined_gradient: bfloat16 [4096, 14336], P('seq', 'tp')
- weight_grad: float32 [7168, 14336], P('seq', 'tp')
All inputs are finite; a program needn't handle non-finite values.
Results may differ from a plain program's by a relative error of at most 0.0057.
Values may be sent and summed in bfloat16 or wider, within the bound.
No kernel may reach another device: no remote copies, remote signals or barrier semaphores. Data moves between devices by JAX's collectives and lax.ppermute only.
A program may use at most 128 MiB of HBM per device.

v0:
```python
import jax
import jax.numpy as jnp
from jax import lax
from jax.sharding import PartitionSpec as P

MODEL_WIDTH = 7168
BLOCK = 128


eps = 1e-06


def half_partial_sums(value_entries, second_half_rows):
    local = jnp.sum(value_entries, axis=1)
    zeros = jnp.zeros_like(local)
    first = jnp.where(second_half_rows, zeros, local)
    second = jnp.where(second_half_rows, local, zeros)
    return jnp.stack([first, second], axis=1)


def pick_half(totals, second_half_rows):
    return jnp.where(second_half_rows, totals[:, 1], totals[:, 0])[:, None]


def input_gradient(cotangent, weight):
    gathered = lax.all_gather(cotangent, "tp", axis=0, tiled=True)
    back = jnp.dot(gathered, weight, preferred_element_type=jnp.float32).astype(jnp.bfloat16)
    total_rows = back.shape[0]
    moved = lax.all_to_all(
        back.reshape(1, total_rows, back.shape[1]), "seq", split_axis=1, concat_axis=0, tiled=True
    )
    return (gathered, jnp.sum(moved.astype(jnp.float32), axis=0))


def per_device(joined, gain, weight_codes, scale_exp, cotangent):
    n_tp = lax.axis_size("tp")
    width = MODEL_WIDTH
    second_half_rows = lax.axis_index("tp") >= n_tp // 2
    factor = jnp.repeat(jnp.exp2(scale_exp.astype(jnp.float32)), BLOCK, axis=1)
    weight = (weight_codes.astype(jnp.float32) * factor).astype(jnp.bfloat16)
    value_entries = joined.astype(jnp.float32)
    sq_totals = lax.psum(half_partial_sums(value_entries * value_entries, second_half_rows), "tp")
    row_scale_factor = lax.rsqrt(pick_half(sq_totals, second_half_rows) / width + eps)
    normalized_hidden = value_entries * row_scale_factor
    normalized_input = (normalized_hidden * gain[None, :]).astype(jnp.bfloat16)
    normed_all = lax.all_gather(normalized_input, "seq", axis=0, tiled=True)
    partial_value = lax.dot_general(
        normed_all, weight, (((1,), (1,)), ((), ())), preferred_element_type=jnp.float32
    ).astype(jnp.bfloat16)
    total_rows = partial_value.shape[0]
    received = lax.all_to_all(
        partial_value.reshape(1, total_rows, partial_value.shape[1]),
        "tp",
        split_axis=1,
        concat_axis=0,
        tiled=True,
    )
    projected = jnp.sum(received.astype(jnp.float32), axis=0).astype(jnp.bfloat16)
    gathered_grad, grad_normed = input_gradient(cotangent, weight)
    upper_bound = grad_normed * gain[None, :]
    product_sums = lax.psum(
        half_partial_sums(upper_bound * normalized_hidden, second_half_rows), "tp"
    )
    product_mean = pick_half(product_sums, second_half_rows) / width
    joined_gradient = (row_scale_factor * (upper_bound - normalized_hidden * product_mean)).astype(
        jnp.bfloat16
    )
    weight_grad = lax.dot_general(
        gathered_grad, normed_all, (((0,), (0,)), ((), ())), preferred_element_type=jnp.float32
    ) / jnp.sqrt(jnp.float32(total_rows))
    return (projected, joined_gradient, weight_grad)


def solution(mesh):
    in_specs = (P("seq", "tp"), P("tp"), P("seq", "tp"), P("seq", "tp"), P("tp", "seq"))
    out_specs = (P("tp", "seq"), P("seq", "tp"), P("seq", "tp"))
    return jax.shard_map(
        per_device, mesh=mesh, in_specs=in_specs, out_specs=out_specs, check_vma=False
    )
```

profile of v0, /device:TPU:1, one launch (start us, length us, event | category | flops | bytes accessed | tf_op | source)
XLA Modules:
  0.0 732.1 jit_solution(11497421778098871084)
XLA Ops:
  7.2 0.7 all-gather.5.cloned.1.call-update
  7.9 0.7 multiply_exponential_fusion
  8.7 0.3 broadcast_in_dim.2
  9.0 1.2 fusion.2
  10.2 48.2 %all-gather.5.cloned.1.call-done = bf16[4096,224]{0,1:T(8,128)(2,1)} async-done(((bf16[256,224]{0,1:T(8,128)(2,1)}), bf16[4096,224]{0,1:T(8,128)(2,1)}) %all-gather.5.cloned.1.call-update) | async-done | bytes 1835024 | tf_op jit(solution)/shard_map/all_gather | solution.py:26
  58.5 6.5 convert_bitcast_fusion
  65.0 32.2 %copy.20 = bf16[1,4096,896]{2,0,1:T(2,128)(2,1)} copy(bf16[1,4096,896]{1,2,0:T(8,128)(2,1)} %convert_bitcast_fusion) | data formatting | bytes 14680064 | tf_op jit(solution)/shard_map/reshape | solution.py:30
  97.2 0.5 broadcast.94
  97.7 157.1 %reduce.3 = bf16[4096,896]{1,0:T(8,128)(2,1)} reduce(bf16[4096,1,896]{2,1,0:T(2,128)(2,1)} %bitcast.38, bf16[]{:T(256)} %broadcast.94), dimensions={1}, to_apply=%bitcast.27.reduce_sub_computation | reduce | bytes 14680066
  254.8 19.5 %reshape.73 = bf16[32,2,57344]{2,1,0:T(2,128)(2,1)} reshape(bf16[4096,896]{1,0:T(8,128)(2,1)} %reduce.3) | data formatting | bytes 14680064
  274.3 10.1 %all-to-all-start.1 = ((bf16[32,2,57344]{2,1,0:T(2,128)(2,1)}), bf16[32,2,57344]{2,1,0:T(2,128)(2,1)}, u32[]{:S(2)}, u32[]{:S(2)}) async-start(bf16[32,2,57344]{2,1,0:T(2,128)(2,1)} %reshape.73), calls=%async_computation.1 | async-start | bytes 14680064 | tf_op jit(solution)/shard_map/all_to_all | solution.py:29
  284.9 24.8 %psum.14 = f32[128,2]{0,1:T(2,128)S(1)} all-reduce(f32[128,2]{0,1:T(2,128)S(1)} %pad_maximum_fusion), channel_id=1, replica_groups=mesh['seq'=32,'tp'=16] {'tp'}, use_global_device_ids=true, to_apply=%region_1.2 | all-reduce | flops 256 | bytes 2048 | tf_op jit(solution)/shard_map/psum | solution.py:42
  309.7 139.7 %all-to-all-done.1 = bf16[32,2,57344]{2,1,0:T(2,128)(2,1)} async-done(((bf16[32,2,57344]{2,1,0:T(2,128)(2,1)}), bf16[32,2,57344]{2,1,0:T(2,128)(2,1)}, u32[]{:S(2)}, u32[]{:S(2)}) %all-to-all-start.1) | async-done | bytes 7340064 | tf_op jit(solution)/shard_map/all_to_all | solution.py:29
  449.4 22.8 %reshape.74 = bf16[4096,1,896]{2,1,0:T(2,128)(2,1)} reshape(bf16[32,2,57344]{2,1,0:T(2,128)(2,1)} %all-to-all-done.1) | data formatting | bytes 14680064
  472.2 11.3 %copy.25 = f32[1,4096,896]{2,1,0:T(8,128)} copy(bf16[1,4096,896]{2,0,1:T(2,128)(2,1)} %bitcast.39) | data formatting | bytes 22020096
  483.5 5.9 reduce_sum.41
  489.6 0.2 fusion.7
  489.8 24.0 %psum.15 = f32[128,2]{0,1:T(2,128)S(1)} all-reduce(f32[128,2]{0,1:T(2,128)S(1)} %pad_maximum_fusion.1), channel_id=1, replica_groups=mesh['seq'=32,'tp'=16] {'tp'}, use_global_device_ids=true, to_apply=%region_5.6 | all-reduce | flops 256 | bytes 2048 | tf_op jit(solution)/shard_map/psum | solution.py:61
  513.8 0.9 fusion.10
  514.7 103.1 %all-gather.3.cloned.1.call-done = bf16[4096,896]{0,1:T(8,128)(2,1)} async-done(((bf16[128,896]{0,1:T(8,128)(2,1)}), bf16[4096,896]{0,1:T(8,128)(2,1)}) %all-gather.3.cloned.1.call-update) | async-done | bytes 7340048 | tf_op jit(solution)/shard_map/all_gather | solution.py:46
  617.8 5.1 fusion
  623.0 8.6 %copy.18 = bf16[1,4096,224]{2,0,1:T(2,128)(2,1)} copy(bf16[1,4096,224]{1,2,0:T(8,128)(2,1)S(1)} %fusion) | data formatting | bytes 3670016 | tf_op jit(solution)/shard_map/reshape | solution.py:52
  631.6 23.6 %reduce.4 = bf16[4096,224]{1,0:T(8,128)(2,1)S(1)} reduce(bf16[4096,1,224]{2,1,0:T(2,128)(2,1)} %bitcast.40, bf16[]{:T(256)} %broadcast.94), dimensions={1}, to_apply=%bitcast.29.reduce_sub_computation | reduce | bytes 3670018
  655.2 4.5 reshape.75
  659.7 10.2 %all-to-all-start = ((bf16[16,2,28672]{2,1,0:T(2,128)(2,1)}), bf16[16,2,28672]{2,1,0:T(2,128)(2,1)S(1)}, u32[]{:S(2)}, u32[]{:S(2)}) async-start(bf16[16,2,28672]{2,1,0:T(2,128)(2,1)} %reshape.75), calls=%async_computation | async-start | bytes 3670016 | tf_op jit(solution)/shard_map/all_to_all | solution.py:51
  669.9 0.8 copy.22
  670.7 6.9 fusion.1
  677.6 35.9 %all-to-all-done = bf16[16,2,28672]{2,1,0:T(2,128)(2,1)S(1)} async-done(((bf16[16,2,28672]{2,1,0:T(2,128)(2,1)}), bf16[16,2,28672]{2,1,0:T(2,128)(2,1)S(1)}, u32[]{:S(2)}, u32[]{:S(2)}) %all-to-all-start) | async-done | bytes 1835040 | tf_op jit(solution)/shard_map/all_to_all | solution.py:51
  713.5 8.1 %reshape.76 = bf16[4096,1,224]{2,1,0:T(2,128)(2,1)} reshape(bf16[16,2,28672]{2,1,0:T(2,128)(2,1)S(1)} %all-to-all-done) | data formatting | bytes 3670016
  721.6 2.5 copy.24
  724.1 0.4 reduce_sum.40
  724.5 0.8 copy.26
  (17 shorter events, 0.8 us)
Async XLA Ops:
  7.2 51.3 %all-gather.5.cloned.1.call-start = ((), (), s32[]{:S(2)}) async-start(), calls=%async_computation.3 | async-start | bytes 1949696 | tf_op jit(solution)/shard_map/all_gather | solution.py:26
  274.3 10.2 %copy-start = (bf16[128,896]{1,0:T(8,128)(2,1)S(1)}, bf16[128,896]{1,0:T(8,128)(2,1)}, u32[]{:S(2)}) copy-start(bf16[128,896]{1,0:T(8,128)(2,1)} %param.5) | copy-start | bytes 688132
  274.3 175.1 %all-to-all-start.1 = ((bf16[32,2,57344]{2,1,0:T(2,128)(2,1)}), bf16[32,2,57344]{2,1,0:T(2,128)(2,1)}, u32[]{:S(2)}, u32[]{:S(2)}) async-start(bf16[32,2,57344]{2,1,0:T(2,128)(2,1)} %reshape.73), calls=%async_computation.1 | async-start | bytes 14680064 | tf_op jit(solution)/shard_map/all_to_all | solution.py:29
  284.5 333.4 %all-gather.3.cloned.1.call-start = ((), (), s32[]{:S(2)}) async-start(), calls=%async_computation.2 | async-start | bytes 7569408 | tf_op jit(solution)/shard_map/all_gather | solution.py:46
  483.5 6.1 copy-start.1
  659.7 53.8 %all-to-all-start = ((bf16[16,2,28672]{2,1,0:T(2,128)(2,1)}), bf16[16,2,28672]{2,1,0:T(2,128)(2,1)S(1)}, u32[]{:S(2)}, u32[]{:S(2)}) async-start(bf16[16,2,28672]{2,1,0:T(2,128)(2,1)} %reshape.75), calls=%async_computation | async-start | bytes 3670016 | tf_op jit(solution)/shard_map/all_to_all | solution.py:51
Sparse Core Ops, SparseCore 0:
  10.0 48.3 all-gather.4
  514.8 102.9 all-gather.2
where the time goes:
time: 735 us; the launch traced here: 732 us
  waiting for transfers between devices  328 us (45%)
  other arithmetic  190 us (26%)
  local copies, waits for them, and re-layouts  112 us (15%)
  blocking collectives  48.8 us (7%)
  starting transfers between devices  20.4 us (3%)
  matrix products  18.6 us (3%)
  between operations  14.1 us (2%)
    unnamed x2, other arithmetic  181 us
    all_to_all x1, waiting for transfers between devices, input_gradient(): lax.all_to_all(back.reshape(1, total_rows, back.shape[1]), 'seq', split_a...  140 us
    all_gather x1, waiting for transfers between devices, per_device(): normed_all = lax.all_gather(normalized_input, 'seq', axis=0, tiled=True)  103 us
    unnamed x15, local copies, waits for them, and re-layouts  71.1 us
    all_gather x1, waiting for transfers between devices, input_gradient(): gathered = lax.all_gather(cotangent, 'tp', axis=0, tiled=True)  48.2 us
    all_to_all x1, waiting for transfers between devices, per_device(): lax.all_to_all(partial_value.reshape(1, total_rows, partial_value.shape[1...  35.9 us
    reshape x1, local copies, waits for them, and re-layouts, input_gradient(): back.reshape(1, total_rows, back.shape[1])  32.2 us
    psum x1, blocking collectives, per_device(): lax.psum(half_partial_sums(value_entries * value_entries, second_half_row...  24.8 us
  transfers between devices with their start and end apart: 4, of which 4 were waited for; matrix products, arithmetic and copies ran while one was open for 1% of the time, Pallas kernels for 0%

commit v1 on v0

v1 whole, which is shorter than its diff:
```python
import jax
import jax.numpy as jnp
from jax import lax
from jax.experimental import pallas as pl
from jax.experimental.pallas import tpu as pltpu
from jax.sharding import Mesh, PartitionSpec as P

MODEL_WIDTH = 7168
BLOCK = 128
TOKENS = 4096
NX, NZ, NY, NC = 4, 8, 8, 2
ROWS = 128
FEATS = 224
COLS = 256
WIDTH = 896
eps = 1e-06
BF16, F32 = jnp.bfloat16, jnp.float32
VMEM = pl.BlockSpec(memory_space=pltpu.VMEM)
ANY = pl.BlockSpec(memory_space=pl.ANY)
PARAMS = pltpu.CompilerParams(vmem_limit_bytes=40 * 1024 * 1024)


def cost(flops, size):
    return pl.CostEstimate(flops=flops, bytes_accessed=size, transcendentals=0)


def row_scales(ss_ref):
    half = lax.axis_index("y") // (NY // 2)
    total = ss_ref[0]
    for p in range(1, 8):
        total = total + ss_ref[p]
    other = ss_ref[8]
    for p in range(9, 16):
        other = other + ss_ref[p]
    total = jnp.where(half == 0, total, other)
    return lax.rsqrt(total / MODEL_WIDTH + eps)


def input_grad_kernel(own, other, weight, grad, cot, sems):
    core = lax.axis_index("c")
    copies = []
    for m in range(8):
        for which, (block, parity) in enumerate(((own, core), (other, 1 - core))):
            start = pl.multiple_of(512 * (m % 2) + COLS * parity, COLS)
            copies.append(
                pltpu.make_async_copy(
                    block.at[m],
                    cot.at[pl.ds(FEATS * (m // 2), FEATS), pl.ds(start, COLS)],
                    sems.at[2 * m + which],
                )
            )
    for copy in copies:
        copy.start()
    for copy in copies:
        copy.wait()
    for j in range(4):
        part = lax.dot_general(
            cot[:, COLS * j : COLS * (j + 1)], weight[...], (((0,), (0,)), ((), ())), preferred_element_type=F32
        )
        grad[2 * j : 2 * j + 2] = part.astype(BF16).reshape(2, ROWS, WIDTH)


def forward_kernel(ss, joined, gain, weight, cot, normed, keep, send, dots):
    core = lax.axis_index("c")
    scales = row_scales(ss).T
    for z in range(NZ):
        value = joined[z].astype(F32) * scales[:, z : z + 1]
        normed[ROWS * z : ROWS * (z + 1), :] = (value * gain[...]).astype(BF16)
    for j in range(4):
        part = lax.dot_general(
            weight[...], normed[COLS * j : COLS * (j + 1), :], (((1,), (1,)), ((), ())), preferred_element_type=F32
        )
        dot = jnp.sum(part * cot[:, COLS * j : COLS * (j + 1)].astype(F32), axis=0, keepdims=True)
        dots[2 * j : 2 * j + 1, :] = dot[:, :ROWS]
        dots[2 * j + 1 : 2 * j + 2, :] = dot[:, ROWS:]
        part = part.astype(BF16)

        @pl.when(core == j % 2)
        def _():
            for i in range(4):
                keep[2 * i + j // 2] = part[FEATS * i : FEATS * (i + 1)]

        @pl.when(core != j % 2)
        def _():
            for i in range(4):
                send[2 * i + j // 2] = part[FEATS * i : FEATS * (i + 1)]


def weight_grad_kernel(cot, normed, out):
    for i in range(4):
        part = jnp.dot(cot[FEATS * i : FEATS * (i + 1), :], normed[...], preferred_element_type=F32)
        out[i] = (part * (1.0 / 64.0)).astype(BF16)


def joined_grad_kernel(ss, dots, grad, joined, gain, out):
    me = lax.axis_index("z")
    half = lax.axis_index("y") // (NY // 2)
    sums = jnp.sum(dots[...], axis=0)
    first = jnp.sum(sums[:8], axis=0, keepdims=True)
    second = jnp.sum(sums[8:], axis=0, keepdims=True)
    c = jnp.where(half == 0, first, second) / MODEL_WIDTH
    c = jnp.broadcast_to(c, (8, ROWS)).T[:, :1]
    scales = row_scales(ss)
    mine = lax.broadcasted_iota(jnp.int32, scales.shape, 0) == me
    scale = jnp.sum(jnp.where(mine, scales, 0.0), axis=0, keepdims=True)
    scale = jnp.broadcast_to(scale, (8, ROWS)).T[:, :1]
    u = grad[...].astype(F32) * gain[...]
    xhat = joined[...].astype(F32) * scale
    out[...] = (scale * (u - xhat * c)).astype(BF16)


def transposed():
    return [(x * NY + y, (y // 2) * NY + 2 * x + y % 2) for x in range(NX) for y in range(NY)]


def spread(value, count):
    return jnp.broadcast_to(value[None], (count,) + value.shape)


def per_device(joined, gain, weight_codes, scale_exp, cotangent):
    swap = [(0, 1), (1, 0)]
    gain = gain[None, :]
    joined_all = lax.all_gather(joined, "z")
    cot = lax.ppermute(cotangent.T, ("x", "y"), transposed())

    values = joined.astype(F32)
    squares = jnp.sum(values * values, axis=1)
    squares = lax.all_to_all(spread(squares, NZ), "z", 0, 0)
    squares = lax.all_to_all(spread(squares, NY * NC), ("y", "c"), 0, 0)

    factor = jnp.repeat(jnp.exp2(scale_exp.astype(F32)), BLOCK, axis=1)
    weight = (weight_codes.astype(F32) * factor).astype(BF16)
    weight = lax.all_to_all(spread(weight, NX), "x", 0, 0).reshape(NX * FEATS, WIDTH)

    own = lax.all_to_all(spread(cot, NY), "y", 0, 0)
    other = lax.ppermute(own, "c", swap)

    flops = 2 * 1024 * WIDTH * WIDTH
    grad, cot = pl.pallas_call(
        input_grad_kernel,
        out_shape=(jax.ShapeDtypeStruct((NZ, ROWS, WIDTH), BF16), jax.ShapeDtypeStruct((WIDTH, 1024), BF16)),
        in_specs=[ANY, ANY, VMEM],
        out_specs=(VMEM, VMEM),
        scratch_shapes=[pltpu.SemaphoreType.DMA((16,))],
        compiler_params=PARAMS,
        cost_estimate=cost(flops, 7 << 20),
        name="input_grad",
    )(own, other, weight)
    grad = lax.psum_scatter(grad, "z")

    normed, keep, send, dots = pl.pallas_call(
        forward_kernel,
        out_shape=(
            jax.ShapeDtypeStruct((1024, WIDTH), BF16),
            jax.ShapeDtypeStruct((8, FEATS, COLS), BF16),
            jax.ShapeDtypeStruct((8, FEATS, COLS), BF16),
            jax.ShapeDtypeStruct((NZ, ROWS), F32),
        ),
        in_specs=[VMEM] * 5,
        out_specs=(VMEM,) * 4,
        compiler_params=PARAMS,
        cost_estimate=cost(flops, 9 << 20),
        name="forward",
    )(squares, joined_all, gain, weight, cot)
    got = lax.ppermute(send, "c", swap)

    partial_wgrad = pl.pallas_call(
        weight_grad_kernel,
        out_shape=jax.ShapeDtypeStruct((NX, FEATS, WIDTH), BF16),
        in_specs=[VMEM, VMEM],
        out_specs=VMEM,
        compiler_params=PARAMS,
        cost_estimate=cost(flops, 6 << 20),
        name="weight_grad",
    )(cot, normed)

    both = (keep.astype(F32) + got.astype(F32)).astype(BF16)
    parts = lax.all_to_all(both, "y", 0, 0)
    projected = jnp.sum(parts.astype(F32), axis=0).astype(BF16)
    projected = lax.ppermute(projected, ("x", "y"), transposed()).T

    dots = jnp.broadcast_to(dots[:, None], (NZ, NY * NC, ROWS)).reshape(NZ * NY * NC, 1, ROWS)
    dots = lax.all_to_all(dots, ("z", "y", "c"), 0, 0).reshape(NZ, NY * NC, ROWS)

    wgrads = lax.all_to_all(partial_wgrad, "x", 0, 0)
    weight_grad = jnp.sum(wgrads.astype(F32), axis=0)

    joined_gradient = pl.pallas_call(
        joined_grad_kernel,
        out_shape=jax.ShapeDtypeStruct((ROWS, WIDTH), BF16),
        in_specs=[VMEM] * 5,
        out_specs=VMEM,
        compiler_params=PARAMS,
        cost_estimate=cost(8 * ROWS * WIDTH, 1 << 20),
        name="joined_grad",
    )(squares, dots, grad, joined, gain)
    return (projected, joined_gradient, weight_grad)


def solution(mesh):
    grid = Mesh(mesh.devices.reshape(NX, NZ, NY, NC), ("x", "z", "y", "c"))
    seq, tp = ("x", "z"), ("y", "c")
    in_specs = (P(seq, tp), P(tp), P(seq, tp), P(seq, tp), P(tp, seq))
    out_specs = (P(tp, seq), P(seq, tp), P(seq, tp))
    return jax.shard_map(per_device, mesh=grid, in_specs=in_specs, out_specs=out_specs, check_vma=False)
```

time: 735 us -> 204 us (0.28)
  waiting for transfers between devices: 328 us -> 96.3 us
  other arithmetic: 190 us -> 3.7 us
  local copies, waits for them, and re-layouts: 112 us -> 12.7 us
  blocking collectives: 48.8 us -> 17.2 us
  starting transfers between devices: 20.4 us -> 46.2 us
  matrix products: 18.6 us -> 0 us
  Pallas kernels: 0 us -> 13.3 us
    unnamed x2 -> x0, other arithmetic: 181 us -> none
    all_gather x2 -> x1, waiting for transfers between devices: 151 us -> 0.01 us  [per_device(): joined_all = lax.all_gather(joined, 'z')]
    all_to_all x2 -> x6, waiting for transfers between devices: 176 us -> 93.3 us  [the longest x1 23.6 us: per_device(): own = lax.all_to_all(spread(cot, NY), 'y', 0, 0)]
    unnamed x15 -> x23, local copies, waits for them, and re-layouts: 71.1 us -> 8.69 us
    psum x2 -> x0, blocking collectives: 48.8 us -> none  [the longest x1 24.8 us: per_device(): lax.psum(half_partial_sums(value_entries * value_entries, second_half_row...]
    reshape x2 -> x0, local copies, waits for them, and re-layouts: 40.8 us -> none  [the longest x1 32.2 us: input_gradient(): back.reshape(1, total_rows, back.shape[1])]
    dot_general x3 -> x0, matrix products: 18.6 us -> none  [the longest x1 6.9 us: per_device(): lax.dot_general(gathered_grad, normed_all, (((0,), (0,)), ((), ())), pref...]
    all_to_all x0 -> x1, blocking collectives: none -> 17.2 us  [per_device(): squares = lax.all_to_all(spread(squares, NZ), 'z', 0, 0)]
  transfers between devices with their start and end apart: 4 -> 12, of which waited for: 4 -> 7; matrix products, arithmetic and copies ran while one was open for 1% -> 4% of each run, Pallas kernels for 0% -> 4%
where the time goes in v1:
time: 204 us
  waiting for transfers between devices  96.3 us (47%)
  starting transfers between devices  46.2 us (23%)
  blocking collectives  17.2 us (8%)
  between operations  14.2 us (7%)
  Pallas kernels  13.3 us (7%)
  local copies, waits for them, and re-layouts  12.7 us (6%)
  other arithmetic  3.7 us (2%)
    all_to_all x1, waiting for transfers between devices, per_device(): own = lax.all_to_all(spread(cot, NY), 'y', 0, 0)  23.6 us
    all_to_all x1, waiting for transfers between devices, per_device(): parts = lax.all_to_all(both, 'y', 0, 0)  21.5 us
    all_to_all x1, waiting for transfers between devices, per_device(): wgrads = lax.all_to_all(partial_wgrad, 'x', 0, 0)  21.5 us
    all_to_all x1, blocking collectives, per_device(): squares = lax.all_to_all(spread(squares, NZ), 'z', 0, 0)  17.2 us
    all_to_all x1, waiting for transfers between devices, per_device(): lax.all_to_all(spread(weight, NX), 'x', 0, 0).reshape(NX * FEATS, WIDTH)  14 us
    all_to_all x1, waiting for transfers between devices, per_device(): lax.all_to_all(dots, ('z', 'y', 'c'), 0, 0).reshape(NZ, NY * NC, ROWS)  10.3 us
    all_to_all x1, starting transfers between devices, per_device(): own = lax.all_to_all(spread(cot, NY), 'y', 0, 0)  9.58 us
    all_to_all x1, starting transfers between devices, per_device(): lax.all_to_all(dots, ('z', 'y', 'c'), 0, 0).reshape(NZ, NY * NC, ROWS)  8.95 us
  transfers between devices with their start and end apart: 12, of which 7 were waited for; matrix products, arithmetic and copies ran while one was open for 4% of the time, Pallas kernels for 4%

profile of v1, /device:TPU:1, one launch (start us, length us, event | category | flops | bytes accessed | tf_op | source)
XLA Modules:
  0.0 203.5 jit_solution(10932561098199404827)
XLA Ops:
  7.9 1.6 collective-permute-start
  9.5 1.1 multiply_reduce_fusion
  10.5 17.2 %all_to_all.36 = f32[8,1,128]{2,1,0:T(1,128)S(1)} all-to-all(f32[8,1,128]{2,1,0:T(1,128)S(1)} %broadcast_in_dim.16), channel_id=1, replica_groups=mesh['x'=4,'z'=8,'y'=8,'c'=2] {'z'}, dimensions={0} | all-to-all | bytes 8192 | tf_op jit(solution)/shard_map/all_to_all | solution.py:128
  27.7 1.0 broadcast_in_dim.44
  28.7 9.6 %all-to-all-start.3 = ((bf16[8,224,256]{2,1,0:T(8,128)(2,1)}), bf16[8,224,256]{2,1,0:T(8,128)(2,1)S(1)}, u32[]{:S(2)}, u32[]{:S(2)}) async-start(bf16[8,224,256]{2,1,0:T(8,128)(2,1)} %broadcast_in_dim.44), calls=%async_computation.3 | async-start | bytes 1835008 | tf_op jit(solution)/shard_map/all_to_all | solution.py:135
  39.0 23.6 %all-to-all-done.3.own = bf16[8,224,256]{2,1,0:T(8,128)(2,1)S(1)} async-done(((bf16[8,224,256]{2,1,0:T(8,128)(2,1)}), bf16[8,224,256]{2,1,0:T(8,128)(2,1)S(1)}, u32[]{:S(2)}, u32[]{:S(2)}) %all-to-all-start.3) | async-done | bytes 917536 | tf_op jit(solution)/shard_map/all_to_all | solution.py:135
  62.6 1.3 broadcast_in_dim.21
  63.9 4.2 %all-to-all-start.2 = ((bf16[4,224,896]{2,1,0:T(8,128)(2,1)}), bf16[4,224,896]{2,1,0:T(8,128)(2,1)S(1)}, u32[]{:S(2)}, u32[]{:S(2)}) async-start(bf16[4,224,896]{2,1,0:T(8,128)(2,1)} %broadcast_in_dim.21), calls=%async_computation.2 | async-start | bytes 3211264 | tf_op jit(solution)/shard_map/all_to_all | solution.py:133
  68.1 4.5 %collective-permute-start.1 = (bf16[8,224,256]{2,1,0:T(8,128)(2,1)S(1)}, bf16[8,224,256]{2,1,0:T(8,128)(2,1)S(1)}, u32[]{:S(2)}, u32[]{:S(2)}) collective-permute-start(bf16[8,224,256]{2,1,0:T(8,128)(2,1)S(1)} %all-to-all-done.3.own), channel_id=1, source_target_pairs={{0,1},{1,0},{2,3},{3,2},{4,5},{5,4},{6,7},{7,6},{8,9},{9,8},{10,11... | collective-permute-start | bytes 2752520 | tf_op jit(solution)/shard_map/ppermute | solution.py:136
  72.6 14.0 %all-to-all-done.2 = bf16[4,224,896]{2,1,0:T(8,128)(2,1)S(1)} async-done(((bf16[4,224,896]{2,1,0:T(8,128)(2,1)}), bf16[4,224,896]{2,1,0:T(8,128)(2,1)S(1)}, u32[]{:S(2)}, u32[]{:S(2)}) %all-to-all-start.2) | async-done | bytes 1605664 | tf_op jit(solution)/shard_map/all_to_all | solution.py:133
  87.2 6.8 %all-to-all-start.1 = ((f32[16,8,128]{2,1,0:T(8,128)}), f32[16,8,128]{2,1,0:T(8,128)S(1)}, u32[]{:S(2)}, u32[]{:S(2)}) async-start(f32[16,8,128]{2,1,0:T(8,128)} %broadcast_in_dim.18), calls=%async_computation.1 | async-start | bytes 131072 | tf_op jit(solution)/shard_map/all_to_all | solution.py:129
  94.1 4.0 %input_grad.1 = (bf16[8,128,896]{2,1,0:T(8,128)(2,1)}, bf16[896,1024]{1,0:T(8,128)(2,1)S(1)}) custom-call(bf16[8,224,256]{2,1,0:T(8,128)(2,1)S(1)} %all-to-all-done.3.own, bf16[8,224,256]{2,1,0:T(8,128)(2,1)S(1)} %collective-permute-done.1.other, bf16[896,896]{1,0:T(8,128)(2,1)S(1)} %bitcast.13), custom_call_target="tpu_custom_call" | custom-call | flops 1644167168 | bytes 7340032 | tf_op jit(solution)/shard_map/input_grad/pallas_call | solution.py:139
  98.1 1.2 copy-done.3
  99.3 2.5 %all-to-all-done.1.ss = f32[16,8,128]{2,1,0:T(8,128)S(1)} async-done(((f32[16,8,128]{2,1,0:T(8,128)}), f32[16,8,128]{2,1,0:T(8,128)S(1)}, u32[]{:S(2)}, u32[]{:S(2)}) %all-to-all-start.1) | async-done | bytes 65568 | tf_op jit(solution)/shard_map/all_to_all | solution.py:129
  101.8 1.5 copy-done.2
  103.3 1.5 copy-done.4
  104.8 5.0 %forward.1 = (bf16[1024,896]{1,0:T(8,128)(2,1)S(1)}, bf16[8,224,256]{2,1,0:T(8,128)(2,1)S(1)}, bf16[8,224,256]{2,1,0:T(8,128)(2,1)S(1)}, f32[8,128]{1,0:T(8,128)S(1)}) custom-call(f32[16,8,128]{2,1,0:T(8,128)S(1)} %all-to-all-done.1.ss, bf16[8,128,896]{2,1,0:T(8,128)(2,1)S(1)} %bitcast.17, f32[1,896]{1,0:T(1,128)S(1)} %broadcast_in_dim.19.gain, ...), custom_call_target="tpu_custom_call" | custom-call | flops 1644167168 | bytes 9437184 | tf_op jit(solution)/shard_map/forward/pallas_call | solution.py:151
  109.9 1.2 copy-done.6
  111.1 2.0 %collective-permute-start.2 = (bf16[8,224,256]{2,1,0:T(8,128)(2,1)S(1)}, bf16[8,224,256]{2,1,0:T(8,128)(2,1)S(1)}, u32[]{:S(2)}, u32[]{:S(2)}) collective-permute-start(bf16[8,224,256]{2,1,0:T(8,128)(2,1)S(1)} %get-tuple-element.11), channel_id=1, source_target_pairs={{0,1},{1,0},{2,3},{3,2},{4,5},{5,4},{6,7},{7,6},{8,9},{9,8},{10,11... | collective-permute-start | bytes 2752520 | tf_op jit(solution)/shard_map/ppermute | solution.py:165
  113.2 2.3 %collective-permute-done.2 = bf16[8,224,256]{2,1,0:T(8,128)(2,1)S(1)} collective-permute-done((bf16[8,224,256]{2,1,0:T(8,128)(2,1)S(1)}, bf16[8,224,256]{2,1,0:T(8,128)(2,1)S(1)}, u32[]{:S(2)}, u32[]{:S(2)}) %collective-permute-start.2) | collective-permute-done | bytes 917536 | tf_op jit(solution)/shard_map/ppermute | solution.py:165
  115.5 1.2 add_convert_fusion
  116.7 4.2 %all-to-all-start.4 = ((bf16[8,224,256]{2,1,0:T(8,128)(2,1)}), bf16[8,224,256]{2,1,0:T(8,128)(2,1)S(1)}, u32[]{:S(2)}, u32[]{:S(2)}) async-start(bf16[8,224,256]{2,1,0:T(8,128)(2,1)} %add_convert_fusion), calls=%async_computation.4 | async-start | bytes 1835008 | tf_op jit(solution)/shard_map/all_to_all | solution.py:178
  120.9 1.6 copy-done.7
  122.5 3.2 %weight_grad.1 = bf16[4,224,896]{2,1,0:T(8,128)(2,1)} custom-call(bf16[896,1024]{1,0:T(8,128)(2,1)S(1)} %copy-done.5, bf16[1024,896]{1,0:T(8,128)(2,1)S(1)} %copy-done.7), custom_call_target="tpu_custom_call" | custom-call | flops 1644167168 | bytes 6291456 | tf_op jit(solution)/shard_map/weight_grad/pallas_call | solution.py:167
  125.8 21.5 %all-to-all-done.4 = bf16[8,224,256]{2,1,0:T(8,128)(2,1)S(1)} async-done(((bf16[8,224,256]{2,1,0:T(8,128)(2,1)}), bf16[8,224,256]{2,1,0:T(8,128)(2,1)S(1)}, u32[]{:S(2)}, u32[]{:S(2)}) %all-to-all-start.4) | async-done | bytes 917536 | tf_op jit(solution)/shard_map/all_to_all | solution.py:178
  147.3 3.6 %all-to-all-start.6 = ((bf16[4,224,896]{2,1,0:T(8,128)(2,1)}), bf16[4,224,896]{2,1,0:T(8,128)(2,1)S(1)}, u32[]{:S(2)}, u32[]{:S(2)}) async-start(bf16[4,224,896]{2,1,0:T(8,128)(2,1)} %weight_grad.1), calls=%async_computation.7 | async-start | bytes 3211264 | tf_op jit(solution)/shard_map/all_to_all | solution.py:185
  151.7 21.5 %all-to-all-done.6 = bf16[4,224,896]{2,1,0:T(8,128)(2,1)S(1)} async-done(((bf16[4,224,896]{2,1,0:T(8,128)(2,1)}), bf16[4,224,896]{2,1,0:T(8,128)(2,1)S(1)}, u32[]{:S(2)}, u32[]{:S(2)}) %all-to-all-start.6) | async-done | bytes 1605664 | tf_op jit(solution)/shard_map/all_to_all | solution.py:185
  173.8 9.0 %all-to-all-start.5 = ((f32[128,1,128]{2,1,0:T(1,128)}), f32[128,1,128]{2,1,0:T(1,128)S(1)}, u32[]{:S(2)}, u32[]{:S(2)}) async-start(f32[128,1,128]{2,1,0:T(1,128)} %bitcast.5), calls=%async_computation.5 | async-start | bytes 131072 | tf_op jit(solution)/shard_map/all_to_all | solution.py:183
  182.7 1.1 convert_reduce_fusion
  183.8 10.3 %all-to-all-done.5 = f32[128,1,128]{2,1,0:T(1,128)S(1)} async-done(((f32[128,1,128]{2,1,0:T(1,128)}), f32[128,1,128]{2,1,0:T(1,128)S(1)}, u32[]{:S(2)}, u32[]{:S(2)}) %all-to-all-start.5) | async-done | bytes 65568 | tf_op jit(solution)/shard_map/all_to_all | solution.py:183
  194.1 0.9 copy-done.1
  195.0 1.0 joined_grad.1
  (36 shorter events, 4.2 us)
Async XLA Ops:
  7.2 31.2 %copy-start.9 = (s32[224,7]{0,1:T(8,128)S(1)}, s32[224,7]{0,1:T(8,128)}, u32[]{:S(2)}) copy-start(s32[224,7]{0,1:T(8,128)} %param.8) | copy-start | bytes 18820
  7.2 94.7 %all-gather.3.cloned.1.call-start = ((), (), s32[]{:S(2)}) async-start(), calls=%async_computation.9 | async-start | bytes 2064384 | tf_op jit(solution)/shard_map/all_gather | solution.py:123
  7.9 19.8 %collective-permute-start = (bf16[224,256]{1,0:T(8,128)(2,1)}, bf16[224,256]{1,0:T(8,128)(2,1)S(1)}, u32[]{:S(2)}, u32[]{:S(2)}) collective-permute-start(bf16[224,256]{1,0:T(8,128)(2,1)} %bitcast.21), channel_id=1, source_target_pairs={{0,0},{2,2},{4,128},{6,130},{8,256},{10,258},{12,384},{14,386},{12... | collective-permute-start | bytes 344072 | tf_op jit(solution)/shard_map/ppermute | solution.py:124
  27.7 11.1 %copy-start.8 = (bf16[224,896]{1,0:T(8,128)(2,1)S(1)}, bf16[224,896]{1,0:T(8,128)(2,1)}, u32[]{:S(2)}) copy-start(bf16[224,896]{1,0:T(8,128)(2,1)} %param.7) | copy-start | bytes 1204228
  28.7 33.8 %all-to-all-start.3 = ((bf16[8,224,256]{2,1,0:T(8,128)(2,1)}), bf16[8,224,256]{2,1,0:T(8,128)(2,1)S(1)}, u32[]{:S(2)}, u32[]{:S(2)}) async-start(bf16[8,224,256]{2,1,0:T(8,128)(2,1)} %broadcast_in_dim.44), calls=%async_computation.3 | async-start | bytes 1835008 | tf_op jit(solution)/shard_map/all_to_all | solution.py:135
  63.9 8.7 %copy-start.10 = (f32[896]{0:T(1024)S(1)}, f32[896]{0:T(1024)}, u32[]{:S(2)}) copy-start(f32[896]{0:T(1024)} %param.6) | copy-start | bytes 10756
  63.9 22.7 %all-to-all-start.2 = ((bf16[4,224,896]{2,1,0:T(8,128)(2,1)}), bf16[4,224,896]{2,1,0:T(8,128)(2,1)S(1)}, u32[]{:S(2)}, u32[]{:S(2)}) async-start(bf16[4,224,896]{2,1,0:T(8,128)(2,1)} %broadcast_in_dim.21), calls=%async_computation.2 | async-start | bytes 3211264 | tf_op jit(solution)/shard_map/all_to_all | solution.py:133
  68.1 26.0 %collective-permute-start.1 = (bf16[8,224,256]{2,1,0:T(8,128)(2,1)S(1)}, bf16[8,224,256]{2,1,0:T(8,128)(2,1)S(1)}, u32[]{:S(2)}, u32[]{:S(2)}) collective-permute-start(bf16[8,224,256]{2,1,0:T(8,128)(2,1)S(1)} %all-to-all-done.3.own), channel_id=1, source_target_pairs={{0,1},{1,0},{2,3},{3,2},{4,5},{5,4},{6,7},{7,6},{8,9},{9,8},{10,11... | collective-permute-start | bytes 2752520 | tf_op jit(solution)/shard_map/ppermute | solution.py:136
  87.2 14.7 %all-to-all-start.1 = ((f32[16,8,128]{2,1,0:T(8,128)}), f32[16,8,128]{2,1,0:T(8,128)S(1)}, u32[]{:S(2)}, u32[]{:S(2)}) async-start(f32[16,8,128]{2,1,0:T(8,128)} %broadcast_in_dim.18), calls=%async_computation.1 | async-start | bytes 131072 | tf_op jit(solution)/shard_map/all_to_all | solution.py:129
  94.0 100.1 %reduce-scatter.2.cloned.1.call-start = ((), (), s32[]{:S(2)}) async-start(), calls=%async_computation.8 | async-start | bytes 2064384 | tf_op jit(solution)/shard_map/reduce_scatter | solution.py:149
  98.1 1.3 copy-start.3
  101.8 1.5 copy-start.2
  103.3 1.5 copy-start.4
  109.9 1.2 copy-start.6
  111.1 4.4 %collective-permute-start.2 = (bf16[8,224,256]{2,1,0:T(8,128)(2,1)S(1)}, bf16[8,224,256]{2,1,0:T(8,128)(2,1)S(1)}, u32[]{:S(2)}, u32[]{:S(2)}) collective-permute-start(bf16[8,224,256]{2,1,0:T(8,128)(2,1)S(1)} %get-tuple-element.11), channel_id=1, source_target_pairs={{0,1},{1,0},{2,3},{3,2},{4,5},{5,4},{6,7},{7,6},{8,9},{9,8},{10,11... | collective-permute-start | bytes 2752520 | tf_op jit(solution)/shard_map/ppermute | solution.py:165
  116.7 4.2 %copy-start.5 = (bf16[896,1024]{1,0:T(8,128)(2,1)S(1)}, bf16[896,1024]{1,0:T(8,128)(2,1)}, u32[]{:S(2)}) copy-start(bf16[896,1024]{1,0:T(8,128)(2,1)} %copy-done.3) | copy-start | bytes 5505028
  116.7 30.6 %all-to-all-start.4 = ((bf16[8,224,256]{2,1,0:T(8,128)(2,1)}), bf16[8,224,256]{2,1,0:T(8,128)(2,1)S(1)}, u32[]{:S(2)}, u32[]{:S(2)}) async-start(bf16[8,224,256]{2,1,0:T(8,128)(2,1)} %add_convert_fusion), calls=%async_computation.4 | async-start | bytes 1835008 | tf_op jit(solution)/shard_map/all_to_all | solution.py:178
  120.9 1.6 copy-start.7
  147.3 25.9 %all-to-all-start.6 = ((bf16[4,224,896]{2,1,0:T(8,128)(2,1)}), bf16[4,224,896]{2,1,0:T(8,128)(2,1)S(1)}, u32[]{:S(2)}, u32[]{:S(2)}) async-start(bf16[4,224,896]{2,1,0:T(8,128)(2,1)} %weight_grad.1), calls=%async_computation.7 | async-start | bytes 3211264 | tf_op jit(solution)/shard_map/all_to_all | solution.py:185
  150.8 43.3 %copy-start = (bf16[128,896]{1,0:T(8,128)(2,1)S(1)}, bf16[128,896]{1,0:T(8,128)(2,1)}, u32[]{:S(2)}) copy-start(bf16[128,896]{1,0:T(8,128)(2,1)} %joined.1) | copy-start | bytes 688132
  151.0 32.9 %collective-permute-start.3 = (bf16[224,256]{1,0:T(8,128)(2,1)S(1)}, bf16[224,256]{1,0:T(8,128)(2,1)S(1)}, u32[]{:S(2)}, u32[]{:S(2)}) collective-permute-start(bf16[224,256]{1,0:T(8,128)(2,1)S(1)} %reduce_sum.31), channel_id=1, source_target_pairs={{0,0},{2,2},{4,128},{6,130},{8,256},{10,258},{12,384},{14,386},{12... | collective-permute-start | bytes 344072 | tf_op jit(solution)/shard_map/ppermute | solution.py:180
  173.8 20.3 %all-to-all-start.5 = ((f32[128,1,128]{2,1,0:T(1,128)}), f32[128,1,128]{2,1,0:T(1,128)S(1)}, u32[]{:S(2)}, u32[]{:S(2)}) async-start(f32[128,1,128]{2,1,0:T(1,128)} %bitcast.5), calls=%async_computation.5 | async-start | bytes 131072 | tf_op jit(solution)/shard_map/all_to_all | solution.py:183
  194.1 0.9 copy-start.1
Sparse Core Ops, SparseCore 0:
  10.1 45.4 all-gather.2
  113.3 35.0 reduce-scatter.1

commit v2 on v1

v2 whole, which is shorter than its diff:
```python
import jax
import jax.numpy as jnp
from jax import lax
from jax.experimental import pallas as pl
from jax.experimental.pallas import tpu as pltpu
from jax.sharding import Mesh, PartitionSpec as P

MODEL_WIDTH = 7168
BLOCK = 128
TOKENS = 4096
NX, NZ, NY, NC = 4, 8, 8, 2
ROWS = 128
FEATS = 224
COLS = 256
WIDTH = 896
eps = 1e-06
BF16, F32 = jnp.bfloat16, jnp.float32
VMEM = pl.BlockSpec(memory_space=pltpu.VMEM)
ANY = pl.BlockSpec(memory_space=pl.ANY)
MIB = 1024 * 1024


def start_all(copies):
    for copy in copies:
        copy.start()
    return copies


def wait_all(copies):
    for copy in copies:
        copy.wait()


def weight_copies(blocks, weight, sems):
    x = lax.axis_index("x")
    copies = []
    for k, block in enumerate(blocks):
        start = pl.multiple_of(FEATS * lax.rem(x + NX - k, NX), 32)
        copies.append(pltpu.make_async_copy(block, weight.at[pl.ds(start, FEATS), :], sems.at[k]))
    return copies


def cot_copies(own, other, cot, sems):
    core = lax.axis_index("c")
    copies = []
    for m in range(8):
        for which, (block, parity) in enumerate(((own, core), (other, 1 - core))):
            start = pl.multiple_of(512 * (m % 2) + COLS * parity, COLS)
            place = cot.at[pl.ds(FEATS * (m // 2), FEATS), pl.ds(start, COLS)]
            copies.append(pltpu.make_async_copy(block.at[m], place, sems.at[4 + 2 * m + which]))
    return copies


def input_grad_kernel(own, other, w0, w1, w2, w3, grad, cot, weight, sems):
    wait_all(start_all(weight_copies((w0, w1, w2, w3), weight, sems) + cot_copies(own, other, cot, sems)))
    for j in range(4):
        part = lax.dot_general(
            cot[:, COLS * j : COLS * (j + 1)], weight[...], (((0,), (0,)), ((), ())), preferred_element_type=F32
        )
        grad[2 * j : 2 * j + 2] = part.astype(BF16).reshape(2, ROWS, WIDTH)


def forward_kernel(joined_in, gain, w0, w1, w2, w3, keep, send, squares, joined, weight, sems):
    core = lax.axis_index("c")
    copies = weight_copies((w0, w1, w2, w3), weight, sems)
    tokens = pltpu.make_async_copy(joined_in, joined, sems.at[4])
    start_all(copies + [tokens])
    wait_all(copies)
    weight[...] = (weight[...].astype(F32) * gain[...]).astype(BF16)
    tokens.wait()
    for j in range(4):
        rows = joined[2 * j : 2 * j + 2].reshape(COLS, WIDTH)
        part = lax.dot_general(
            weight[...], rows, (((1,), (1,)), ((), ())), preferred_element_type=F32
        ).astype(BF16)

        @pl.when(core == j % 2)
        def _():
            for i in range(4):
                keep[2 * i + j // 2] = part[FEATS * i : FEATS * (i + 1)]

        @pl.when(core != j % 2)
        def _():
            for i in range(4):
                send[2 * i + j // 2] = part[FEATS * i : FEATS * (i + 1)]

    lane = lax.broadcasted_iota(jnp.int32, (ROWS, ROWS), 1)
    sums = jnp.zeros((ROWS, ROWS), F32)
    for z in range(NZ):
        value = joined[z].astype(F32)
        sums = jnp.where(lane == z, jnp.sum(value * value, axis=1, keepdims=True), sums)
    squares[...] = sums.T[:NZ]


def project_kernel(ss, parts, out):
    j = 2 * lax.rem(lax.axis_index("y"), 2) + lax.axis_index("c")
    row = lax.broadcasted_iota(jnp.int32, (NZ, ROWS), 0)
    total = jnp.zeros((FEATS, COLS), F32)
    for half in range(2):
        scales = half_scales(ss, half)
        pair = [jnp.sum(jnp.where(row == 2 * j + i, scales, 0.0), axis=0, keepdims=True) for i in range(2)]
        part = parts[4 * half].astype(F32)
        for y in range(4 * half + 1, 4 * half + 4):
            part = part + parts[y].astype(F32)
        total = total + part * jnp.concatenate(pair, axis=1)
    out[...] = total.astype(BF16)


def weight_grad_kernel(ss, gain, own, other, joined_in, mine, o1, o2, o3, cot, joined, sems):
    x = lax.axis_index("x")
    copies = cot_copies(own, other, cot, sems)
    rows = pltpu.make_async_copy(joined_in, joined, sems.at[0])
    start_all(copies + [rows])
    scales = row_scales(ss)
    wait_all(copies)
    for z in range(NZ):
        part = cot[:, ROWS * z : ROWS * (z + 1)].astype(F32) * scales[z : z + 1]
        cot[:, ROWS * z : ROWS * (z + 1)] = part.astype(BF16)
    rows.wait()
    tokens = joined[...].reshape(NZ * ROWS, WIDTH)
    columns = gain[...] * (1.0 / 64.0)
    for k, out in enumerate((mine, o1, o2, o3)):
        start = pl.multiple_of(FEATS * lax.rem(x + k, NX), 32)
        part = jnp.dot(cot[pl.ds(start, FEATS), :], tokens, preferred_element_type=F32)
        out[...] = (part * columns).astype(out.dtype)


def half_scales(ss, half):
    return lax.rsqrt(ss[half] / MODEL_WIDTH + eps)


def row_scales(ss):
    return jnp.where(lax.axis_index("y") < NY // 2, half_scales(ss, 0), half_scales(ss, 1))


def column(row):
    return jnp.broadcast_to(row, (8, ROWS)).T[:, :1]


def own_scale(ss):
    scales = row_scales(ss)
    mine = lax.broadcasted_iota(jnp.int32, scales.shape, 0) == lax.axis_index("z")
    return column(jnp.sum(jnp.where(mine, scales, 0.0), axis=0, keepdims=True))


def dots_kernel(ss, grad, joined, gain, out):
    u = grad[...].astype(F32) * gain[...]
    xhat = joined[...].astype(F32) * own_scale(ss)
    dots = jnp.sum(u * xhat, axis=1, keepdims=True)
    out[...] = jnp.broadcast_to(dots, (ROWS, ROWS)).T[:1]


def joined_grad_kernel(ss, dots, grad, joined, gain, out):
    c = column(half_sum(dots[...]) / MODEL_WIDTH)
    scale = own_scale(ss)
    u = grad[...].astype(F32) * gain[...]
    xhat = joined[...].astype(F32) * scale
    out[...] = (scale * (u - xhat * c)).astype(BF16)


def half_sum(rows):
    first = jnp.sum(rows[:8], axis=0, keepdims=True)
    second = jnp.sum(rows[8:], axis=0, keepdims=True)
    return jnp.where(lax.axis_index("y") < NY // 2, first, second)


def over_tp(rows):
    return lax.all_to_all(jnp.broadcast_to(rows[None], (NY * NC,) + rows.shape), ("y", "c"), 0, 0)


def transposed():
    return [(x * NY + y, (y // 2) * NY + 2 * x + y % 2) for x in range(NX) for y in range(NY)]


def shifted(value, k):
    return lax.ppermute(value, "x", [(i, (i + k) % NX) for i in range(NX)])


def kernel(body, name, outs, flops, specs, out_specs=None, scratch=(), limit=40):
    return pl.pallas_call(
        body,
        out_shape=tuple(jax.ShapeDtypeStruct(shape, dtype) for shape, dtype in outs),
        in_specs=specs,
        out_specs=out_specs or (VMEM,) * len(outs),
        scratch_shapes=scratch,
        compiler_params=pltpu.CompilerParams(vmem_limit_bytes=limit * MIB),
        cost_estimate=pl.CostEstimate(flops=flops, bytes_accessed=6 << 20, transcendentals=0),
        name=name,
    )


def per_device(joined, gain, weight_codes, scale_exp, cotangent):
    swap = [(0, 1), (1, 0)]
    flops = 2 * 1024 * WIDTH * WIDTH
    bricks, square, blocks, block = (NZ, ROWS, WIDTH), (WIDTH, WIDTH), (8, FEATS, COLS), (FEATS, WIDTH)
    gain = gain[None, :]
    joined_all = lax.all_gather(joined, "z")
    cot = lax.ppermute(cotangent.T, ("x", "y"), transposed())

    factor = jnp.repeat(jnp.exp2(scale_exp.astype(F32)), BLOCK, axis=1)
    weight = (weight_codes.astype(F32) * factor).astype(BF16)
    weights = [weight] + [shifted(weight, k) for k in (1, 2, 3)]

    own = lax.all_gather(cot, "y")
    own, weights = lax.optimization_barrier((own, weights))
    other = lax.ppermute(own, "c", swap)

    scratch = [pltpu.VMEM((WIDTH, 1024), BF16), pltpu.VMEM(square, BF16), pltpu.VMEM(bricks, BF16), pltpu.SemaphoreType.DMA((21,))]
    (grad,) = kernel(
        input_grad_kernel,
        "input_grad",
        ((bricks, BF16),),
        flops,
        [ANY] * 6,
        scratch=[scratch[0], scratch[1], scratch[3]],
    )(own, other, *weights)
    grad = lax.psum_scatter(grad, "z")

    keep, send, squares = kernel(
        forward_kernel,
        "forward",
        ((blocks, BF16), (blocks, BF16), ((NZ, ROWS), F32)),
        flops,
        [ANY, VMEM, ANY, ANY, ANY, ANY],
        scratch=[scratch[2], scratch[1], scratch[3]],
    )(joined_all, gain, *weights)
    got = lax.ppermute(send, "c", swap)
    squares = over_tp(squares)
    squares = jnp.stack([jnp.sum(squares[:8], axis=0), jnp.sum(squares[8:], axis=0)])

    mine, *others = kernel(
        weight_grad_kernel,
        "weight_grad",
        ((block, F32), (block, BF16), (block, BF16), (block, BF16)),
        flops,
        [VMEM, VMEM, ANY, ANY, ANY],
        scratch=[scratch[0], scratch[2], scratch[3]],
    )(squares, gain, own, other, joined_all)
    others = [shifted(other, k + 1) for k, other in enumerate(others)]

    both = (keep.astype(F32) + got.astype(F32)).astype(BF16)
    both, squares = lax.optimization_barrier((both, squares))
    parts = lax.all_to_all(both, "y", 0, 0)
    (projected,) = kernel(project_kernel, "project", (((FEATS, COLS), BF16),), 16 * FEATS * COLS, [VMEM] * 2)(squares, parts)
    projected = lax.ppermute(projected, ("x", "y"), transposed()).T
    weight_grad = mine + others[0].astype(F32) + others[1].astype(F32) + others[2].astype(F32)

    (dots,) = kernel(dots_kernel, "dots", (((1, ROWS), F32),), 4 * ROWS * WIDTH, [VMEM] * 4)(squares, grad, joined, gain)
    dots = over_tp(dots).reshape(NY * NC, ROWS)
    (joined_gradient,) = kernel(
        joined_grad_kernel, "joined_grad", (((ROWS, WIDTH), BF16),), 8 * ROWS * WIDTH, [VMEM] * 5
    )(squares, dots, grad, joined, gain)
    return (projected, joined_gradient, weight_grad)


def solution(mesh):
    grid = Mesh(mesh.devices.reshape(NX, NZ, NY, NC), ("x", "z", "y", "c"))
    seq, tp = ("x", "z"), ("y", "c")
    in_specs = (P(seq, tp), P(tp), P(seq, tp), P(seq, tp), P(tp, seq))
    out_specs = (P(tp, seq), P(seq, tp), P(seq, tp))
    return jax.shard_map(per_device, mesh=grid, in_specs=in_specs, out_specs=out_specs, check_vma=False)
```

time: 204 us -> 147 us (0.72)
  the two profiles are of different devices: /device:TPU:1 before, /device:TPU:433 now
where the time goes in v2:
time: 147 us
  starting transfers between devices  50.7 us (34%)
  blocking collectives  31.7 us (22%)
  waiting for transfers between devices  19.5 us (13%)
  Pallas kernels  16.7 us (11%)
  between operations  14.3 us (10%)
  local copies, waits for them, and re-layouts  8.44 us (6%)
  other arithmetic  5.29 us (4%)
    all_gather x1, blocking collectives, per_device(): own = lax.all_gather(cot, 'y')  22 us
    ppermute x6, starting transfers between devices, shifted(): return lax.ppermute(value, 'x', [(i, (i + k) % NX) for i in range(NX)])  20.3 us
    ppermute x1, waiting for transfers between devices, per_device(): projected = lax.ppermute(projected, ('x', 'y'), transposed()).T  10.9 us
    all_to_all x1, blocking collectives, over_tp(): lax.all_to_all(jnp.broadcast_to(rows[None], (NY * NC,) + rows.shape), ('y...  9.74 us
    ppermute x1, starting transfers between devices, per_device(): other = lax.ppermute(own, 'c', swap)  8.35 us
    unnamed x17, local copies, waits for them, and re-layouts  7.4 us
    all_to_all x1, starting transfers between devices, over_tp(): lax.all_to_all(jnp.broadcast_to(rows[None], (NY * NC,) + rows.shape), ('y...  7.24 us
    all_to_all x1, starting transfers between devices, per_device(): parts = lax.all_to_all(both, 'y', 0, 0)  6.79 us
  transfers between devices with their start and end apart: 14, of which 3 were waited for; matrix products, arithmetic and copies ran while one was open for 4% of the time, Pallas kernels for 11%

profile of v2, /device:TPU:433, one launch (start us, length us, event | category | flops | bytes accessed | tf_op | source)
XLA Modules:
  0.0 146.7 jit_solution(10640588478585144110)
XLA Ops:
  7.2 0.7 all-gather.4.cloned.1.call-update
  7.9 3.7 %collective-permute-start = (bf16[224,256]{1,0:T(8,128)(2,1)}, bf16[224,256]{1,0:T(8,128)(2,1)S(1)}, u32[]{:S(2)}, u32[]{:S(2)}) collective-permute-start(bf16[224,256]{1,0:T(8,128)(2,1)} %bitcast.27), channel_id=1, source_target_pairs={{0,0},{2,2},{4,128},{6,130},{8,256},{10,258},{12,384},{14,386},{12... | collective-permute-start | bytes 344072 | tf_op jit(solution)/shard_map/ppermute | solution.py:198
  11.7 0.7 multiply_exponential_fusion
  12.8 1.2 fusion.w0
  14.0 4.5 %collective-permute-start.1 = (bf16[224,896]{1,0:T(8,128)(2,1)S(1)}, bf16[224,896]{1,0:T(8,128)(2,1)S(1)}, u32[]{:S(2)}, u32[]{:S(2)}) collective-permute-start(bf16[224,896]{1,0:T(8,128)(2,1)S(1)} %fusion.w0), channel_id=1, source_target_pairs={{0,128},{128,256},{256,384},{384,0},{1,129},{129,257},{257,385},{3... | collective-permute-start | bytes 1204232 | tf_op jit(solution)/shard_map/ppermute | solution.py:176
  18.5 2.8 %collective-permute-start.2 = (bf16[224,896]{1,0:T(8,128)(2,1)S(1)}, bf16[224,896]{1,0:T(8,128)(2,1)S(1)}, u32[]{:S(2)}, u32[]{:S(2)}) collective-permute-start(bf16[224,896]{1,0:T(8,128)(2,1)S(1)} %fusion.w0), channel_id=1, source_target_pairs={{0,256},{128,384},{256,0},{384,128},{1,257},{129,385},{257,1},{385... | collective-permute-start | bytes 1204232 | tf_op jit(solution)/shard_map/ppermute | solution.py:176
  21.3 4.0 %collective-permute-start.3 = (bf16[224,896]{1,0:T(8,128)(2,1)S(1)}, bf16[224,896]{1,0:T(8,128)(2,1)S(1)}, u32[]{:S(2)}, u32[]{:S(2)}) collective-permute-start(bf16[224,896]{1,0:T(8,128)(2,1)S(1)} %fusion.w0), channel_id=1, source_target_pairs={{0,384},{128,0},{256,128},{384,256},{1,385},{129,1},{257,129},{385... | collective-permute-start | bytes 1204232 | tf_op jit(solution)/shard_map/ppermute | solution.py:176
  25.3 22.0 %all-gather.1 = bf16[1792,256]{1,0:T(8,128)(2,1)S(1)} all-gather(bf16[224,256]{1,0:T(8,128)(2,1)S(1)} %collective-permute-done), channel_id=3, replica_groups=mesh['x'=4,'z'=8,'y'=8,'c'=2] {'y'}, dimensions={0}, use_global_device_ids=true | all-gather | bytes 1032192 | tf_op jit(solution)/shard_map/all_gather | solution.py:204
  47.3 8.3 %collective-permute-start.6 = (bf16[8,224,256]{2,1,0:T(8,128)(2,1)S(1)}, bf16[8,224,256]{2,1,0:T(8,128)(2,1)S(1)}, u32[]{:S(2)}, u32[]{:S(2)}) collective-permute-start(bf16[8,224,256]{2,1,0:T(8,128)(2,1)S(1)} %bitcast.16), channel_id=1, source_target_pairs={{0,1},{1,0},{2,3},{3,2},{4,5},{5,4},{6,7},{7,6},{8,9},{9,8},{10,11... | collective-permute-start | bytes 2752520 | tf_op jit(solution)/shard_map/ppermute | solution.py:206
  55.6 2.1 %collective-permute-done.6.other = bf16[8,224,256]{2,1,0:T(8,128)(2,1)S(1)} collective-permute-done((bf16[8,224,256]{2,1,0:T(8,128)(2,1)S(1)}, bf16[8,224,256]{2,1,0:T(8,128)(2,1)S(1)}, u32[]{:S(2)}, u32[]{:S(2)}) %collective-permute-start.6) | collective-permute-done | bytes 917536 | tf_op jit(solution)/shard_map/ppermute | solution.py:206
  57.7 4.8 %input_grad.1 = bf16[8,128,896]{2,1,0:T(8,128)(2,1)} custom-call(bf16[8,224,256]{2,1,0:T(8,128)(2,1)S(1)} %bitcast.17, bf16[8,224,256]{2,1,0:T(8,128)(2,1)S(1)} %collective-permute-done.6.other, bf16[224,896]{1,0:T(8,128)(2,1)S(1)} %fusion.w0, bf16[224,896]{1,0:T(8,128)(2,1)S(1)} %collective-permute-done.1.w1, ...), custom_call_target="tpu_custom_call" | custom-call | flops 1644167168 | bytes 6291456 | tf_op jit(solution)/shard_map/input_grad/pallas_call | solution.py:209
  62.5 0.9 copy-done.5
  63.5 0.7 copy-done.7
  64.2 1.5 %copy-done.3 = bf16[1024,896]{1,0:T(8,128)(2,1)S(1)} copy-done((bf16[1024,896]{1,0:T(8,128)(2,1)S(1)}, bf16[1024,896]{1,0:T(8,128)(2,1)}, u32[]{:S(2)}) %copy-start.3) | copy-done | bytes 1835032
  65.7 6.5 %forward.1 = (bf16[8,224,256]{2,1,0:T(8,128)(2,1)S(1)}, bf16[8,224,256]{2,1,0:T(8,128)(2,1)S(1)}, f32[8,128]{1,0:T(8,128)S(1)}) custom-call(bf16[8,128,896]{2,1,0:T(8,128)(2,1)S(1)} %bitcast.21, f32[1,896]{1,0:T(1,128)S(1)} %broadcast_in_dim.20.gain, bf16[224,896]{1,0:T(8,128)(2,1)S(1)} %fusion.w0, bf16[224,896]{1,0:T(8,128)(2,1)S(1)} %collective-permute-done.1.w1, ...), custom_call_target="tpu_custom_call" | custom-call | flops 1644167168 | bytes 6291456 | tf_op jit(solution)/shard_map/forward/pallas_call | solution.py:219
  72.2 2.3 %collective-permute-start.4 = (bf16[8,224,256]{2,1,0:T(8,128)(2,1)S(1)}, bf16[8,224,256]{2,1,0:T(8,128)(2,1)S(1)}, u32[]{:S(2)}, u32[]{:S(2)}) collective-permute-start(bf16[8,224,256]{2,1,0:T(8,128)(2,1)S(1)} %get-tuple-element.22), channel_id=1, source_target_pairs={{0,1},{1,0},{2,3},{3,2},{4,5},{5,4},{6,7},{7,6},{8,9},{9,8},{10,11... | collective-permute-start | bytes 2752520 | tf_op jit(solution)/shard_map/ppermute | solution.py:227
  74.5 9.7 %all_to_all.15 = f32[16,8,128]{2,1,0:T(8,128)S(1)} all-to-all(f32[16,8,128]{2,1,0:T(8,128)S(1)} %broadcast_in_dim.22), channel_id=1, replica_groups=mesh['x'=4,'z'=8,'y'=8,'c'=2] {'y','c'}, dimensions={0} | all-to-all | bytes 131072 | tf_op jit(solution)/shard_map/all_to_all | solution.py:168
  84.2 1.2 add_convert_fusion
  85.4 6.8 %all-to-all-start.1 = ((bf16[8,224,256]{2,1,0:T(8,128)(2,1)}), bf16[8,224,256]{2,1,0:T(8,128)(2,1)S(1)}, u32[]{:S(2)}, u32[]{:S(2)}) async-start(bf16[8,224,256]{2,1,0:T(8,128)(2,1)} %add_convert_fusion), calls=%async_computation.1 | async-start | bytes 1835008 | tf_op jit(solution)/shard_map/all_to_all | solution.py:243
  92.2 1.5 %copy-done.4 = bf16[1024,896]{1,0:T(8,128)(2,1)S(1)} copy-done((bf16[1024,896]{1,0:T(8,128)(2,1)S(1)}, bf16[1024,896]{1,0:T(8,128)(2,1)}, u32[]{:S(2)}) %copy-start.4) | copy-done | bytes 1835032
  93.7 1.2 copy-done.6
  94.9 4.0 %weight_grad.1 = (f32[224,896]{1,0:T(8,128)S(1)}, bf16[224,896]{1,0:T(8,128)(2,1)S(1)}, bf16[224,896]{1,0:T(8,128)(2,1)}, bf16[224,896]{1,0:T(8,128)(2,1)}) custom-call(f32[2,8,128]{2,1,0:T(8,128)S(1)} %pad_maximum_fusion.ss, f32[1,896]{1,0:T(1,128)S(1)} %broadcast_in_dim.20.gain, bf16[8,224,256]{2,1,0:T(8,128)(2,1)S(1)} %bitcast.18, ...), custom_call_target="tpu_custom_call" | custom-call | flops 1644167168 | bytes 6291456 | tf_op jit(solution)/shard_map/weight_grad/pallas_call | solution.py:231
  98.9 2.0 %collective-permute-start.9 = (bf16[224,896]{1,0:T(8,128)(2,1)}, bf16[224,896]{1,0:T(8,128)(2,1)S(1)}, u32[]{:S(2)}, u32[]{:S(2)}) collective-permute-start(bf16[224,896]{1,0:T(8,128)(2,1)} %get-tuple-element.30), channel_id=1, source_target_pairs={{0,384},{128,0},{256,128},{384,256},{1,385},{129,1},{257,129},{385... | collective-permute-start | bytes 1204232 | tf_op jit(solution)/shard_map/ppermute | solution.py:176
  100.9 5.2 %collective-permute-start.8 = (bf16[224,896]{1,0:T(8,128)(2,1)}, bf16[224,896]{1,0:T(8,128)(2,1)}, u32[]{:S(2)}, u32[]{:S(2)}) collective-permute-start(bf16[224,896]{1,0:T(8,128)(2,1)} %get-tuple-element.29), channel_id=1, source_target_pairs={{0,256},{128,384},{256,0},{384,128},{1,257},{129,385},{257,1},{385... | collective-permute-start | bytes 1204232 | tf_op jit(solution)/shard_map/ppermute | solution.py:176
  106.1 1.9 %collective-permute-start.7 = (bf16[224,896]{1,0:T(8,128)(2,1)S(1)}, bf16[224,896]{1,0:T(8,128)(2,1)}, u32[]{:S(2)}, u32[]{:S(2)}) collective-permute-start(bf16[224,896]{1,0:T(8,128)(2,1)S(1)} %get-tuple-element.28), channel_id=1, source_target_pairs={{0,128},{128,256},{256,384},{384,0},{1,129},{129,257},{257,385},{3... | collective-permute-start | bytes 1204232 | tf_op jit(solution)/shard_map/ppermute | solution.py:176
  108.1 0.9 copy-done.1
  109.3 5.8 %all-to-all-done.1.parts = bf16[8,224,256]{2,1,0:T(8,128)(2,1)S(1)} async-done(((bf16[8,224,256]{2,1,0:T(8,128)(2,1)}), bf16[8,224,256]{2,1,0:T(8,128)(2,1)S(1)}, u32[]{:S(2)}, u32[]{:S(2)}) %all-to-all-start.1) | async-done | bytes 917536 | tf_op jit(solution)/shard_map/all_to_all | solution.py:243
  115.7 7.2 %all-to-all-start.2 = ((f32[16,1,128]{2,1,0:T(1,128)}), f32[16,1,128]{2,1,0:T(1,128)S(1)}, u32[]{:S(2)}, u32[]{:S(2)}) async-start(f32[16,1,128]{2,1,0:T(1,128)} %broadcast_in_dim.24), calls=%async_computation.3 | async-start | bytes 16384 | tf_op jit(solution)/shard_map/all_to_all | solution.py:168
  123.1 1.9 %collective-permute-start.5 = (bf16[224,256]{1,0:T(8,128)(2,1)S(1)}, bf16[224,256]{1,0:T(8,128)(2,1)S(1)}, u32[]{:S(2)}, u32[]{:S(2)}) collective-permute-start(bf16[224,256]{1,0:T(8,128)(2,1)S(1)} %project.1), channel_id=1, source_target_pairs={{0,0},{2,2},{4,128},{6,130},{8,256},{10,258},{12,384},{14,386},{12... | collective-permute-start | bytes 344072 | tf_op jit(solution)/shard_map/ppermute | solution.py:245
  125.1 2.2 %convert_add_fusion = f32[224,896]{1,0:T(8,128)} fusion(bf16[224,896]{1,0:T(8,128)(2,1)S(1)} %collective-permute-done.9, bf16[224,896]{1,0:T(8,128)(2,1)} %collective-permute-done.8, f32[224,896]{1,0:T(8,128)S(1)} %get-tuple-element.27, bf16[224,896]{1,0:T(8,128)(2,1)} %collective-permute-done.7), kind=kLoop, calls=%fused_computation.3 | loop fusion | flops 1204224 | bytes 2809856 | tf_op jit(solution)/shard_map/add | solution.py:246
  127.3 1.0 joined_grad.1
  128.2 10.9 %collective-permute-done.5 = bf16[224,256]{1,0:T(8,128)(2,1)S(1)} collective-permute-done((bf16[224,256]{1,0:T(8,128)(2,1)S(1)}, bf16[224,256]{1,0:T(8,128)(2,1)S(1)}, u32[]{:S(2)}, u32[]{:S(2)}) %collective-permute-start.5) | collective-permute-done | bytes 114720 | tf_op jit(solution)/shard_map/ppermute | solution.py:245
  (34 shorter events, 2.3 us)
Async XLA Ops:
  7.2 57.0 %all-gather.4.cloned.1.call-start = ((), (), s32[]{:S(2)}) async-start(), calls=%async_computation.5 | async-start | bytes 2064384 | tf_op jit(solution)/shard_map/all_gather | solution.py:197
  7.9 100.2 %reduce-scatter.2.cloned.1.call-start = ((), (), s32[]{:S(2)}) async-start(), calls=%async_computation.4 | async-start | bytes 2064384 | tf_op jit(solution)/shard_map/reduce_scatter | solution.py:217
  7.9 17.3 %collective-permute-start = (bf16[224,256]{1,0:T(8,128)(2,1)}, bf16[224,256]{1,0:T(8,128)(2,1)S(1)}, u32[]{:S(2)}, u32[]{:S(2)}) collective-permute-start(bf16[224,256]{1,0:T(8,128)(2,1)} %bitcast.27), channel_id=1, source_target_pairs={{0,0},{2,2},{4,128},{6,130},{8,256},{10,258},{12,384},{14,386},{12... | collective-permute-start | bytes 344072 | tf_op jit(solution)/shard_map/ppermute | solution.py:198
  14.0 33.2 %collective-permute-start.1 = (bf16[224,896]{1,0:T(8,128)(2,1)S(1)}, bf16[224,896]{1,0:T(8,128)(2,1)S(1)}, u32[]{:S(2)}, u32[]{:S(2)}) collective-permute-start(bf16[224,896]{1,0:T(8,128)(2,1)S(1)} %fusion.w0), channel_id=1, source_target_pairs={{0,128},{128,256},{256,384},{384,0},{1,129},{129,257},{257,385},{3... | collective-permute-start | bytes 1204232 | tf_op jit(solution)/shard_map/ppermute | solution.py:176
  18.5 28.7 %collective-permute-start.2 = (bf16[224,896]{1,0:T(8,128)(2,1)S(1)}, bf16[224,896]{1,0:T(8,128)(2,1)S(1)}, u32[]{:S(2)}, u32[]{:S(2)}) collective-permute-start(bf16[224,896]{1,0:T(8,128)(2,1)S(1)} %fusion.w0), channel_id=1, source_target_pairs={{0,256},{128,384},{256,0},{384,128},{1,257},{129,385},{257,1},{385... | collective-permute-start | bytes 1204232 | tf_op jit(solution)/shard_map/ppermute | solution.py:176
  21.3 26.0 %collective-permute-start.3 = (bf16[224,896]{1,0:T(8,128)(2,1)S(1)}, bf16[224,896]{1,0:T(8,128)(2,1)S(1)}, u32[]{:S(2)}, u32[]{:S(2)}) collective-permute-start(bf16[224,896]{1,0:T(8,128)(2,1)S(1)} %fusion.w0), channel_id=1, source_target_pairs={{0,384},{128,0},{256,128},{384,256},{1,385},{129,1},{257,129},{385... | collective-permute-start | bytes 1204232 | tf_op jit(solution)/shard_map/ppermute | solution.py:176
  47.3 10.4 %collective-permute-start.6 = (bf16[8,224,256]{2,1,0:T(8,128)(2,1)S(1)}, bf16[8,224,256]{2,1,0:T(8,128)(2,1)S(1)}, u32[]{:S(2)}, u32[]{:S(2)}) collective-permute-start(bf16[8,224,256]{2,1,0:T(8,128)(2,1)S(1)} %bitcast.16), channel_id=1, source_target_pairs={{0,1},{1,0},{2,3},{3,2},{4,5},{5,4},{6,7},{7,6},{8,9},{9,8},{10,11... | collective-permute-start | bytes 2752520 | tf_op jit(solution)/shard_map/ppermute | solution.py:206
  62.5 1.0 copy-start.5
  63.5 0.7 copy-start.7
  64.2 1.5 %copy-start.3 = (bf16[1024,896]{1,0:T(8,128)(2,1)S(1)}, bf16[1024,896]{1,0:T(8,128)(2,1)}, u32[]{:S(2)}) copy-start(bf16[1024,896]{1,0:T(8,128)(2,1)} %all-gather.4.cloned.1.call-done) | copy-start | bytes 5505028
  72.2 12.1 %collective-permute-start.4 = (bf16[8,224,256]{2,1,0:T(8,128)(2,1)S(1)}, bf16[8,224,256]{2,1,0:T(8,128)(2,1)S(1)}, u32[]{:S(2)}, u32[]{:S(2)}) collective-permute-start(bf16[8,224,256]{2,1,0:T(8,128)(2,1)S(1)} %get-tuple-element.22), channel_id=1, source_target_pairs={{0,1},{1,0},{2,3},{3,2},{4,5},{5,4},{6,7},{7,6},{8,9},{9,8},{10,11... | collective-permute-start | bytes 2752520 | tf_op jit(solution)/shard_map/ppermute | solution.py:227
  85.4 29.7 %all-to-all-start.1 = ((bf16[8,224,256]{2,1,0:T(8,128)(2,1)}), bf16[8,224,256]{2,1,0:T(8,128)(2,1)S(1)}, u32[]{:S(2)}, u32[]{:S(2)}) async-start(bf16[8,224,256]{2,1,0:T(8,128)(2,1)} %add_convert_fusion), calls=%async_computation.1 | async-start | bytes 1835008 | tf_op jit(solution)/shard_map/all_to_all | solution.py:243
  92.2 1.5 %copy-start.4 = (bf16[1024,896]{1,0:T(8,128)(2,1)S(1)}, bf16[1024,896]{1,0:T(8,128)(2,1)}, u32[]{:S(2)}) copy-start(bf16[1024,896]{1,0:T(8,128)(2,1)} %all-gather.4.cloned.1.call-done) | copy-start | bytes 5505028
  93.7 1.2 copy-start.6
  94.9 13.1 %copy-start = (bf16[128,896]{1,0:T(8,128)(2,1)S(1)}, bf16[128,896]{1,0:T(8,128)(2,1)}, u32[]{:S(2)}) copy-start(bf16[128,896]{1,0:T(8,128)(2,1)} %joined.3) | copy-start | bytes 688132
  98.9 26.1 %collective-permute-start.9 = (bf16[224,896]{1,0:T(8,128)(2,1)}, bf16[224,896]{1,0:T(8,128)(2,1)S(1)}, u32[]{:S(2)}, u32[]{:S(2)}) collective-permute-start(bf16[224,896]{1,0:T(8,128)(2,1)} %get-tuple-element.30), channel_id=1, source_target_pairs={{0,384},{128,0},{256,128},{384,256},{1,385},{129,1},{257,129},{385... | collective-permute-start | bytes 1204232 | tf_op jit(solution)/shard_map/ppermute | solution.py:176
  100.9 24.1 %collective-permute-start.8 = (bf16[224,896]{1,0:T(8,128)(2,1)}, bf16[224,896]{1,0:T(8,128)(2,1)}, u32[]{:S(2)}, u32[]{:S(2)}) collective-permute-start(bf16[224,896]{1,0:T(8,128)(2,1)} %get-tuple-element.29), channel_id=1, source_target_pairs={{0,256},{128,384},{256,0},{384,128},{1,257},{129,385},{257,1},{385... | collective-permute-start | bytes 1204232 | tf_op jit(solution)/shard_map/ppermute | solution.py:176
  106.1 18.9 %collective-permute-start.7 = (bf16[224,896]{1,0:T(8,128)(2,1)S(1)}, bf16[224,896]{1,0:T(8,128)(2,1)}, u32[]{:S(2)}, u32[]{:S(2)}) collective-permute-start(bf16[224,896]{1,0:T(8,128)(2,1)S(1)} %get-tuple-element.28), channel_id=1, source_target_pairs={{0,128},{128,256},{256,384},{384,0},{1,129},{129,257},{257,385},{3... | collective-permute-start | bytes 1204232 | tf_op jit(solution)/shard_map/ppermute | solution.py:176
  108.1 0.9 copy-start.1
  115.7 11.5 %all-to-all-start.2 = ((f32[16,1,128]{2,1,0:T(1,128)}), f32[16,1,128]{2,1,0:T(1,128)S(1)}, u32[]{:S(2)}, u32[]{:S(2)}) async-start(f32[16,1,128]{2,1,0:T(1,128)} %broadcast_in_dim.24), calls=%async_computation.3 | async-start | bytes 16384 | tf_op jit(solution)/shard_map/all_to_all | solution.py:168
  122.9 4.3 %copy-start.2 = (bf16[1,128,896]{2,1,0:T(8,128)(2,1)S(1)}, bf16[1,128,896]{2,1,0:T(8,128)(2,1)}, u32[]{:S(2)}) copy-start(bf16[1,128,896]{2,1,0:T(8,128)(2,1)} %reduce-scatter.2.cloned.1.call-done) | copy-start | bytes 688132
  123.1 16.1 %collective-permute-start.5 = (bf16[224,256]{1,0:T(8,128)(2,1)S(1)}, bf16[224,256]{1,0:T(8,128)(2,1)S(1)}, u32[]{:S(2)}, u32[]{:S(2)}) collective-permute-start(bf16[224,256]{1,0:T(8,128)(2,1)S(1)} %project.1), channel_id=1, source_target_pairs={{0,0},{2,2},{4,128},{6,130},{8,256},{10,258},{12,384},{14,386},{12... | collective-permute-start | bytes 344072 | tf_op jit(solution)/shard_map/ppermute | solution.py:245
Sparse Core Ops, SparseCore 0:
  10.1 37.2 all-gather.3
  63.6 34.5 reduce-scatter.1

commit v3 on v2

--- a/solution.py
+++ b/solution.py
@@ -31,15 +31,6 @@
         copy.wait()
 
 
-def weight_copies(blocks, weight, sems):
-    x = lax.axis_index("x")
-    copies = []
-    for k, block in enumerate(blocks):
-        start = pl.multiple_of(FEATS * lax.rem(x + NX - k, NX), 32)
-        copies.append(pltpu.make_async_copy(block, weight.at[pl.ds(start, FEATS), :], sems.at[k]))
-    return copies
-
-
 def cot_copies(own, other, cot, sems):
     core = lax.axis_index("c")
     copies = []
@@ -47,12 +38,12 @@
         for which, (block, parity) in enumerate(((own, core), (other, 1 - core))):
             start = pl.multiple_of(512 * (m % 2) + COLS * parity, COLS)
             place = cot.at[pl.ds(FEATS * (m // 2), FEATS), pl.ds(start, COLS)]
-            copies.append(pltpu.make_async_copy(block.at[m], place, sems.at[4 + 2 * m + which]))
+            copies.append(pltpu.make_async_copy(block.at[m], place, sems.at[2 * m + which]))
     return copies
 
 
-def input_grad_kernel(own, other, w0, w1, w2, w3, grad, cot, weight, sems):
-    wait_all(start_all(weight_copies((w0, w1, w2, w3), weight, sems) + cot_copies(own, other, cot, sems)))
+def input_grad_kernel(own, other, weight, grad, cot, sems):
+    wait_all(start_all(cot_copies(own, other, cot, sems)))
     for j in range(4):
         part = lax.dot_general(
             cot[:, COLS * j : COLS * (j + 1)], weight[...], (((0,), (0,)), ((), ())), preferred_element_type=F32
@@ -60,14 +51,9 @@
         grad[2 * j : 2 * j + 2] = part.astype(BF16).reshape(2, ROWS, WIDTH)
 
 
-def forward_kernel(joined_in, gain, w0, w1, w2, w3, keep, send, squares, joined, weight, sems):
+def forward_kernel(joined, gain, weight_in, keep, send, squares, weight):
     core = lax.axis_index("c")
-    copies = weight_copies((w0, w1, w2, w3), weight, sems)
-    tokens = pltpu.make_async_copy(joined_in, joined, sems.at[4])
-    start_all(copies + [tokens])
-    wait_all(copies)
-    weight[...] = (weight[...].astype(F32) * gain[...]).astype(BF16)
-    tokens.wait()
+    weight[...] = (weight_in[...].astype(F32) * gain[...]).astype(BF16)
     for j in range(4):
         rows = joined[2 * j : 2 * j + 2].reshape(COLS, WIDTH)
         part = lax.dot_general(
@@ -92,24 +78,21 @@
     squares[...] = sums.T[:NZ]
 
 
-def project_kernel(ss, parts, out):
-    j = 2 * lax.rem(lax.axis_index("y"), 2) + lax.axis_index("c")
+def scale_kernel(ss, keep, got, out):
+    scales = row_scales(ss)
     row = lax.broadcasted_iota(jnp.int32, (NZ, ROWS), 0)
-    total = jnp.zeros((FEATS, COLS), F32)
-    for half in range(2):
-        scales = half_scales(ss, half)
+    for parity in range(2):
+        j = 2 * parity + lax.axis_index("c")
         pair = [jnp.sum(jnp.where(row == 2 * j + i, scales, 0.0), axis=0, keepdims=True) for i in range(2)]
-        part = parts[4 * half].astype(F32)
-        for y in range(4 * half + 1, 4 * half + 4):
-            part = part + parts[y].astype(F32)
-        total = total + part * jnp.concatenate(pair, axis=1)
-    out[...] = total.astype(BF16)
+        scale = jnp.concatenate(pair, axis=1)
+        for m in range(parity, 8, 2):
+            out[m] = ((keep[m].astype(F32) + got[m].astype(F32)) * scale).astype(BF16)
 
 
 def weight_grad_kernel(ss, gain, own, other, joined_in, mine, o1, o2, o3, cot, joined, sems):
     x = lax.axis_index("x")
     copies = cot_copies(own, other, cot, sems)
-    rows = pltpu.make_async_copy(joined_in, joined, sems.at[0])
+    rows = pltpu.make_async_copy(joined_in, joined, sems.at[16])
     start_all(copies + [rows])
     scales = row_scales(ss)
     wait_all(copies)
@@ -125,12 +108,8 @@
         out[...] = (part * columns).astype(out.dtype)
 
 
-def half_scales(ss, half):
-    return lax.rsqrt(ss[half] / MODEL_WIDTH + eps)
-
-
 def row_scales(ss):
-    return jnp.where(lax.axis_index("y") < NY // 2, half_scales(ss, 0), half_scales(ss, 1))
+    return lax.rsqrt(ss[...] / MODEL_WIDTH + eps)
 
 
 def column(row):
@@ -150,22 +129,18 @@
     out[...] = jnp.broadcast_to(dots, (ROWS, ROWS)).T[:1]
 
 
-def joined_grad_kernel(ss, dots, grad, joined, gain, out):
-    c = column(half_sum(dots[...]) / MODEL_WIDTH)
+def last_kernel(ss, dots, grad, joined, gain, mine, o1, o2, o3, out, weight_grad):
+    weight_grad[...] = mine[...] + o1[...].astype(F32) + o2[...].astype(F32) + o3[...].astype(F32)
+    c = column(dots[...] / MODEL_WIDTH)
     scale = own_scale(ss)
     u = grad[...].astype(F32) * gain[...]
     xhat = joined[...].astype(F32) * scale
     out[...] = (scale * (u - xhat * c)).astype(BF16)
 
 
-def half_sum(rows):
-    first = jnp.sum(rows[:8], axis=0, keepdims=True)
-    second = jnp.sum(rows[8:], axis=0, keepdims=True)
-    return jnp.where(lax.axis_index("y") < NY // 2, first, second)
-
-
-def over_tp(rows):
-    return lax.all_to_all(jnp.broadcast_to(rows[None], (NY * NC,) + rows.shape), ("y", "c"), 0, 0)
+def over_half(rows):
+    groups = [list(range(8)), list(range(8, 16))]
+    return lax.all_to_all(jnp.broadcast_to(rows[None], (8,) + rows.shape), ("y", "c"), 0, 0, axis_index_groups=groups)
 
 
 def transposed():
@@ -199,21 +174,21 @@
 
     factor = jnp.repeat(jnp.exp2(scale_exp.astype(F32)), BLOCK, axis=1)
     weight = (weight_codes.astype(F32) * factor).astype(BF16)
-    weights = [weight] + [shifted(weight, k) for k in (1, 2, 3)]
+    weight = jnp.broadcast_to(weight[None], (NX, FEATS, WIDTH))
+    weight = lax.all_to_all(weight, "x", 0, 0).reshape(square)
 
     own = lax.all_gather(cot, "y")
-    own, weights = lax.optimization_barrier((own, weights))
     other = lax.ppermute(own, "c", swap)
 
-    scratch = [pltpu.VMEM((WIDTH, 1024), BF16), pltpu.VMEM(square, BF16), pltpu.VMEM(bricks, BF16), pltpu.SemaphoreType.DMA((21,))]
+    scratch = [pltpu.VMEM((WIDTH, 1024), BF16), pltpu.VMEM(square, BF16), pltpu.VMEM(bricks, BF16), pltpu.SemaphoreType.DMA((17,))]
     (grad,) = kernel(
         input_grad_kernel,
         "input_grad",
         ((bricks, BF16),),
         flops,
-        [ANY] * 6,
-        scratch=[scratch[0], scratch[1], scratch[3]],
-    )(own, other, *weights)
+        [ANY, ANY, VMEM],
+        scratch=[scratch[0], scratch[3]],
+    )(own, other, weight)
     grad = lax.psum_scatter(grad, "z")
 
     keep, send, squares = kernel(
@@ -221,12 +196,11 @@
         "forward",
         ((blocks, BF16), (blocks, BF16), ((NZ, ROWS), F32)),
         flops,
-        [ANY, VMEM, ANY, ANY, ANY, ANY],
-        scratch=[scratch[2], scratch[1], scratch[3]],
-    )(joined_all, gain, *weights)
+        [VMEM] * 3,
+        scratch=[scratch[1]],
+    )(joined_all, gain, weight)
     got = lax.ppermute(send, "c", swap)
-    squares = over_tp(squares)
-    squares = jnp.stack([jnp.sum(squares[:8], axis=0), jnp.sum(squares[8:], axis=0)])
+    squares = jnp.sum(over_half(squares), axis=0)
 
     mine, *others = kernel(
         weight_grad_kernel,
@@ -238,18 +212,16 @@
     )(squares, gain, own, other, joined_all)
     others = [shifted(other, k + 1) for k, other in enumerate(others)]
 
-    both = (keep.astype(F32) + got.astype(F32)).astype(BF16)
-    both, squares = lax.optimization_barrier((both, squares))
+    (both,) = kernel(scale_kernel, "scale", ((blocks, BF16),), 4 * 8 * FEATS * COLS, [VMEM] * 3)(squares, keep, got)
     parts = lax.all_to_all(both, "y", 0, 0)
-    (projected,) = kernel(project_kernel, "project", (((FEATS, COLS), BF16),), 16 * FEATS * COLS, [VMEM] * 2)(squares, parts)
+    projected = jnp.sum(parts.astype(F32), axis=0).astype(BF16)
+    grad, projected = lax.optimization_barrier((grad, projected))
+    (dots,) = kernel(dots_kernel, "dots", (((1, ROWS), F32),), 4 * ROWS * WIDTH, [VMEM] * 4)(squares, grad, joined, gain)
     projected = lax.ppermute(projected, ("x", "y"), transposed()).T
-    weight_grad = mine + others[0].astype(F32) + others[1].astype(F32) + others[2].astype(F32)
-
-    (dots,) = kernel(dots_kernel, "dots", (((1, ROWS), F32),), 4 * ROWS * WIDTH, [VMEM] * 4)(squares, grad, joined, gain)
-    dots = over_tp(dots).reshape(NY * NC, ROWS)
-    (joined_gradient,) = kernel(
-        joined_grad_kernel, "joined_grad", (((ROWS, WIDTH), BF16),), 8 * ROWS * WIDTH, [VMEM] * 5
-    )(squares, dots, grad, joined, gain)
+    dots = jnp.sum(over_half(dots), axis=0)
+    joined_gradient, weight_grad = kernel(
+        last_kernel, "last", (((ROWS, WIDTH), BF16), (block, F32)), 8 * ROWS * WIDTH, [VMEM] * 9
+    )(squares, dots, grad, joined, gain, mine, *others)
     return (projected, joined_gradient, weight_grad)
 
 

time: 147 us -> 137 us (0.932)
  the two profiles are of different devices: /device:TPU:433 before, /device:TPU:1 now
where the time goes in v3:
time: 137 us; the launch traced here: 136 us
  blocking collectives  45.6 us (33%)
  starting transfers between devices  36.6 us (27%)
  Pallas kernels  16.9 us (12%)
  between operations  14.2 us (10%)
  waiting for transfers between devices  11.4 us (8%)
  local copies, waits for them, and re-layouts  7.93 us (6%)
  other arithmetic  3.23 us (2%)
    all_gather x1, blocking collectives, per_device(): own = lax.all_gather(cot, 'y')  24.8 us
    all_to_all x2, blocking collectives, over_half(): lax.all_to_all(jnp.broadcast_to(rows[None], (8,) + rows.shape), ('y', 'c'...  20.9 us
    all_to_all x1, starting transfers between devices, per_device(): weight = lax.all_to_all(weight, 'x', 0, 0).reshape(square)  10.7 us
    ppermute x3, starting transfers between devices, shifted(): return lax.ppermute(value, 'x', [(i, (i + k) % NX) for i in range(NX)])  10.1 us
    all_to_all x1, waiting for transfers between devices, per_device(): parts = lax.all_to_all(both, 'y', 0, 0)  8.56 us
    ppermute x1, starting transfers between devices, per_device(): other = lax.ppermute(own, 'c', swap)  6.88 us
    unnamed x17, local copies, waits for them, and re-layouts  6.19 us
    pallas_call x1, Pallas kernels, per_device(): kernel(forward_kernel, 'forward', ((blocks, BF16), (blocks, BF16), ((NZ,...  5.98 us
  transfers between devices with their start and end apart: 11, of which 2 were waited for; matrix products, arithmetic and copies ran while one was open for 4% of the time, Pallas kernels for 12%

profile of v3, /device:TPU:1, one launch (start us, length us, event | category | flops | bytes accessed | tf_op | source)
XLA Modules:
  0.0 135.8 jit_solution(15106023904832101090)
XLA Ops:
  7.2 0.7 all-gather.4.cloned.1.call-update
  7.9 1.6 %collective-permute-start = (bf16[224,256]{1,0:T(8,128)(2,1)}, bf16[224,256]{1,0:T(8,128)(2,1)S(1)}, u32[]{:S(2)}, u32[]{:S(2)}) collective-permute-start(bf16[224,256]{1,0:T(8,128)(2,1)} %bitcast.28), channel_id=1, source_target_pairs={{0,0},{2,2},{4,128},{6,130},{8,256},{10,258},{12,384},{14,386},{12... | collective-permute-start | bytes 344072 | tf_op jit(solution)/shard_map/ppermute | solution.py:173
  9.5 0.7 multiply_exponential_fusion
  10.3 0.3 broadcast_in_dim.12
  10.6 1.2 fusion
  11.8 1.3 broadcast_in_dim.13
  13.1 10.7 %all-to-all-start = ((bf16[4,224,896]{2,1,0:T(8,128)(2,1)}), bf16[4,224,896]{2,1,0:T(8,128)(2,1)S(1)}, u32[]{:S(2)}, u32[]{:S(2)}) async-start(bf16[4,224,896]{2,1,0:T(8,128)(2,1)} %broadcast_in_dim.13), calls=%async_computation | async-start | bytes 3211264 | tf_op jit(solution)/shard_map/all_to_all | solution.py:178
  23.8 24.8 %all-gather = bf16[1792,256]{1,0:T(8,128)(2,1)S(1)} all-gather(bf16[224,256]{1,0:T(8,128)(2,1)S(1)} %collective-permute-done), channel_id=2, replica_groups=mesh['x'=4,'z'=8,'y'=8,'c'=2] {'y'}, dimensions={0}, use_global_device_ids=true | all-gather | bytes 1032192 | tf_op jit(solution)/shard_map/all_gather | solution.py:180
  48.5 6.9 %collective-permute-start.1 = (bf16[8,224,256]{2,1,0:T(8,128)(2,1)S(1)}, bf16[8,224,256]{2,1,0:T(8,128)(2,1)S(1)}, u32[]{:S(2)}, u32[]{:S(2)}) collective-permute-start(bf16[8,224,256]{2,1,0:T(8,128)(2,1)S(1)} %bitcast.18), channel_id=1, source_target_pairs={{0,1},{1,0},{2,3},{3,2},{4,5},{5,4},{6,7},{7,6},{8,9},{9,8},{10,11... | collective-permute-start | bytes 2752520 | tf_op jit(solution)/shard_map/ppermute | solution.py:181
  55.4 2.1 %collective-permute-done.1.other = bf16[8,224,256]{2,1,0:T(8,128)(2,1)S(1)} collective-permute-done((bf16[8,224,256]{2,1,0:T(8,128)(2,1)S(1)}, bf16[8,224,256]{2,1,0:T(8,128)(2,1)S(1)}, u32[]{:S(2)}, u32[]{:S(2)}) %collective-permute-start.1) | collective-permute-done | bytes 917536 | tf_op jit(solution)/shard_map/ppermute | solution.py:181
  57.5 4.0 %input_grad.1 = bf16[8,128,896]{2,1,0:T(8,128)(2,1)} custom-call(bf16[8,224,256]{2,1,0:T(8,128)(2,1)S(1)} %bitcast.19, bf16[8,224,256]{2,1,0:T(8,128)(2,1)S(1)} %collective-permute-done.1.other, bf16[896,896]{1,0:T(8,128)(2,1)S(1)} %bitcast.14), custom_call_target="tpu_custom_call" | custom-call | flops 1644167168 | bytes 6291456 | tf_op jit(solution)/shard_map/input_grad/pallas_call | solution.py:184
  61.6 0.7 copy-done.7
  62.2 1.5 %copy-done.3 = bf16[1024,896]{1,0:T(8,128)(2,1)S(1)} copy-done((bf16[1024,896]{1,0:T(8,128)(2,1)S(1)}, bf16[1024,896]{1,0:T(8,128)(2,1)}, u32[]{:S(2)}) %copy-start.3) | copy-done | bytes 1835032
  63.7 6.0 %forward.1 = (bf16[8,224,256]{2,1,0:T(8,128)(2,1)S(1)}, bf16[8,224,256]{2,1,0:T(8,128)(2,1)}, f32[8,128]{1,0:T(8,128)S(1)}) custom-call(bf16[8,128,896]{2,1,0:T(8,128)(2,1)S(1)} %bitcast.23, f32[1,896]{1,0:T(1,128)S(1)} %broadcast_in_dim.28.gain, bf16[896,896]{1,0:T(8,128)(2,1)S(1)} %bitcast.15), custom_call_target="tpu_custom_call" | custom-call | flops 1644167168 | bytes 6291456 | tf_op jit(solution)/shard_map/forward/pallas_call | solution.py:194
  69.7 2.3 %collective-permute-start.2 = (bf16[8,224,256]{2,1,0:T(8,128)(2,1)}, bf16[8,224,256]{2,1,0:T(8,128)(2,1)S(1)}, u32[]{:S(2)}, u32[]{:S(2)}) collective-permute-start(bf16[8,224,256]{2,1,0:T(8,128)(2,1)} %get-tuple-element.16), channel_id=1, source_target_pairs={{0,1},{1,0},{2,3},{3,2},{4,5},{5,4},{6,7},{7,6},{8,9},{9,8},{10,11... | collective-permute-start | bytes 2752520 | tf_op jit(solution)/shard_map/ppermute | solution.py:202
  72.0 7.5 %all_to_all.20 = f32[8,8,128]{2,1,0:T(8,128)S(1)} all-to-all(f32[8,8,128]{2,1,0:T(8,128)S(1)} %broadcast_in_dim.29), channel_id=1, replica_groups={{0,1,2,3,4,5,6,7},{8,9,10,11,12,13,14,15},{16,17,18,19,20,21,22,23},{24..., dimensions={0} | all-to-all | bytes 65536 | tf_op jit(solution)/shard_map/all_to_all | solution.py:143
  79.5 1.2 scale.1
  80.7 4.4 %all-to-all-start.2 = ((bf16[8,224,256]{2,1,0:T(8,128)(2,1)}), bf16[8,224,256]{2,1,0:T(8,128)(2,1)}, u32[]{:S(2)}, u32[]{:S(2)}) async-start(bf16[8,224,256]{2,1,0:T(8,128)(2,1)} %scale.1), calls=%async_computation.3 | async-start | bytes 1835008 | tf_op jit(solution)/shard_map/all_to_all | solution.py:216
  85.1 1.5 %copy-done.4 = bf16[1024,896]{1,0:T(8,128)(2,1)S(1)} copy-done((bf16[1024,896]{1,0:T(8,128)(2,1)S(1)}, bf16[1024,896]{1,0:T(8,128)(2,1)}, u32[]{:S(2)}) %copy-start.4) | copy-done | bytes 1835032
  86.6 4.0 %weight_grad.1 = (f32[224,896]{1,0:T(8,128)S(1)}, bf16[224,896]{1,0:T(8,128)(2,1)}, bf16[224,896]{1,0:T(8,128)(2,1)}, bf16[224,896]{1,0:T(8,128)(2,1)}) custom-call(f32[8,128]{1,0:T(8,128)S(1)} %reduce_sum.32.ss, f32[1,896]{1,0:T(1,128)S(1)} %broadcast_in_dim.28.gain, bf16[8,224,256]{2,1,0:T(8,128)(2,1)S(1)} %bitcast.20, bf16[8,224,256]{2,1,0:T(8,128)(2,1)S(1)} %copy-done.6, ...), custom_call_target="tpu_custom_call" | custom-call | flops 1644167168 | bytes 6291456 | tf_op jit(solution)/shard_map/weight_grad/pallas_call | solution.py:205
  90.6 2.7 %collective-permute-start.4 = (bf16[224,896]{1,0:T(8,128)(2,1)}, bf16[224,896]{1,0:T(8,128)(2,1)S(1)}, u32[]{:S(2)}, u32[]{:S(2)}) collective-permute-start(bf16[224,896]{1,0:T(8,128)(2,1)} %get-tuple-element.20), channel_id=1, source_target_pairs={{0,128},{128,256},{256,384},{384,0},{1,129},{129,257},{257,385},{3... | collective-permute-start | bytes 1204232 | tf_op jit(solution)/shard_map/ppermute | solution.py:151
  93.2 4.4 %collective-permute-start.5 = (bf16[224,896]{1,0:T(8,128)(2,1)}, bf16[224,896]{1,0:T(8,128)(2,1)S(1)}, u32[]{:S(2)}, u32[]{:S(2)}) collective-permute-start(bf16[224,896]{1,0:T(8,128)(2,1)} %get-tuple-element.21), channel_id=1, source_target_pairs={{0,256},{128,384},{256,0},{384,128},{1,257},{129,385},{257,1},{385... | collective-permute-start | bytes 1204232 | tf_op jit(solution)/shard_map/ppermute | solution.py:151
  97.6 3.0 %collective-permute-start.6 = (bf16[224,896]{1,0:T(8,128)(2,1)}, bf16[224,896]{1,0:T(8,128)(2,1)S(1)}, u32[]{:S(2)}, u32[]{:S(2)}) collective-permute-start(bf16[224,896]{1,0:T(8,128)(2,1)} %get-tuple-element.22), channel_id=1, source_target_pairs={{0,384},{128,0},{256,128},{384,256},{1,385},{129,1},{257,129},{385... | collective-permute-start | bytes 1204232 | tf_op jit(solution)/shard_map/ppermute | solution.py:151
  100.7 8.6 %all-to-all-done.2 = bf16[8,224,256]{2,1,0:T(8,128)(2,1)} async-done(((bf16[8,224,256]{2,1,0:T(8,128)(2,1)}), bf16[8,224,256]{2,1,0:T(8,128)(2,1)}, u32[]{:S(2)}, u32[]{:S(2)}) %all-to-all-start.2) | async-done | bytes 917536 | tf_op jit(solution)/shard_map/all_to_all | solution.py:216
  109.3 1.3 reduce_sum.33
  110.6 0.7 collective-permute-start.3
  111.3 0.9 copy-done.1
  112.2 0.3 dots.1
  112.5 13.4 %all_to_all.21 = f32[8,1,128]{2,1,0:T(1,128)S(1)} all-to-all(f32[8,1,128]{2,1,0:T(1,128)S(1)} %broadcast_in_dim.31), channel_id=1, replica_groups={{0,1,2,3,4,5,6,7},{8,9,10,11,12,13,14,15},{16,17,18,19,20,21,22,23},{24..., dimensions={0} | all-to-all | bytes 8192 | tf_op jit(solution)/shard_map/all_to_all | solution.py:143
  126.0 0.9 copy-done.2
  126.9 1.4 %last.1 = (bf16[128,896]{1,0:T(8,128)(2,1)}, f32[224,896]{1,0:T(8,128)}) custom-call(f32[8,128]{1,0:T(8,128)S(1)} %reduce_sum.32.ss, f32[1,128]{1,0:T(1,128)S(1)} %bitcast.21, bf16[128,896]{1,0:T(8,128)(2,1)S(1)} %bitcast.17, bf16[128,896]{1,0:T(8,128)(2,1)S(1)} %copy-done, f32[1,896]{1,0:T(1,128)S(1)} %broadcast_in_dim.28.gain, ...), custom_call_target="tpu_custom_call" | custom-call | flops 917504 | bytes 6291456 | tf_op jit(solution)/shard_map/last/pallas_call | solution.py:222
  128.3 0.6 copy.16
  (29 shorter events, 0.3 us)
Async XLA Ops:
  7.2 55.0 %all-gather.4.cloned.1.call-start = ((), (), s32[]{:S(2)}) async-start(), calls=%async_computation.6 | async-start | bytes 2064384 | tf_op jit(solution)/shard_map/all_gather | solution.py:172
  7.9 15.9 %collective-permute-start = (bf16[224,256]{1,0:T(8,128)(2,1)}, bf16[224,256]{1,0:T(8,128)(2,1)S(1)}, u32[]{:S(2)}, u32[]{:S(2)}) collective-permute-start(bf16[224,256]{1,0:T(8,128)(2,1)} %bitcast.28), channel_id=1, source_target_pairs={{0,0},{2,2},{4,128},{6,130},{8,256},{10,258},{12,384},{14,386},{12... | collective-permute-start | bytes 344072 | tf_op jit(solution)/shard_map/ppermute | solution.py:173
  13.1 44.4 %all-to-all-start = ((bf16[4,224,896]{2,1,0:T(8,128)(2,1)}), bf16[4,224,896]{2,1,0:T(8,128)(2,1)S(1)}, u32[]{:S(2)}, u32[]{:S(2)}) async-start(bf16[4,224,896]{2,1,0:T(8,128)(2,1)} %broadcast_in_dim.13), calls=%async_computation | async-start | bytes 3211264 | tf_op jit(solution)/shard_map/all_to_all | solution.py:178
  23.8 86.8 %reduce-scatter.2.cloned.1.call-start = ((), (), s32[]{:S(2)}) async-start(), calls=%async_computation.5 | async-start | bytes 2064384 | tf_op jit(solution)/shard_map/reduce_scatter | solution.py:192
  48.5 9.0 %collective-permute-start.1 = (bf16[8,224,256]{2,1,0:T(8,128)(2,1)S(1)}, bf16[8,224,256]{2,1,0:T(8,128)(2,1)S(1)}, u32[]{:S(2)}, u32[]{:S(2)}) collective-permute-start(bf16[8,224,256]{2,1,0:T(8,128)(2,1)S(1)} %bitcast.18), channel_id=1, source_target_pairs={{0,1},{1,0},{2,3},{3,2},{4,5},{5,4},{6,7},{7,6},{8,9},{9,8},{10,11... | collective-permute-start | bytes 2752520 | tf_op jit(solution)/shard_map/ppermute | solution.py:181
  57.5 4.0 %copy-start.5 = (bf16[8,224,256]{2,1,0:T(8,128)(2,1)}, bf16[8,224,256]{2,1,0:T(8,128)(2,1)S(1)}, u32[]{:S(2)}) copy-start(bf16[8,224,256]{2,1,0:T(8,128)(2,1)S(1)} %collective-permute-done.1.other) | copy-start | bytes 2752516
  61.5 0.7 copy-start.7
  62.2 1.5 %copy-start.3 = (bf16[1024,896]{1,0:T(8,128)(2,1)S(1)}, bf16[1024,896]{1,0:T(8,128)(2,1)}, u32[]{:S(2)}) copy-start(bf16[1024,896]{1,0:T(8,128)(2,1)} %all-gather.4.cloned.1.call-done) | copy-start | bytes 5505028
  69.7 9.8 %collective-permute-start.2 = (bf16[8,224,256]{2,1,0:T(8,128)(2,1)}, bf16[8,224,256]{2,1,0:T(8,128)(2,1)S(1)}, u32[]{:S(2)}, u32[]{:S(2)}) collective-permute-start(bf16[8,224,256]{2,1,0:T(8,128)(2,1)} %get-tuple-element.16), channel_id=1, source_target_pairs={{0,1},{1,0},{2,3},{3,2},{4,5},{5,4},{6,7},{7,6},{8,9},{9,8},{10,11... | collective-permute-start | bytes 2752520 | tf_op jit(solution)/shard_map/ppermute | solution.py:202
  80.7 4.4 %copy-start.6 = (bf16[8,224,256]{2,1,0:T(8,128)(2,1)S(1)}, bf16[8,224,256]{2,1,0:T(8,128)(2,1)}, u32[]{:S(2)}) copy-start(bf16[8,224,256]{2,1,0:T(8,128)(2,1)} %copy-done.5) | copy-start | bytes 2752516
  80.7 28.6 %all-to-all-start.2 = ((bf16[8,224,256]{2,1,0:T(8,128)(2,1)}), bf16[8,224,256]{2,1,0:T(8,128)(2,1)}, u32[]{:S(2)}, u32[]{:S(2)}) async-start(bf16[8,224,256]{2,1,0:T(8,128)(2,1)} %scale.1), calls=%async_computation.3 | async-start | bytes 1835008 | tf_op jit(solution)/shard_map/all_to_all | solution.py:216
  85.1 1.5 %copy-start.4 = (bf16[1024,896]{1,0:T(8,128)(2,1)S(1)}, bf16[1024,896]{1,0:T(8,128)(2,1)}, u32[]{:S(2)}) copy-start(bf16[1024,896]{1,0:T(8,128)(2,1)} %all-gather.4.cloned.1.call-done) | copy-start | bytes 5505028
  86.6 24.7 %copy-start = (bf16[128,896]{1,0:T(8,128)(2,1)S(1)}, bf16[128,896]{1,0:T(8,128)(2,1)}, u32[]{:S(2)}) copy-start(bf16[128,896]{1,0:T(8,128)(2,1)} %joined.3) | copy-start | bytes 688132
  90.6 35.4 %collective-permute-start.4 = (bf16[224,896]{1,0:T(8,128)(2,1)}, bf16[224,896]{1,0:T(8,128)(2,1)S(1)}, u32[]{:S(2)}, u32[]{:S(2)}) collective-permute-start(bf16[224,896]{1,0:T(8,128)(2,1)} %get-tuple-element.20), channel_id=1, source_target_pairs={{0,128},{128,256},{256,384},{384,0},{1,129},{129,257},{257,385},{3... | collective-permute-start | bytes 1204232 | tf_op jit(solution)/shard_map/ppermute | solution.py:151
  93.2 32.7 %collective-permute-start.5 = (bf16[224,896]{1,0:T(8,128)(2,1)}, bf16[224,896]{1,0:T(8,128)(2,1)S(1)}, u32[]{:S(2)}, u32[]{:S(2)}) collective-permute-start(bf16[224,896]{1,0:T(8,128)(2,1)} %get-tuple-element.21), channel_id=1, source_target_pairs={{0,256},{128,384},{256,0},{384,128},{1,257},{129,385},{257,1},{385... | collective-permute-start | bytes 1204232 | tf_op jit(solution)/shard_map/ppermute | solution.py:151
  97.6 28.3 %collective-permute-start.6 = (bf16[224,896]{1,0:T(8,128)(2,1)}, bf16[224,896]{1,0:T(8,128)(2,1)S(1)}, u32[]{:S(2)}, u32[]{:S(2)}) collective-permute-start(bf16[224,896]{1,0:T(8,128)(2,1)} %get-tuple-element.22), channel_id=1, source_target_pairs={{0,384},{128,0},{256,128},{384,256},{1,385},{129,1},{257,129},{385... | collective-permute-start | bytes 1204232 | tf_op jit(solution)/shard_map/ppermute | solution.py:151
  110.6 17.7 %collective-permute-start.3 = (bf16[224,256]{1,0:T(8,128)(2,1)S(1)}, bf16[224,256]{1,0:T(8,128)(2,1)S(1)}, u32[]{:S(2)}, u32[]{:S(2)}) collective-permute-start(bf16[224,256]{1,0:T(8,128)(2,1)S(1)} %reduce_sum.33), channel_id=1, source_target_pairs={{0,0},{2,2},{4,128},{6,130},{8,256},{10,258},{12,384},{14,386},{12... | collective-permute-start | bytes 344072 | tf_op jit(solution)/shard_map/ppermute | solution.py:220
  111.3 0.9 copy-start.1
  126.0 0.9 copy-start.2
Sparse Core Ops, SparseCore 0:
  10.1 45.6 all-gather.3
  61.7 40.8 reduce-scatter.1

commit v4 on v3

--- a/solution.py
+++ b/solution.py
@@ -54,21 +54,20 @@
 def forward_kernel(joined, gain, weight_in, keep, send, squares, weight):
     core = lax.axis_index("c")
     weight[...] = (weight_in[...].astype(F32) * gain[...]).astype(BF16)
+    rows = joined[...].reshape(NZ * ROWS, WIDTH)
+    part = lax.dot_general(weight[...], rows, (((1,), (1,)), ((), ())), preferred_element_type=F32).astype(BF16)
     for j in range(4):
-        rows = joined[2 * j : 2 * j + 2].reshape(COLS, WIDTH)
-        part = lax.dot_general(
-            weight[...], rows, (((1,), (1,)), ((), ())), preferred_element_type=F32
-        ).astype(BF16)
+        columns = part[:, COLS * j : COLS * (j + 1)]
 
         @pl.when(core == j % 2)
         def _():
             for i in range(4):
-                keep[2 * i + j // 2] = part[FEATS * i : FEATS * (i + 1)]
+                keep[2 * i + j // 2] = columns[FEATS * i : FEATS * (i + 1)]
 
         @pl.when(core != j % 2)
         def _():
             for i in range(4):
-                send[2 * i + j // 2] = part[FEATS * i : FEATS * (i + 1)]
+                send[2 * i + j // 2] = columns[FEATS * i : FEATS * (i + 1)]
 
     lane = lax.broadcasted_iota(jnp.int32, (ROWS, ROWS), 1)
     sums = jnp.zeros((ROWS, ROWS), F32)
@@ -122,7 +121,8 @@
     return column(jnp.sum(jnp.where(mine, scales, 0.0), axis=0, keepdims=True))
 
 
-def dots_kernel(ss, grad, joined, gain, out):
+def dots_kernel(ss, grad, joined, gain, out, grad_out):
+    grad_out[...] = grad[...]
     u = grad[...].astype(F32) * gain[...]
     xhat = joined[...].astype(F32) * own_scale(ss)
     dots = jnp.sum(u * xhat, axis=1, keepdims=True)
@@ -216,7 +216,9 @@
     parts = lax.all_to_all(both, "y", 0, 0)
     projected = jnp.sum(parts.astype(F32), axis=0).astype(BF16)
     grad, projected = lax.optimization_barrier((grad, projected))
-    (dots,) = kernel(dots_kernel, "dots", (((1, ROWS), F32),), 4 * ROWS * WIDTH, [VMEM] * 4)(squares, grad, joined, gain)
+    dots, grad = kernel(
+        dots_kernel, "dots", (((1, ROWS), F32), ((ROWS, WIDTH), BF16)), 4 * ROWS * WIDTH, [VMEM] * 4
+    )(squares, grad, joined, gain)
     projected = lax.ppermute(projected, ("x", "y"), transposed()).T
     dots = jnp.sum(over_half(dots), axis=0)
     joined_gradient, weight_grad = kernel(

time: 137 us -> 133 us (0.971)
  Pallas kernels: 16.9 us -> 14.5 us
    pallas_call x1, Pallas kernels: 5.98 us -> 3.62 us  [per_device(): kernel(forward_kernel, 'forward', ((blocks, BF16), (blocks, BF16), ((NZ,...]
    unnamed x17 -> x15, local copies, waits for them, and re-layouts: 6.19 us -> 5.26 us
  transfers between devices with their start and end apart: 11 -> 11, of which waited for: 2 -> 2; matrix products, arithmetic and copies ran while one was open for 4% -> 4% of each run, Pallas kernels for 12% -> 11%
where the time goes in v4:
time: 133 us
  blocking collectives  45.6 us (34%)
  starting transfers between devices  36.6 us (28%)
  Pallas kernels  14.5 us (11%)
  between operations  14.2 us (11%)
  waiting for transfers between devices  11.4 us (9%)
  local copies, waits for them, and re-layouts  7 us (5%)
  other arithmetic  3.23 us (2%)
    all_gather x1, blocking collectives, per_device(): own = lax.all_gather(cot, 'y')  24.8 us
    all_to_all x2, blocking collectives, over_half(): lax.all_to_all(jnp.broadcast_to(rows[None], (8,) + rows.shape), ('y', 'c'...  20.9 us
    all_to_all x1, starting transfers between devices, per_device(): weight = lax.all_to_all(weight, 'x', 0, 0).reshape(square)  10.7 us
    ppermute x3, starting transfers between devices, shifted(): return lax.ppermute(value, 'x', [(i, (i + k) % NX) for i in range(NX)])  10.1 us
    all_to_all x1, waiting for transfers between devices, per_device(): parts = lax.all_to_all(both, 'y', 0, 0)  8.56 us
    ppermute x1, starting transfers between devices, per_device(): other = lax.ppermute(own, 'c', swap)  6.88 us
    unnamed x15, local copies, waits for them, and re-layouts  5.26 us
    all_to_all x1, starting transfers between devices, per_device(): parts = lax.all_to_all(both, 'y', 0, 0)  4.36 us
  transfers between devices with their start and end apart: 11, of which 2 were waited for; matrix products, arithmetic and copies ran while one was open for 4% of the time, Pallas kernels for 11%

profile of v4, /device:TPU:1, one launch (start us, length us, event | category | flops | bytes accessed | tf_op | source)
XLA Modules:
  0.0 132.5 jit_solution(15748715983878886585)
XLA Ops:
  7.2 0.7 all-gather.4.cloned.1.call-update
  7.9 1.6 %collective-permute-start = (bf16[224,256]{1,0:T(8,128)(2,1)}, bf16[224,256]{1,0:T(8,128)(2,1)S(1)}, u32[]{:S(2)}, u32[]{:S(2)}) collective-permute-start(bf16[224,256]{1,0:T(8,128)(2,1)} %bitcast.27), channel_id=1, source_target_pairs={{0,0},{2,2},{4,128},{6,130},{8,256},{10,258},{12,384},{14,386},{12... | collective-permute-start | bytes 344072 | tf_op jit(solution)/shard_map/ppermute | solution.py:173
  9.5 0.7 multiply_exponential_fusion
  10.2 0.1 copy.11
  10.3 0.3 broadcast_in_dim.12
  10.6 1.2 fusion
  11.8 1.3 broadcast_in_dim.13
  13.1 10.7 %all-to-all-start = ((bf16[4,224,896]{2,1,0:T(8,128)(2,1)}), bf16[4,224,896]{2,1,0:T(8,128)(2,1)S(1)}, u32[]{:S(2)}, u32[]{:S(2)}) async-start(bf16[4,224,896]{2,1,0:T(8,128)(2,1)} %broadcast_in_dim.13), calls=%async_computation | async-start | bytes 3211264 | tf_op jit(solution)/shard_map/all_to_all | solution.py:178
  23.8 24.8 %all-gather = bf16[1792,256]{1,0:T(8,128)(2,1)S(1)} all-gather(bf16[224,256]{1,0:T(8,128)(2,1)S(1)} %collective-permute-done), channel_id=2, replica_groups=mesh['x'=4,'z'=8,'y'=8,'c'=2] {'y'}, dimensions={0}, use_global_device_ids=true | all-gather | bytes 1032192 | tf_op jit(solution)/shard_map/all_gather | solution.py:180
  48.5 6.9 %collective-permute-start.1 = (bf16[8,224,256]{2,1,0:T(8,128)(2,1)S(1)}, bf16[8,224,256]{2,1,0:T(8,128)(2,1)S(1)}, u32[]{:S(2)}, u32[]{:S(2)}) collective-permute-start(bf16[8,224,256]{2,1,0:T(8,128)(2,1)S(1)} %bitcast.16), channel_id=1, source_target_pairs={{0,1},{1,0},{2,3},{3,2},{4,5},{5,4},{6,7},{7,6},{8,9},{9,8},{10,11... | collective-permute-start | bytes 2752520 | tf_op jit(solution)/shard_map/ppermute | solution.py:181
  55.4 2.1 %collective-permute-done.1.other = bf16[8,224,256]{2,1,0:T(8,128)(2,1)S(1)} collective-permute-done((bf16[8,224,256]{2,1,0:T(8,128)(2,1)S(1)}, bf16[8,224,256]{2,1,0:T(8,128)(2,1)S(1)}, u32[]{:S(2)}, u32[]{:S(2)}) %collective-permute-start.1) | collective-permute-done | bytes 917536 | tf_op jit(solution)/shard_map/ppermute | solution.py:181
  57.5 4.0 %input_grad.1 = bf16[8,128,896]{2,1,0:T(8,128)(2,1)} custom-call(bf16[8,224,256]{2,1,0:T(8,128)(2,1)S(1)} %bitcast.17, bf16[8,224,256]{2,1,0:T(8,128)(2,1)S(1)} %collective-permute-done.1.other, bf16[896,896]{1,0:T(8,128)(2,1)S(1)} %bitcast.14), custom_call_target="tpu_custom_call" | custom-call | flops 1644167168 | bytes 6291456 | tf_op jit(solution)/shard_map/input_grad/pallas_call | solution.py:184
  61.6 0.7 copy-done.6
  62.2 1.5 %copy-done.2 = bf16[1024,896]{1,0:T(8,128)(2,1)S(1)} copy-done((bf16[1024,896]{1,0:T(8,128)(2,1)S(1)}, bf16[1024,896]{1,0:T(8,128)(2,1)}, u32[]{:S(2)}) %copy-start.2) | copy-done | bytes 1835032
  63.7 3.6 %forward.1 = (bf16[8,224,256]{2,1,0:T(8,128)(2,1)S(1)}, bf16[8,224,256]{2,1,0:T(8,128)(2,1)}, f32[8,128]{1,0:T(8,128)S(1)}) custom-call(bf16[8,128,896]{2,1,0:T(8,128)(2,1)S(1)} %bitcast.22, f32[1,896]{1,0:T(1,128)S(1)} %broadcast_in_dim.28.gain, bf16[896,896]{1,0:T(8,128)(2,1)S(1)} %bitcast.15), custom_call_target="tpu_custom_call" | custom-call | flops 1644167168 | bytes 6291456 | tf_op jit(solution)/shard_map/forward/pallas_call | solution.py:194
  67.3 2.3 %collective-permute-start.2 = (bf16[8,224,256]{2,1,0:T(8,128)(2,1)}, bf16[8,224,256]{2,1,0:T(8,128)(2,1)S(1)}, u32[]{:S(2)}, u32[]{:S(2)}) collective-permute-start(bf16[8,224,256]{2,1,0:T(8,128)(2,1)} %get-tuple-element.18), channel_id=1, source_target_pairs={{0,1},{1,0},{2,3},{3,2},{4,5},{5,4},{6,7},{7,6},{8,9},{9,8},{10,11... | collective-permute-start | bytes 2752520 | tf_op jit(solution)/shard_map/ppermute | solution.py:202
  69.6 7.5 %all_to_all.20 = f32[8,8,128]{2,1,0:T(8,128)S(1)} all-to-all(f32[8,8,128]{2,1,0:T(8,128)S(1)} %broadcast_in_dim.29), channel_id=1, replica_groups={{0,1,2,3,4,5,6,7},{8,9,10,11,12,13,14,15},{16,17,18,19,20,21,22,23},{24..., dimensions={0} | all-to-all | bytes 65536 | tf_op jit(solution)/shard_map/all_to_all | solution.py:143
  77.1 1.2 scale.1
  78.3 4.4 %all-to-all-start.2 = ((bf16[8,224,256]{2,1,0:T(8,128)(2,1)}), bf16[8,224,256]{2,1,0:T(8,128)(2,1)}, u32[]{:S(2)}, u32[]{:S(2)}) async-start(bf16[8,224,256]{2,1,0:T(8,128)(2,1)} %scale.1), calls=%async_computation.3 | async-start | bytes 1835008 | tf_op jit(solution)/shard_map/all_to_all | solution.py:216
  82.7 1.5 %copy-done.3 = bf16[1024,896]{1,0:T(8,128)(2,1)S(1)} copy-done((bf16[1024,896]{1,0:T(8,128)(2,1)S(1)}, bf16[1024,896]{1,0:T(8,128)(2,1)}, u32[]{:S(2)}) %copy-start.3) | copy-done | bytes 1835032
  84.2 4.0 %weight_grad.1 = (f32[224,896]{1,0:T(8,128)S(1)}, bf16[224,896]{1,0:T(8,128)(2,1)}, bf16[224,896]{1,0:T(8,128)(2,1)}, bf16[224,896]{1,0:T(8,128)(2,1)}) custom-call(f32[8,128]{1,0:T(8,128)S(1)} %reduce_sum.32.ss, f32[1,896]{1,0:T(1,128)S(1)} %broadcast_in_dim.28.gain, bf16[8,224,256]{2,1,0:T(8,128)(2,1)S(1)} %bitcast.18, bf16[8,224,256]{2,1,0:T(8,128)(2,1)S(1)} %copy-done.5, ...), custom_call_target="tpu_custom_call" | custom-call | flops 1644167168 | bytes 6291456 | tf_op jit(solution)/shard_map/weight_grad/pallas_call | solution.py:205
  88.2 2.7 %collective-permute-start.4 = (bf16[224,896]{1,0:T(8,128)(2,1)}, bf16[224,896]{1,0:T(8,128)(2,1)S(1)}, u32[]{:S(2)}, u32[]{:S(2)}) collective-permute-start(bf16[224,896]{1,0:T(8,128)(2,1)} %get-tuple-element.24), channel_id=1, source_target_pairs={{0,128},{128,256},{256,384},{384,0},{1,129},{129,257},{257,385},{3... | collective-permute-start | bytes 1204232 | tf_op jit(solution)/shard_map/ppermute | solution.py:151
  90.9 4.4 %collective-permute-start.5 = (bf16[224,896]{1,0:T(8,128)(2,1)}, bf16[224,896]{1,0:T(8,128)(2,1)S(1)}, u32[]{:S(2)}, u32[]{:S(2)}) collective-permute-start(bf16[224,896]{1,0:T(8,128)(2,1)} %get-tuple-element.25), channel_id=1, source_target_pairs={{0,256},{128,384},{256,0},{384,128},{1,257},{129,385},{257,1},{385... | collective-permute-start | bytes 1204232 | tf_op jit(solution)/shard_map/ppermute | solution.py:151
  95.3 3.0 %collective-permute-start.6 = (bf16[224,896]{1,0:T(8,128)(2,1)}, bf16[224,896]{1,0:T(8,128)(2,1)S(1)}, u32[]{:S(2)}, u32[]{:S(2)}) collective-permute-start(bf16[224,896]{1,0:T(8,128)(2,1)} %get-tuple-element.26), channel_id=1, source_target_pairs={{0,384},{128,0},{256,128},{384,256},{1,385},{129,1},{257,129},{385... | collective-permute-start | bytes 1204232 | tf_op jit(solution)/shard_map/ppermute | solution.py:151
  98.3 8.6 %all-to-all-done.2 = bf16[8,224,256]{2,1,0:T(8,128)(2,1)} async-done(((bf16[8,224,256]{2,1,0:T(8,128)(2,1)}), bf16[8,224,256]{2,1,0:T(8,128)(2,1)}, u32[]{:S(2)}, u32[]{:S(2)}) %all-to-all-start.2) | async-done | bytes 917536 | tf_op jit(solution)/shard_map/all_to_all | solution.py:216
  106.9 1.3 reduce_sum.33
  108.2 0.7 collective-permute-start.3
  108.9 0.9 copy-done.1
  109.8 0.3 dots.1
  110.2 13.4 %all_to_all.21 = f32[8,1,128]{2,1,0:T(1,128)S(1)} all-to-all(f32[8,1,128]{2,1,0:T(1,128)S(1)} %broadcast_in_dim.31), channel_id=1, replica_groups={{0,1,2,3,4,5,6,7},{8,9,10,11,12,13,14,15},{16,17,18,19,20,21,22,23},{24..., dimensions={0} | all-to-all | bytes 8192 | tf_op jit(solution)/shard_map/all_to_all | solution.py:143
  123.6 1.4 %last.1 = (bf16[128,896]{1,0:T(8,128)(2,1)}, f32[224,896]{1,0:T(8,128)}) custom-call(f32[8,128]{1,0:T(8,128)S(1)} %reduce_sum.32.ss, f32[1,128]{1,0:T(1,128)S(1)} %bitcast.20, bf16[128,896]{1,0:T(8,128)(2,1)S(1)} %get-tuple-element.22.grad, bf16[128,896]{1,0:T(8,128)(2,1)S(1)} %copy-done, f32[1,896]{1,0:T(1,128)S(1)} %broadcast_in_dim.28.gain, ...), custom_call_target="tpu_custom_call" | custom-call | flops 917504 | bytes 6291456 | tf_op jit(solution)/shard_map/last/pallas_call | solution.py:224
  125.0 0.6 copy.16
  (27 shorter events, 0.2 us)
Async XLA Ops:
  7.2 55.0 %all-gather.4.cloned.1.call-start = ((), (), s32[]{:S(2)}) async-start(), calls=%async_computation.6 | async-start | bytes 2064384 | tf_op jit(solution)/shard_map/all_gather | solution.py:172
  7.9 15.9 %collective-permute-start = (bf16[224,256]{1,0:T(8,128)(2,1)}, bf16[224,256]{1,0:T(8,128)(2,1)S(1)}, u32[]{:S(2)}, u32[]{:S(2)}) collective-permute-start(bf16[224,256]{1,0:T(8,128)(2,1)} %bitcast.27), channel_id=1, source_target_pairs={{0,0},{2,2},{4,128},{6,130},{8,256},{10,258},{12,384},{14,386},{12... | collective-permute-start | bytes 344072 | tf_op jit(solution)/shard_map/ppermute | solution.py:173
  13.1 44.4 %all-to-all-start = ((bf16[4,224,896]{2,1,0:T(8,128)(2,1)}), bf16[4,224,896]{2,1,0:T(8,128)(2,1)S(1)}, u32[]{:S(2)}, u32[]{:S(2)}) async-start(bf16[4,224,896]{2,1,0:T(8,128)(2,1)} %broadcast_in_dim.13), calls=%async_computation | async-start | bytes 3211264 | tf_op jit(solution)/shard_map/all_to_all | solution.py:178
  23.8 84.4 %reduce-scatter.2.cloned.1.call-start = ((), (), s32[]{:S(2)}) async-start(), calls=%async_computation.5 | async-start | bytes 2064384 | tf_op jit(solution)/shard_map/reduce_scatter | solution.py:192
  48.5 9.0 %collective-permute-start.1 = (bf16[8,224,256]{2,1,0:T(8,128)(2,1)S(1)}, bf16[8,224,256]{2,1,0:T(8,128)(2,1)S(1)}, u32[]{:S(2)}, u32[]{:S(2)}) collective-permute-start(bf16[8,224,256]{2,1,0:T(8,128)(2,1)S(1)} %bitcast.16), channel_id=1, source_target_pairs={{0,1},{1,0},{2,3},{3,2},{4,5},{5,4},{6,7},{7,6},{8,9},{9,8},{10,11... | collective-permute-start | bytes 2752520 | tf_op jit(solution)/shard_map/ppermute | solution.py:181
  57.5 4.0 %copy-start.4 = (bf16[8,224,256]{2,1,0:T(8,128)(2,1)}, bf16[8,224,256]{2,1,0:T(8,128)(2,1)S(1)}, u32[]{:S(2)}) copy-start(bf16[8,224,256]{2,1,0:T(8,128)(2,1)S(1)} %collective-permute-done.1.other) | copy-start | bytes 2752516
  61.5 0.7 copy-start.6
  62.2 1.5 %copy-start.2 = (bf16[1024,896]{1,0:T(8,128)(2,1)S(1)}, bf16[1024,896]{1,0:T(8,128)(2,1)}, u32[]{:S(2)}) copy-start(bf16[1024,896]{1,0:T(8,128)(2,1)} %all-gather.4.cloned.1.call-done) | copy-start | bytes 5505028
  67.3 9.8 %collective-permute-start.2 = (bf16[8,224,256]{2,1,0:T(8,128)(2,1)}, bf16[8,224,256]{2,1,0:T(8,128)(2,1)S(1)}, u32[]{:S(2)}, u32[]{:S(2)}) collective-permute-start(bf16[8,224,256]{2,1,0:T(8,128)(2,1)} %get-tuple-element.18), channel_id=1, source_target_pairs={{0,1},{1,0},{2,3},{3,2},{4,5},{5,4},{6,7},{7,6},{8,9},{9,8},{10,11... | collective-permute-start | bytes 2752520 | tf_op jit(solution)/shard_map/ppermute | solution.py:202
  78.3 4.4 %copy-start.5 = (bf16[8,224,256]{2,1,0:T(8,128)(2,1)S(1)}, bf16[8,224,256]{2,1,0:T(8,128)(2,1)}, u32[]{:S(2)}) copy-start(bf16[8,224,256]{2,1,0:T(8,128)(2,1)} %copy-done.4) | copy-start | bytes 2752516
  78.3 28.6 %all-to-all-start.2 = ((bf16[8,224,256]{2,1,0:T(8,128)(2,1)}), bf16[8,224,256]{2,1,0:T(8,128)(2,1)}, u32[]{:S(2)}, u32[]{:S(2)}) async-start(bf16[8,224,256]{2,1,0:T(8,128)(2,1)} %scale.1), calls=%async_computation.3 | async-start | bytes 1835008 | tf_op jit(solution)/shard_map/all_to_all | solution.py:216
  82.7 1.5 %copy-start.3 = (bf16[1024,896]{1,0:T(8,128)(2,1)S(1)}, bf16[1024,896]{1,0:T(8,128)(2,1)}, u32[]{:S(2)}) copy-start(bf16[1024,896]{1,0:T(8,128)(2,1)} %all-gather.4.cloned.1.call-done) | copy-start | bytes 5505028
  84.2 24.7 %copy-start = (bf16[128,896]{1,0:T(8,128)(2,1)S(1)}, bf16[128,896]{1,0:T(8,128)(2,1)}, u32[]{:S(2)}) copy-start(bf16[128,896]{1,0:T(8,128)(2,1)} %joined.3) | copy-start | bytes 688132
  88.2 35.4 %collective-permute-start.4 = (bf16[224,896]{1,0:T(8,128)(2,1)}, bf16[224,896]{1,0:T(8,128)(2,1)S(1)}, u32[]{:S(2)}, u32[]{:S(2)}) collective-permute-start(bf16[224,896]{1,0:T(8,128)(2,1)} %get-tuple-element.24), channel_id=1, source_target_pairs={{0,128},{128,256},{256,384},{384,0},{1,129},{129,257},{257,385},{3... | collective-permute-start | bytes 1204232 | tf_op jit(solution)/shard_map/ppermute | solution.py:151
  90.9 32.7 %collective-permute-start.5 = (bf16[224,896]{1,0:T(8,128)(2,1)}, bf16[224,896]{1,0:T(8,128)(2,1)S(1)}, u32[]{:S(2)}, u32[]{:S(2)}) collective-permute-start(bf16[224,896]{1,0:T(8,128)(2,1)} %get-tuple-element.25), channel_id=1, source_target_pairs={{0,256},{128,384},{256,0},{384,128},{1,257},{129,385},{257,1},{385... | collective-permute-start | bytes 1204232 | tf_op jit(solution)/shard_map/ppermute | solution.py:151
  95.3 28.3 %collective-permute-start.6 = (bf16[224,896]{1,0:T(8,128)(2,1)}, bf16[224,896]{1,0:T(8,128)(2,1)S(1)}, u32[]{:S(2)}, u32[]{:S(2)}) collective-permute-start(bf16[224,896]{1,0:T(8,128)(2,1)} %get-tuple-element.26), channel_id=1, source_target_pairs={{0,384},{128,0},{256,128},{384,256},{1,385},{129,1},{257,129},{385... | collective-permute-start | bytes 1204232 | tf_op jit(solution)/shard_map/ppermute | solution.py:151
  108.2 16.8 %collective-permute-start.3 = (bf16[224,256]{1,0:T(8,128)(2,1)S(1)}, bf16[224,256]{1,0:T(8,128)(2,1)S(1)}, u32[]{:S(2)}, u32[]{:S(2)}) collective-permute-start(bf16[224,256]{1,0:T(8,128)(2,1)S(1)} %reduce_sum.33), channel_id=1, source_target_pairs={{0,0},{2,2},{4,128},{6,130},{8,256},{10,258},{12,384},{14,386},{12... | collective-permute-start | bytes 344072 | tf_op jit(solution)/shard_map/ppermute | solution.py:222
  108.9 0.9 copy-start.1
Sparse Core Ops, SparseCore 0:
  10.1 45.6 all-gather.3
  61.7 40.8 reduce-scatter.1

commit v5 on v4

--- a/solution.py
+++ b/solution.py
@@ -20,6 +20,15 @@
 MIB = 1024 * 1024
 
 
+def scaled_weight_kernel(codes, exponents, out):
+    factors = jnp.exp2(exponents[...].astype(F32))
+    for b in range(WIDTH // BLOCK):
+        columns = slice(BLOCK * b, BLOCK * (b + 1))
+        part = (codes[:, columns].astype(F32) * factors[:, b : b + 1]).astype(BF16)
+        for k in range(NX):
+            out[k, :, columns] = part
+
+
 def start_all(copies):
     for copy in copies:
         copy.start()
@@ -34,11 +43,13 @@
 def cot_copies(own, other, cot, sems):
     core = lax.axis_index("c")
     copies = []
-    for m in range(8):
-        for which, (block, parity) in enumerate(((own, core), (other, 1 - core))):
-            start = pl.multiple_of(512 * (m % 2) + COLS * parity, COLS)
-            place = cot.at[pl.ds(FEATS * (m // 2), FEATS), pl.ds(start, COLS)]
-            copies.append(pltpu.make_async_copy(block.at[m], place, sems.at[2 * m + which]))
+    for i in range(NX):
+        for half in range(2):
+            slot = traced_place(i, half)
+            for which, (block, parity) in enumerate(((own, core), (other, 1 - core))):
+                start = pl.multiple_of(512 * half + COLS * parity, COLS)
+                place = cot.at[pl.ds(FEATS * i, FEATS), pl.ds(start, COLS)]
+                copies.append(pltpu.make_async_copy(block.at[slot], place, sems.at[4 * i + 2 * half + which]))
     return copies
 
 
@@ -62,19 +73,19 @@
         @pl.when(core == j % 2)
         def _():
             for i in range(4):
-                keep[2 * i + j // 2] = columns[FEATS * i : FEATS * (i + 1)]
+                keep[traced_place(i, j // 2)] = columns[FEATS * i : FEATS * (i + 1)]
 
         @pl.when(core != j % 2)
         def _():
             for i in range(4):
-                send[2 * i + j // 2] = columns[FEATS * i : FEATS * (i + 1)]
+                send[traced_place(i, j // 2)] = columns[FEATS * i : FEATS * (i + 1)]
 
     lane = lax.broadcasted_iota(jnp.int32, (ROWS, ROWS), 1)
     sums = jnp.zeros((ROWS, ROWS), F32)
     for z in range(NZ):
         value = joined[z].astype(F32)
         sums = jnp.where(lane == z, jnp.sum(value * value, axis=1, keepdims=True), sums)
-    squares[...] = sums.T[:NZ]
+    squares[...] = jnp.broadcast_to(sums.T[None, :NZ], (8, NZ, ROWS))
 
 
 def scale_kernel(ss, keep, got, out):
@@ -84,7 +95,8 @@
         j = 2 * parity + lax.axis_index("c")
         pair = [jnp.sum(jnp.where(row == 2 * j + i, scales, 0.0), axis=0, keepdims=True) for i in range(2)]
         scale = jnp.concatenate(pair, axis=1)
-        for m in range(parity, 8, 2):
+        for i in range(NX):
+            m = traced_place(i, parity)
             out[m] = ((keep[m].astype(F32) + got[m].astype(F32)) * scale).astype(BF16)
 
 
@@ -108,7 +120,7 @@
 
 
 def row_scales(ss):
-    return lax.rsqrt(ss[...] / MODEL_WIDTH + eps)
+    return lax.rsqrt(jnp.sum(ss[...], axis=0) / MODEL_WIDTH + eps)
 
 
 def column(row):
@@ -126,25 +138,41 @@
     u = grad[...].astype(F32) * gain[...]
     xhat = joined[...].astype(F32) * own_scale(ss)
     dots = jnp.sum(u * xhat, axis=1, keepdims=True)
-    out[...] = jnp.broadcast_to(dots, (ROWS, ROWS)).T[:1]
-
-
-def last_kernel(ss, dots, grad, joined, gain, mine, o1, o2, o3, out, weight_grad):
+    out[...] = jnp.broadcast_to(jnp.broadcast_to(dots, (ROWS, ROWS)).T[None, :1], (8, 1, ROWS))
+
+
+def last_kernel(ss, dots, grad, joined, gain, mine, o1, o2, o3, projected_in, out, weight_grad, projected):
+    projected[...] = projected_in[...]
     weight_grad[...] = mine[...] + o1[...].astype(F32) + o2[...].astype(F32) + o3[...].astype(F32)
-    c = column(dots[...] / MODEL_WIDTH)
+    c = column(jnp.sum(dots[...], axis=0) / MODEL_WIDTH)
     scale = own_scale(ss)
     u = grad[...].astype(F32) * gain[...]
     xhat = joined[...].astype(F32) * scale
     out[...] = (scale * (u - xhat * c)).astype(BF16)
 
 
-def over_half(rows):
+def over_half(copies):
     groups = [list(range(8)), list(range(8, 16))]
-    return lax.all_to_all(jnp.broadcast_to(rows[None], (8,) + rows.shape), ("y", "c"), 0, 0, axis_index_groups=groups)
-
-
-def transposed():
-    return [(x * NY + y, (y // 2) * NY + 2 * x + y % 2) for x in range(NX) for y in range(NY)]
+    return lax.all_to_all(copies, ("y", "c"), 0, 0, axis_index_groups=groups)
+
+
+def meeting_place(x, source, parity):
+    away = (source + NX - x) % NX
+    along = (3, 2, 0, 1)[away]
+    return (2 * x + 1 + along) % NY if parity else (2 * x + NY - along) % NY
+
+
+def to_meeting_place():
+    return [
+        (source * NY + y, (y // 2) * NY + meeting_place(y // 2, source, y % 2)) for source in range(NX) for y in range(NY)
+    ]
+
+
+def traced_place(source, parity):
+    x = lax.axis_index("x")
+    away = lax.rem(source + NX - x, NX)
+    along = jnp.where(away == 0, 3, jnp.where(away == 1, 2, jnp.where(away == 2, 0, 1)))
+    return lax.rem(2 * x + 1 + along, NY) if parity else lax.rem(2 * x + NY - along, NY)
 
 
 def shifted(value, k):
@@ -170,11 +198,11 @@
     bricks, square, blocks, block = (NZ, ROWS, WIDTH), (WIDTH, WIDTH), (8, FEATS, COLS), (FEATS, WIDTH)
     gain = gain[None, :]
     joined_all = lax.all_gather(joined, "z")
-    cot = lax.ppermute(cotangent.T, ("x", "y"), transposed())
-
-    factor = jnp.repeat(jnp.exp2(scale_exp.astype(F32)), BLOCK, axis=1)
-    weight = (weight_codes.astype(F32) * factor).astype(BF16)
-    weight = jnp.broadcast_to(weight[None], (NX, FEATS, WIDTH))
+    cot = lax.ppermute(cotangent.T, ("x", "y"), to_meeting_place())
+
+    (weight,) = kernel(
+        scaled_weight_kernel, "scaled_weight", (((NX,) + block, BF16),), 4 * FEATS * WIDTH, [VMEM] * 2
+    )(weight_codes, scale_exp)
     weight = lax.all_to_all(weight, "x", 0, 0).reshape(square)
 
     own = lax.all_gather(cot, "y")
@@ -194,13 +222,13 @@
     keep, send, squares = kernel(
         forward_kernel,
         "forward",
-        ((blocks, BF16), (blocks, BF16), ((NZ, ROWS), F32)),
+        ((blocks, BF16), (blocks, BF16), ((8, NZ, ROWS), F32)),
         flops,
         [VMEM] * 3,
         scratch=[scratch[1]],
     )(joined_all, gain, weight)
     got = lax.ppermute(send, "c", swap)
-    squares = jnp.sum(over_half(squares), axis=0)
+    squares = over_half(squares)
 
     mine, *others = kernel(
         weight_grad_kernel,
@@ -217,14 +245,18 @@
     projected = jnp.sum(parts.astype(F32), axis=0).astype(BF16)
     grad, projected = lax.optimization_barrier((grad, projected))
     dots, grad = kernel(
-        dots_kernel, "dots", (((1, ROWS), F32), ((ROWS, WIDTH), BF16)), 4 * ROWS * WIDTH, [VMEM] * 4
+        dots_kernel, "dots", (((8, 1, ROWS), F32), ((ROWS, WIDTH), BF16)), 4 * ROWS * WIDTH, [VMEM] * 4
     )(squares, grad, joined, gain)
-    projected = lax.ppermute(projected, ("x", "y"), transposed()).T
-    dots = jnp.sum(over_half(dots), axis=0)
-    joined_gradient, weight_grad = kernel(
-        last_kernel, "last", (((ROWS, WIDTH), BF16), (block, F32)), 8 * ROWS * WIDTH, [VMEM] * 9
-    )(squares, dots, grad, joined, gain, mine, *others)
-    return (projected, joined_gradient, weight_grad)
+    projected = lax.ppermute(projected, ("x", "y"), [(b, a) for a, b in to_meeting_place()])
+    dots = over_half(dots)
+    joined_gradient, weight_grad, projected = kernel(
+        last_kernel,
+        "last",
+        (((ROWS, WIDTH), BF16), (block, F32), ((FEATS, COLS), BF16)),
+        8 * ROWS * WIDTH,
+        [VMEM] * 10,
+    )(squares, dots, grad, joined, gain, mine, *others, projected)
+    return (projected.T, joined_gradient, weight_grad)
 
 
 def solution(mesh):

time: 133 us -> 134 us (level)
  blocking collectives: 45.6 us -> 32.6 us
  starting transfers between devices: 36.6 us -> 44.3 us
  waiting for transfers between devices: 11.4 us -> 18 us
  other arithmetic: 3.23 us -> 1.31 us
  Pallas kernels: 14.5 us -> 16 us
    all_to_all x2 -> x1, blocking collectives: 20.9 us -> 9.48 us  [over_half(): return lax.all_to_all(copies, ('y', 'c'), 0, 0, axis_index_groups=groups)]
    ppermute x2, starting transfers between devices: 2.22 us -> 12.1 us  [the longest x1 7.5 us: per_device(): cot = lax.ppermute(cotangent.T, ('x', 'y'), to_meeting_place())]
    all_to_all x1, starting transfers between devices: 10.7 us -> 3.56 us  [per_device(): weight = lax.all_to_all(weight, 'x', 0, 0).reshape(square)]
    all_to_all x0 -> x1, waiting for transfers between devices: none -> 4.8 us  [over_half(): return lax.all_to_all(copies, ('y', 'c'), 0, 0, axis_index_groups=groups)]
    all_to_all x0 -> x1, starting transfers between devices: none -> 3.98 us  [over_half(): return lax.all_to_all(copies, ('y', 'c'), 0, 0, axis_index_groups=groups)]
    all_to_all x1, waiting for transfers between devices: 8.56 us -> 10.4 us  [per_device(): parts = lax.all_to_all(both, 'y', 0, 0)]
    broadcast_in_dim x4 -> x0, local copies, waits for them, and re-layouts: 1.61 us -> none  [the longest x1 1.3 us: per_device(): weight = jnp.broadcast_to(weight[None], (NX, FEATS, WIDTH))]
    all_gather x1, blocking collectives: 24.8 us -> 23.1 us  [per_device(): own = lax.all_gather(cot, 'y')]
  transfers between devices with their start and end apart: 11 -> 12, of which waited for: 2 -> 3; matrix products, arithmetic and copies ran while one was open for 4% -> 2% of each run, Pallas kernels for 11% -> 11%
where the time goes in v5:
time: 134 us; the launch traced here: 133 us
  starting transfers between devices  44.3 us (33%)
  blocking collectives  32.6 us (24%)
  waiting for transfers between devices  18 us (13%)
  Pallas kernels  16 us (12%)
  between operations  14.2 us (11%)
  local copies, waits for them, and re-layouts  6.43 us (5%)
    all_gather x1, blocking collectives, per_device(): own = lax.all_gather(cot, 'y')  23.1 us
    ppermute x3, starting transfers between devices, shifted(): return lax.ppermute(value, 'x', [(i, (i + k) % NX) for i in range(NX)])  10.5 us
    all_to_all x1, waiting for transfers between devices, per_device(): parts = lax.all_to_all(both, 'y', 0, 0)  10.4 us
    all_to_all x1, blocking collectives, over_half(): return lax.all_to_all(copies, ('y', 'c'), 0, 0, axis_index_groups=groups)  9.48 us
    ppermute x1, starting transfers between devices, per_device(): cot = lax.ppermute(cotangent.T, ('x', 'y'), to_meeting_place())  7.5 us
    ppermute x1, starting transfers between devices, per_device(): other = lax.ppermute(own, 'c', swap)  7.11 us
    unnamed x13, local copies, waits for them, and re-layouts  6.42 us
    all_to_all x1, waiting for transfers between devices, over_half(): return lax.all_to_all(copies, ('y', 'c'), 0, 0, axis_index_groups=groups)  4.8 us
  transfers between devices with their start and end apart: 12, of which 3 were waited for; matrix products, arithmetic and copies ran while one was open for 2% of the time, Pallas kernels for 11%

profile of v5, /device:TPU:1, one launch (start us, length us, event | category | flops | bytes accessed | tf_op | source)
XLA Modules:
  0.0 132.9 jit_solution(7350674303427693934)
XLA Ops:
  7.2 0.0 all-gather.4.cloned.1.call-start
  7.2 0.7 all-gather.4.cloned.1.call-update
  7.9 7.5 %collective-permute-start = (bf16[224,256]{1,0:T(8,128)(2,1)}, bf16[224,256]{1,0:T(8,128)(2,1)S(1)}, u32[]{:S(2)}, u32[]{:S(2)}) collective-permute-start(bf16[224,256]{1,0:T(8,128)(2,1)} %bitcast.14), channel_id=1, source_target_pairs={{0,10},{2,8},{4,130},{6,136},{8,264},{10,266},{12,392},{14,386},{1... | collective-permute-start | bytes 344072 | tf_op jit(solution)/shard_map/ppermute | solution.py:201
  15.4 0.8 copy.8.exponents
  16.2 1.0 copy-done.1
  17.2 1.5 %scaled_weight.1 = bf16[4,224,896]{2,1,0:T(8,128)(2,1)} custom-call(bf16[224,896]{1,0:T(8,128)(2,1)S(1)} %copy-done.1, s32[224,7]{1,0:T(8,128)S(1)} %copy.8.exponents), custom_call_target="tpu_custom_call" | custom-call | flops 802816 | bytes 6291456 | tf_op jit(solution)/shard_map/scaled_weight/pallas_call | solution.py:203
  18.7 3.6 %all-to-all-start = ((bf16[4,224,896]{2,1,0:T(8,128)(2,1)}), bf16[4,224,896]{2,1,0:T(8,128)(2,1)S(1)}, u32[]{:S(2)}, u32[]{:S(2)}) async-start(bf16[4,224,896]{2,1,0:T(8,128)(2,1)} %scaled_weight.1), calls=%async_computation | async-start | bytes 3211264 | tf_op jit(solution)/shard_map/all_to_all | solution.py:206
  22.3 0.0 reduce-scatter.2.cloned.1.call-start
  22.3 23.1 %all-gather.1 = bf16[1792,256]{1,0:T(8,128)(2,1)S(1)} all-gather(bf16[224,256]{1,0:T(8,128)(2,1)S(1)} %collective-permute-done), channel_id=3, replica_groups=mesh['x'=4,'z'=8,'y'=8,'c'=2] {'y'}, dimensions={0}, use_global_device_ids=true | all-gather | bytes 1032192 | tf_op jit(solution)/shard_map/all_gather | solution.py:208
  45.5 7.1 %collective-permute-start.1 = (bf16[8,224,256]{2,1,0:T(8,128)(2,1)S(1)}, bf16[8,224,256]{2,1,0:T(8,128)(2,1)S(1)}, u32[]{:S(2)}, u32[]{:S(2)}) collective-permute-start(bf16[8,224,256]{2,1,0:T(8,128)(2,1)S(1)} %bitcast.8), channel_id=1, source_target_pairs={{0,1},{1,0},{2,3},{3,2},{4,5},{5,4},{6,7},{7,6},{8,9},{9,8},{10,11... | collective-permute-start | bytes 2752520 | tf_op jit(solution)/shard_map/ppermute | solution.py:209
  52.6 2.1 %collective-permute-done.1.other = bf16[8,224,256]{2,1,0:T(8,128)(2,1)S(1)} collective-permute-done((bf16[8,224,256]{2,1,0:T(8,128)(2,1)S(1)}, bf16[8,224,256]{2,1,0:T(8,128)(2,1)S(1)}, u32[]{:S(2)}, u32[]{:S(2)}) %collective-permute-start.1) | collective-permute-done | bytes 917536 | tf_op jit(solution)/shard_map/ppermute | solution.py:209
  54.7 4.0 %input_grad.1 = bf16[8,128,896]{2,1,0:T(8,128)(2,1)} custom-call(bf16[8,224,256]{2,1,0:T(8,128)(2,1)S(1)} %bitcast.9, bf16[8,224,256]{2,1,0:T(8,128)(2,1)S(1)} %collective-permute-done.1.other, bf16[896,896]{1,0:T(8,128)(2,1)S(1)} %bitcast.6), custom_call_target="tpu_custom_call" | custom-call | flops 1644167168 | bytes 6291456 | tf_op jit(solution)/shard_map/input_grad/pallas_call | solution.py:212
  58.7 0.7 copy-done.5
  59.4 1.5 %copy-done.3 = bf16[1024,896]{1,0:T(8,128)(2,1)S(1)} copy-done((bf16[1024,896]{1,0:T(8,128)(2,1)S(1)}, bf16[1024,896]{1,0:T(8,128)(2,1)}, u32[]{:S(2)}) %copy-start.3) | copy-done | bytes 1835032
  60.9 2.8 %forward.1 = (bf16[8,224,256]{2,1,0:T(8,128)(2,1)S(1)}, bf16[8,224,256]{2,1,0:T(8,128)(2,1)S(1)}, f32[8,8,128]{2,1,0:T(8,128)S(1)}) custom-call(bf16[8,128,896]{2,1,0:T(8,128)(2,1)S(1)} %bitcast.12, f32[1,896]{1,0:T(1,128)S(1)} %broadcast_in_dim.3.gain, bf16[896,896]{1,0:T(8,128)(2,1)S(1)} %bitcast.7), custom_call_target="tpu_custom_call" | custom-call | flops 1644167168 | bytes 6291456 | tf_op jit(solution)/shard_map/forward/pallas_call | solution.py:222
  63.7 2.6 %collective-permute-start.2 = (bf16[8,224,256]{2,1,0:T(8,128)(2,1)S(1)}, bf16[8,224,256]{2,1,0:T(8,128)(2,1)S(1)}, u32[]{:S(2)}, u32[]{:S(2)}) collective-permute-start(bf16[8,224,256]{2,1,0:T(8,128)(2,1)S(1)} %get-tuple-element.19), channel_id=1, source_target_pairs={{0,1},{1,0},{2,3},{3,2},{4,5},{5,4},{6,7},{7,6},{8,9},{9,8},{10,11... | collective-permute-start | bytes 2752520 | tf_op jit(solution)/shard_map/ppermute | solution.py:230
  66.3 9.5 %all_to_all.20.ss = f32[8,8,128]{2,1,0:T(8,128)S(1)} all-to-all(f32[8,8,128]{2,1,0:T(8,128)S(1)} %get-tuple-element.17), channel_id=1, replica_groups={{0,1,2,3,4,5,6,7},{8,9,10,11,12,13,14,15},{16,17,18,19,20,21,22,23},{24..., dimensions={0} | all-to-all | bytes 65536 | tf_op jit(solution)/shard_map/all_to_all | solution.py:156
  75.8 1.4 %scale.1 = bf16[8,224,256]{2,1,0:T(8,128)(2,1)} custom-call(f32[8,8,128]{2,1,0:T(8,128)S(1)} %all_to_all.20.ss, bf16[8,224,256]{2,1,0:T(8,128)(2,1)S(1)} %get-tuple-element.18.keep, bf16[8,224,256]{2,1,0:T(8,128)(2,1)S(1)} %collective-permute-done.2.got), custom_call_target="tpu_custom_call" | custom-call | flops 1835008 | bytes 6291456 | tf_op jit(solution)/shard_map/scale/pallas_call | solution.py:243
  77.1 4.3 %all-to-all-start.2 = ((bf16[8,224,256]{2,1,0:T(8,128)(2,1)}), bf16[8,224,256]{2,1,0:T(8,128)(2,1)}, u32[]{:S(2)}, u32[]{:S(2)}) async-start(bf16[8,224,256]{2,1,0:T(8,128)(2,1)} %scale.1), calls=%async_computation.3 | async-start | bytes 1835008 | tf_op jit(solution)/shard_map/all_to_all | solution.py:244
  81.5 1.5 %copy-done.4 = bf16[1024,896]{1,0:T(8,128)(2,1)S(1)} copy-done((bf16[1024,896]{1,0:T(8,128)(2,1)S(1)}, bf16[1024,896]{1,0:T(8,128)(2,1)}, u32[]{:S(2)}) %copy-start.4) | copy-done | bytes 1835032
  83.0 4.0 %weight_grad.1 = (f32[224,896]{1,0:T(8,128)S(1)}, bf16[224,896]{1,0:T(8,128)(2,1)}, bf16[224,896]{1,0:T(8,128)(2,1)}, bf16[224,896]{1,0:T(8,128)(2,1)}) custom-call(f32[8,8,128]{2,1,0:T(8,128)S(1)} %all_to_all.20.ss, f32[1,896]{1,0:T(1,128)S(1)} %broadcast_in_dim.3.gain, bf16[8,224,256]{2,1,0:T(8,128)(2,1)S(1)} %bitcast.10, ...), custom_call_target="tpu_custom_call" | custom-call | flops 1644167168 | bytes 6291456 | tf_op jit(solution)/shard_map/weight_grad/pallas_call | solution.py:233
  87.0 3.1 %collective-permute-start.3 = (bf16[224,896]{1,0:T(8,128)(2,1)}, bf16[224,896]{1,0:T(8,128)(2,1)S(1)}, u32[]{:S(2)}, u32[]{:S(2)}) collective-permute-start(bf16[224,896]{1,0:T(8,128)(2,1)} %get-tuple-element.24), channel_id=1, source_target_pairs={{0,128},{128,256},{256,384},{384,0},{1,129},{129,257},{257,385},{3... | collective-permute-start | bytes 1204232 | tf_op jit(solution)/shard_map/ppermute | solution.py:179
  90.1 4.3 %collective-permute-start.4 = (bf16[224,896]{1,0:T(8,128)(2,1)}, bf16[224,896]{1,0:T(8,128)(2,1)S(1)}, u32[]{:S(2)}, u32[]{:S(2)}) collective-permute-start(bf16[224,896]{1,0:T(8,128)(2,1)} %get-tuple-element.25), channel_id=1, source_target_pairs={{0,256},{128,384},{256,0},{384,128},{1,257},{129,385},{257,1},{385... | collective-permute-start | bytes 1204232 | tf_op jit(solution)/shard_map/ppermute | solution.py:179
  94.4 3.1 %collective-permute-start.5 = (bf16[224,896]{1,0:T(8,128)(2,1)}, bf16[224,896]{1,0:T(8,128)(2,1)S(1)}, u32[]{:S(2)}, u32[]{:S(2)}) collective-permute-start(bf16[224,896]{1,0:T(8,128)(2,1)} %get-tuple-element.26), channel_id=1, source_target_pairs={{0,384},{128,0},{256,128},{384,256},{1,385},{129,1},{257,129},{385... | collective-permute-start | bytes 1204232 | tf_op jit(solution)/shard_map/ppermute | solution.py:179
  97.5 10.4 %all-to-all-done.2 = bf16[8,224,256]{2,1,0:T(8,128)(2,1)} async-done(((bf16[8,224,256]{2,1,0:T(8,128)(2,1)}), bf16[8,224,256]{2,1,0:T(8,128)(2,1)}, u32[]{:S(2)}, u32[]{:S(2)}) %all-to-all-start.2) | async-done | bytes 917536 | tf_op jit(solution)/shard_map/all_to_all | solution.py:244
  107.9 1.3 reduce_sum.12
  109.3 4.6 %collective-permute-start.6 = (bf16[224,256]{1,0:T(8,128)(2,1)S(1)}, bf16[224,256]{1,0:T(8,128)(2,1)S(1)}, u32[]{:S(2)}, u32[]{:S(2)}) collective-permute-start(bf16[224,256]{1,0:T(8,128)(2,1)S(1)} %reduce_sum.12), channel_id=1, source_target_pairs={{10,0},{8,2},{130,4},{136,6},{264,8},{266,10},{392,12},{386,14},{1... | collective-permute-start | bytes 344072 | tf_op jit(solution)/shard_map/ppermute | solution.py:250
  113.9 0.9 copy-done.2
  114.8 0.9 dots.1
  115.8 4.0 %all-to-all-start.3 = ((f32[8,1,128]{2,1,0:T(1,128)}), f32[8,1,128]{2,1,0:T(1,128)S(1)}, u32[]{:S(2)}, u32[]{:S(2)}) async-start(f32[8,1,128]{2,1,0:T(1,128)} %get-tuple-element.21), calls=%async_computation.4 | async-start | bytes 8192 | tf_op jit(solution)/shard_map/all_to_all | solution.py:156
  119.8 4.8 %all-to-all-done.3.dots = f32[8,1,128]{2,1,0:T(1,128)S(1)} async-done(((f32[8,1,128]{2,1,0:T(1,128)}), f32[8,1,128]{2,1,0:T(1,128)S(1)}, u32[]{:S(2)}, u32[]{:S(2)}) %all-to-all-start.3) | async-done | bytes 4128 | tf_op jit(solution)/shard_map/all_to_all | solution.py:156
  124.6 1.5 %last.1 = (bf16[128,896]{1,0:T(8,128)(2,1)}, f32[224,896]{1,0:T(8,128)}, bf16[224,256]{1,0:T(8,128)(2,1)}) custom-call(f32[8,8,128]{2,1,0:T(8,128)S(1)} %all_to_all.20.ss, f32[8,1,128]{2,1,0:T(1,128)S(1)} %all-to-all-done.3.dots, bf16[128,896]{1,0:T(8,128)(2,1)S(1)} %get-tuple-element.22.grad, bf16[128,896]{1,0:T(8,128)(2,1)S(1)} %copy-done, ...), custom_call_target="tpu_custom_call" | custom-call | flops 917504 | bytes 6291456 | tf_op jit(solution)/shard_map/last/pallas_call | solution.py:252
  (18 shorter events, 0.1 us)
Async XLA Ops:
  7.2 52.2 %all-gather.4.cloned.1.call-start = ((), (), s32[]{:S(2)}) async-start(), calls=%async_computation.6 | async-start | bytes 2064384 | tf_op jit(solution)/shard_map/all_gather | solution.py:200
  7.9 14.4 %collective-permute-start = (bf16[224,256]{1,0:T(8,128)(2,1)}, bf16[224,256]{1,0:T(8,128)(2,1)S(1)}, u32[]{:S(2)}, u32[]{:S(2)}) collective-permute-start(bf16[224,256]{1,0:T(8,128)(2,1)} %bitcast.14), channel_id=1, source_target_pairs={{0,10},{2,8},{4,130},{6,136},{8,264},{10,266},{12,392},{14,386},{1... | collective-permute-start | bytes 344072 | tf_op jit(solution)/shard_map/ppermute | solution.py:201
  16.2 1.0 copy-start.1
  18.7 36.0 %all-to-all-start = ((bf16[4,224,896]{2,1,0:T(8,128)(2,1)}), bf16[4,224,896]{2,1,0:T(8,128)(2,1)S(1)}, u32[]{:S(2)}, u32[]{:S(2)}) async-start(bf16[4,224,896]{2,1,0:T(8,128)(2,1)} %scaled_weight.1), calls=%async_computation | async-start | bytes 3211264 | tf_op jit(solution)/shard_map/all_to_all | solution.py:206
  22.3 87.0 %reduce-scatter.2.cloned.1.call-start = ((), (), s32[]{:S(2)}) async-start(), calls=%async_computation.5 | async-start | bytes 2064384 | tf_op jit(solution)/shard_map/reduce_scatter | solution.py:220
  45.5 9.2 %collective-permute-start.1 = (bf16[8,224,256]{2,1,0:T(8,128)(2,1)S(1)}, bf16[8,224,256]{2,1,0:T(8,128)(2,1)S(1)}, u32[]{:S(2)}, u32[]{:S(2)}) collective-permute-start(bf16[8,224,256]{2,1,0:T(8,128)(2,1)S(1)} %bitcast.8), channel_id=1, source_target_pairs={{0,1},{1,0},{2,3},{3,2},{4,5},{5,4},{6,7},{7,6},{8,9},{9,8},{10,11... | collective-permute-start | bytes 2752520 | tf_op jit(solution)/shard_map/ppermute | solution.py:209
  58.7 0.7 copy-start.5
  59.4 1.5 %copy-start.3 = (bf16[1024,896]{1,0:T(8,128)(2,1)S(1)}, bf16[1024,896]{1,0:T(8,128)(2,1)}, u32[]{:S(2)}) copy-start(bf16[1024,896]{1,0:T(8,128)(2,1)} %all-gather.4.cloned.1.call-done) | copy-start | bytes 5505028
  63.7 12.1 %collective-permute-start.2 = (bf16[8,224,256]{2,1,0:T(8,128)(2,1)S(1)}, bf16[8,224,256]{2,1,0:T(8,128)(2,1)S(1)}, u32[]{:S(2)}, u32[]{:S(2)}) collective-permute-start(bf16[8,224,256]{2,1,0:T(8,128)(2,1)S(1)} %get-tuple-element.19), channel_id=1, source_target_pairs={{0,1},{1,0},{2,3},{3,2},{4,5},{5,4},{6,7},{7,6},{8,9},{9,8},{10,11... | collective-permute-start | bytes 2752520 | tf_op jit(solution)/shard_map/ppermute | solution.py:230
  77.1 30.8 %all-to-all-start.2 = ((bf16[8,224,256]{2,1,0:T(8,128)(2,1)}), bf16[8,224,256]{2,1,0:T(8,128)(2,1)}, u32[]{:S(2)}, u32[]{:S(2)}) async-start(bf16[8,224,256]{2,1,0:T(8,128)(2,1)} %scale.1), calls=%async_computation.3 | async-start | bytes 1835008 | tf_op jit(solution)/shard_map/all_to_all | solution.py:244
  81.4 1.5 %copy-start.4 = (bf16[1024,896]{1,0:T(8,128)(2,1)S(1)}, bf16[1024,896]{1,0:T(8,128)(2,1)}, u32[]{:S(2)}) copy-start(bf16[1024,896]{1,0:T(8,128)(2,1)} %all-gather.4.cloned.1.call-done) | copy-start | bytes 5505028
  83.0 30.9 %copy-start = (bf16[128,896]{1,0:T(8,128)(2,1)S(1)}, bf16[128,896]{1,0:T(8,128)(2,1)}, u32[]{:S(2)}) copy-start(bf16[128,896]{1,0:T(8,128)(2,1)} %joined.3) | copy-start | bytes 688132
  87.0 32.8 %collective-permute-start.3 = (bf16[224,896]{1,0:T(8,128)(2,1)}, bf16[224,896]{1,0:T(8,128)(2,1)S(1)}, u32[]{:S(2)}, u32[]{:S(2)}) collective-permute-start(bf16[224,896]{1,0:T(8,128)(2,1)} %get-tuple-element.24), channel_id=1, source_target_pairs={{0,128},{128,256},{256,384},{384,0},{1,129},{129,257},{257,385},{3... | collective-permute-start | bytes 1204232 | tf_op jit(solution)/shard_map/ppermute | solution.py:179
  90.1 29.7 %collective-permute-start.4 = (bf16[224,896]{1,0:T(8,128)(2,1)}, bf16[224,896]{1,0:T(8,128)(2,1)S(1)}, u32[]{:S(2)}, u32[]{:S(2)}) collective-permute-start(bf16[224,896]{1,0:T(8,128)(2,1)} %get-tuple-element.25), channel_id=1, source_target_pairs={{0,256},{128,384},{256,0},{384,128},{1,257},{129,385},{257,1},{385... | collective-permute-start | bytes 1204232 | tf_op jit(solution)/shard_map/ppermute | solution.py:179
  94.4 25.4 %collective-permute-start.5 = (bf16[224,896]{1,0:T(8,128)(2,1)}, bf16[224,896]{1,0:T(8,128)(2,1)S(1)}, u32[]{:S(2)}, u32[]{:S(2)}) collective-permute-start(bf16[224,896]{1,0:T(8,128)(2,1)} %get-tuple-element.26), channel_id=1, source_target_pairs={{0,384},{128,0},{256,128},{384,256},{1,385},{129,1},{257,129},{385... | collective-permute-start | bytes 1204232 | tf_op jit(solution)/shard_map/ppermute | solution.py:179
  109.3 15.3 %collective-permute-start.6 = (bf16[224,256]{1,0:T(8,128)(2,1)S(1)}, bf16[224,256]{1,0:T(8,128)(2,1)S(1)}, u32[]{:S(2)}, u32[]{:S(2)}) collective-permute-start(bf16[224,256]{1,0:T(8,128)(2,1)S(1)} %reduce_sum.12), channel_id=1, source_target_pairs={{10,0},{8,2},{130,4},{136,6},{264,8},{266,10},{392,12},{386,14},{1... | collective-permute-start | bytes 344072 | tf_op jit(solution)/shard_map/ppermute | solution.py:250
  113.9 0.9 copy-start.2
  115.8 8.8 %all-to-all-start.3 = ((f32[8,1,128]{2,1,0:T(1,128)}), f32[8,1,128]{2,1,0:T(1,128)S(1)}, u32[]{:S(2)}, u32[]{:S(2)}) async-start(f32[8,1,128]{2,1,0:T(1,128)} %get-tuple-element.21), calls=%async_computation.4 | async-start | bytes 8192 | tf_op jit(solution)/shard_map/all_to_all | solution.py:156
Sparse Core Ops, SparseCore 0:
  10.1 45.6 all-gather.3
  58.8 42.4 reduce-scatter.1

commit v6 on v5

--- a/solution.py
+++ b/solution.py
@@ -43,13 +43,11 @@
 def cot_copies(own, other, cot, sems):
     core = lax.axis_index("c")
     copies = []
-    for i in range(NX):
-        for half in range(2):
-            slot = traced_place(i, half)
-            for which, (block, parity) in enumerate(((own, core), (other, 1 - core))):
-                start = pl.multiple_of(512 * half + COLS * parity, COLS)
-                place = cot.at[pl.ds(FEATS * i, FEATS), pl.ds(start, COLS)]
-                copies.append(pltpu.make_async_copy(block.at[slot], place, sems.at[4 * i + 2 * half + which]))
+    for m in range(8):
+        for which, (block, parity) in enumerate(((own, core), (other, 1 - core))):
+            start = pl.multiple_of(512 * (m % 2) + COLS * parity, COLS)
+            place = cot.at[pl.ds(FEATS * (m // 2), FEATS), pl.ds(start, COLS)]
+            copies.append(pltpu.make_async_copy(block.at[m], place, sems.at[2 * m + which]))
     return copies
 
 
@@ -73,12 +71,12 @@
         @pl.when(core == j % 2)
         def _():
             for i in range(4):
-                keep[traced_place(i, j // 2)] = columns[FEATS * i : FEATS * (i + 1)]
+                keep[2 * i + j // 2] = columns[FEATS * i : FEATS * (i + 1)]
 
         @pl.when(core != j % 2)
         def _():
             for i in range(4):
-                send[traced_place(i, j // 2)] = columns[FEATS * i : FEATS * (i + 1)]
+                send[2 * i + j // 2] = columns[FEATS * i : FEATS * (i + 1)]
 
     lane = lax.broadcasted_iota(jnp.int32, (ROWS, ROWS), 1)
     sums = jnp.zeros((ROWS, ROWS), F32)
@@ -95,8 +93,7 @@
         j = 2 * parity + lax.axis_index("c")
         pair = [jnp.sum(jnp.where(row == 2 * j + i, scales, 0.0), axis=0, keepdims=True) for i in range(2)]
         scale = jnp.concatenate(pair, axis=1)
-        for i in range(NX):
-            m = traced_place(i, parity)
+        for m in range(parity, 8, 2):
             out[m] = ((keep[m].astype(F32) + got[m].astype(F32)) * scale).astype(BF16)
 
 
@@ -156,23 +153,8 @@
     return lax.all_to_all(copies, ("y", "c"), 0, 0, axis_index_groups=groups)
 
 
-def meeting_place(x, source, parity):
-    away = (source + NX - x) % NX
-    along = (3, 2, 0, 1)[away]
-    return (2 * x + 1 + along) % NY if parity else (2 * x + NY - along) % NY
-
-
-def to_meeting_place():
-    return [
-        (source * NY + y, (y // 2) * NY + meeting_place(y // 2, source, y % 2)) for source in range(NX) for y in range(NY)
-    ]
-
-
-def traced_place(source, parity):
-    x = lax.axis_index("x")
-    away = lax.rem(source + NX - x, NX)
-    along = jnp.where(away == 0, 3, jnp.where(away == 1, 2, jnp.where(away == 2, 0, 1)))
-    return lax.rem(2 * x + 1 + along, NY) if parity else lax.rem(2 * x + NY - along, NY)
+def transposed():
+    return [(x * NY + y, (y // 2) * NY + 2 * x + y % 2) for x in range(NX) for y in range(NY)]
 
 
 def shifted(value, k):
@@ -198,7 +180,7 @@
     bricks, square, blocks, block = (NZ, ROWS, WIDTH), (WIDTH, WIDTH), (8, FEATS, COLS), (FEATS, WIDTH)
     gain = gain[None, :]
     joined_all = lax.all_gather(joined, "z")
-    cot = lax.ppermute(cotangent.T, ("x", "y"), to_meeting_place())
+    cot = lax.ppermute(cotangent.T, ("x", "y"), transposed())
 
     (weight,) = kernel(
         scaled_weight_kernel, "scaled_weight", (((NX,) + block, BF16),), 4 * FEATS * WIDTH, [VMEM] * 2
@@ -247,7 +229,7 @@
     dots, grad = kernel(
         dots_kernel, "dots", (((8, 1, ROWS), F32), ((ROWS, WIDTH), BF16)), 4 * ROWS * WIDTH, [VMEM] * 4
     )(squares, grad, joined, gain)
-    projected = lax.ppermute(projected, ("x", "y"), [(b, a) for a, b in to_meeting_place()])
+    projected = lax.ppermute(projected, ("x", "y"), transposed())
     dots = over_half(dots)
     joined_gradient, weight_grad, projected = kernel(
         last_kernel,

time: 134 us -> 133 us (level)
  waiting for transfers between devices: 18 us -> 16.1 us
    ppermute x2, starting transfers between devices: 12.1 us -> 2.22 us  [the longest x1 1.56 us: per_device(): cot = lax.ppermute(cotangent.T, ('x', 'y'), transposed())]
    all_to_all x1, starting transfers between devices: 3.56 us -> 10.7 us  [per_device(): weight = lax.all_to_all(weight, 'x', 0, 0).reshape(square)]
    all_to_all x1, starting transfers between devices: 3.98 us -> 8.73 us  [over_half(): return lax.all_to_all(copies, ('y', 'c'), 0, 0, axis_index_groups=groups)]
    all_to_all x1, blocking collectives: 9.48 us -> 7.48 us  [over_half(): return lax.all_to_all(copies, ('y', 'c'), 0, 0, axis_index_groups=groups)]
    all_gather x1, blocking collectives: 23.1 us -> 25.1 us  [per_device(): own = lax.all_gather(cot, 'y')]
    all_to_all x1, waiting for transfers between devices: 10.4 us -> 8.56 us  [per_device(): parts = lax.all_to_all(both, 'y', 0, 0)]
where the time goes in v6:
time: 133 us; the launch traced here: 132 us
  starting transfers between devices  45.2 us (34%)
  blocking collectives  32.6 us (25%)
  waiting for transfers between devices  16.1 us (12%)
  Pallas kernels  15.8 us (12%)
  between operations  14.2 us (11%)
  local copies, waits for them, and re-layouts  6.41 us (5%)
    all_gather x1, blocking collectives, per_device(): own = lax.all_gather(cot, 'y')  25.1 us
    all_to_all x1, starting transfers between devices, per_device(): weight = lax.all_to_all(weight, 'x', 0, 0).reshape(square)  10.7 us
    ppermute x3, starting transfers between devices, shifted(): return lax.ppermute(value, 'x', [(i, (i + k) % NX) for i in range(NX)])  10.1 us
    all_to_all x1, starting transfers between devices, over_half(): return lax.all_to_all(copies, ('y', 'c'), 0, 0, axis_index_groups=groups)  8.73 us
    all_to_all x1, waiting for transfers between devices, per_device(): parts = lax.all_to_all(both, 'y', 0, 0)  8.56 us
    all_to_all x1, blocking collectives, over_half(): return lax.all_to_all(copies, ('y', 'c'), 0, 0, axis_index_groups=groups)  7.48 us
    ppermute x1, starting transfers between devices, per_device(): other = lax.ppermute(own, 'c', swap)  6.88 us
    unnamed x13, local copies, waits for them, and re-layouts  6.41 us
  transfers between devices with their start and end apart: 12, of which 3 were waited for; matrix products, arithmetic and copies ran while one was open for 2% of the time, Pallas kernels for 11%

profile of v6, /device:TPU:1, one launch (start us, length us, event | category | flops | bytes accessed | tf_op | source)
XLA Modules:
  0.0 131.6 jit_solution(13511078508125748640)
XLA Ops:
  7.2 0.0 all-gather.4.cloned.1.call-start
  7.2 0.7 all-gather.4.cloned.1.call-update
  7.9 1.6 %collective-permute-start = (bf16[224,256]{1,0:T(8,128)(2,1)}, bf16[224,256]{1,0:T(8,128)(2,1)S(1)}, u32[]{:S(2)}, u32[]{:S(2)}) collective-permute-start(bf16[224,256]{1,0:T(8,128)(2,1)} %bitcast.14), channel_id=1, source_target_pairs={{0,0},{2,2},{4,128},{6,130},{8,256},{10,258},{12,384},{14,386},{12... | collective-permute-start | bytes 344072 | tf_op jit(solution)/shard_map/ppermute | solution.py:183
  9.5 0.8 copy.8.exponents
  10.3 1.0 copy-done.1
  11.3 1.5 %scaled_weight.1 = bf16[4,224,896]{2,1,0:T(8,128)(2,1)} custom-call(bf16[224,896]{1,0:T(8,128)(2,1)S(1)} %copy-done.1, s32[224,7]{1,0:T(8,128)S(1)} %copy.8.exponents), custom_call_target="tpu_custom_call" | custom-call | flops 802816 | bytes 6291456 | tf_op jit(solution)/shard_map/scaled_weight/pallas_call | solution.py:185
  12.8 10.7 %all-to-all-start = ((bf16[4,224,896]{2,1,0:T(8,128)(2,1)}), bf16[4,224,896]{2,1,0:T(8,128)(2,1)S(1)}, u32[]{:S(2)}, u32[]{:S(2)}) async-start(bf16[4,224,896]{2,1,0:T(8,128)(2,1)} %scaled_weight.1), calls=%async_computation | async-start | bytes 3211264 | tf_op jit(solution)/shard_map/all_to_all | solution.py:188
  23.5 25.1 %all-gather.1 = bf16[1792,256]{1,0:T(8,128)(2,1)S(1)} all-gather(bf16[224,256]{1,0:T(8,128)(2,1)S(1)} %collective-permute-done), channel_id=3, replica_groups=mesh['x'=4,'z'=8,'y'=8,'c'=2] {'y'}, dimensions={0}, use_global_device_ids=true | all-gather | bytes 1032192 | tf_op jit(solution)/shard_map/all_gather | solution.py:190
  48.5 6.9 %collective-permute-start.1 = (bf16[8,224,256]{2,1,0:T(8,128)(2,1)S(1)}, bf16[8,224,256]{2,1,0:T(8,128)(2,1)S(1)}, u32[]{:S(2)}, u32[]{:S(2)}) collective-permute-start(bf16[8,224,256]{2,1,0:T(8,128)(2,1)S(1)} %bitcast.8), channel_id=1, source_target_pairs={{0,1},{1,0},{2,3},{3,2},{4,5},{5,4},{6,7},{7,6},{8,9},{9,8},{10,11... | collective-permute-start | bytes 2752520 | tf_op jit(solution)/shard_map/ppermute | solution.py:191
  55.4 2.1 %collective-permute-done.1.other = bf16[8,224,256]{2,1,0:T(8,128)(2,1)S(1)} collective-permute-done((bf16[8,224,256]{2,1,0:T(8,128)(2,1)S(1)}, bf16[8,224,256]{2,1,0:T(8,128)(2,1)S(1)}, u32[]{:S(2)}, u32[]{:S(2)}) %collective-permute-start.1) | collective-permute-done | bytes 917536 | tf_op jit(solution)/shard_map/ppermute | solution.py:191
  57.5 4.0 %input_grad.1 = bf16[8,128,896]{2,1,0:T(8,128)(2,1)} custom-call(bf16[8,224,256]{2,1,0:T(8,128)(2,1)S(1)} %bitcast.9, bf16[8,224,256]{2,1,0:T(8,128)(2,1)S(1)} %collective-permute-done.1.other, bf16[896,896]{1,0:T(8,128)(2,1)S(1)} %bitcast.6), custom_call_target="tpu_custom_call" | custom-call | flops 1644167168 | bytes 6291456 | tf_op jit(solution)/shard_map/input_grad/pallas_call | solution.py:194
  61.5 0.7 copy-done.5
  62.2 1.5 %copy-done.3 = bf16[1024,896]{1,0:T(8,128)(2,1)S(1)} copy-done((bf16[1024,896]{1,0:T(8,128)(2,1)S(1)}, bf16[1024,896]{1,0:T(8,128)(2,1)}, u32[]{:S(2)}) %copy-start.3) | copy-done | bytes 1835032
  63.7 2.8 %forward.1 = (bf16[8,224,256]{2,1,0:T(8,128)(2,1)S(1)}, bf16[8,224,256]{2,1,0:T(8,128)(2,1)S(1)}, f32[8,8,128]{2,1,0:T(8,128)S(1)}) custom-call(bf16[8,128,896]{2,1,0:T(8,128)(2,1)S(1)} %bitcast.12, f32[1,896]{1,0:T(1,128)S(1)} %broadcast_in_dim.3.gain, bf16[896,896]{1,0:T(8,128)(2,1)S(1)} %bitcast.7), custom_call_target="tpu_custom_call" | custom-call | flops 1644167168 | bytes 6291456 | tf_op jit(solution)/shard_map/forward/pallas_call | solution.py:204
  66.5 2.3 %collective-permute-start.2 = (bf16[8,224,256]{2,1,0:T(8,128)(2,1)S(1)}, bf16[8,224,256]{2,1,0:T(8,128)(2,1)S(1)}, u32[]{:S(2)}, u32[]{:S(2)}) collective-permute-start(bf16[8,224,256]{2,1,0:T(8,128)(2,1)S(1)} %get-tuple-element.19), channel_id=1, source_target_pairs={{0,1},{1,0},{2,3},{3,2},{4,5},{5,4},{6,7},{7,6},{8,9},{9,8},{10,11... | collective-permute-start | bytes 2752520 | tf_op jit(solution)/shard_map/ppermute | solution.py:212
  68.7 7.5 %all_to_all.20.ss = f32[8,8,128]{2,1,0:T(8,128)S(1)} all-to-all(f32[8,8,128]{2,1,0:T(8,128)S(1)} %get-tuple-element.17), channel_id=1, replica_groups={{0,1,2,3,4,5,6,7},{8,9,10,11,12,13,14,15},{16,17,18,19,20,21,22,23},{24..., dimensions={0} | all-to-all | bytes 65536 | tf_op jit(solution)/shard_map/all_to_all | solution.py:153
  76.2 1.2 scale.1
  77.4 4.2 %all-to-all-start.2 = ((bf16[8,224,256]{2,1,0:T(8,128)(2,1)}), bf16[8,224,256]{2,1,0:T(8,128)(2,1)}, u32[]{:S(2)}, u32[]{:S(2)}) async-start(bf16[8,224,256]{2,1,0:T(8,128)(2,1)} %scale.1), calls=%async_computation.3 | async-start | bytes 1835008 | tf_op jit(solution)/shard_map/all_to_all | solution.py:226
  81.7 1.5 %copy-done.4 = bf16[1024,896]{1,0:T(8,128)(2,1)S(1)} copy-done((bf16[1024,896]{1,0:T(8,128)(2,1)S(1)}, bf16[1024,896]{1,0:T(8,128)(2,1)}, u32[]{:S(2)}) %copy-start.4) | copy-done | bytes 1835032
  83.2 4.0 %weight_grad.1 = (f32[224,896]{1,0:T(8,128)S(1)}, bf16[224,896]{1,0:T(8,128)(2,1)}, bf16[224,896]{1,0:T(8,128)(2,1)}, bf16[224,896]{1,0:T(8,128)(2,1)}) custom-call(f32[8,8,128]{2,1,0:T(8,128)S(1)} %all_to_all.20.ss, f32[1,896]{1,0:T(1,128)S(1)} %broadcast_in_dim.3.gain, bf16[8,224,256]{2,1,0:T(8,128)(2,1)S(1)} %bitcast.10, ...), custom_call_target="tpu_custom_call" | custom-call | flops 1644167168 | bytes 6291456 | tf_op jit(solution)/shard_map/weight_grad/pallas_call | solution.py:215
  87.2 2.7 %collective-permute-start.3 = (bf16[224,896]{1,0:T(8,128)(2,1)}, bf16[224,896]{1,0:T(8,128)(2,1)S(1)}, u32[]{:S(2)}, u32[]{:S(2)}) collective-permute-start(bf16[224,896]{1,0:T(8,128)(2,1)} %get-tuple-element.24), channel_id=1, source_target_pairs={{0,128},{128,256},{256,384},{384,0},{1,129},{129,257},{257,385},{3... | collective-permute-start | bytes 1204232 | tf_op jit(solution)/shard_map/ppermute | solution.py:161
  89.9 4.3 %collective-permute-start.4 = (bf16[224,896]{1,0:T(8,128)(2,1)}, bf16[224,896]{1,0:T(8,128)(2,1)S(1)}, u32[]{:S(2)}, u32[]{:S(2)}) collective-permute-start(bf16[224,896]{1,0:T(8,128)(2,1)} %get-tuple-element.25), channel_id=1, source_target_pairs={{0,256},{128,384},{256,0},{384,128},{1,257},{129,385},{257,1},{385... | collective-permute-start | bytes 1204232 | tf_op jit(solution)/shard_map/ppermute | solution.py:161
  94.2 3.1 %collective-permute-start.5 = (bf16[224,896]{1,0:T(8,128)(2,1)}, bf16[224,896]{1,0:T(8,128)(2,1)S(1)}, u32[]{:S(2)}, u32[]{:S(2)}) collective-permute-start(bf16[224,896]{1,0:T(8,128)(2,1)} %get-tuple-element.26), channel_id=1, source_target_pairs={{0,384},{128,0},{256,128},{384,256},{1,385},{129,1},{257,129},{385... | collective-permute-start | bytes 1204232 | tf_op jit(solution)/shard_map/ppermute | solution.py:161
  97.3 8.6 %all-to-all-done.2 = bf16[8,224,256]{2,1,0:T(8,128)(2,1)} async-done(((bf16[8,224,256]{2,1,0:T(8,128)(2,1)}), bf16[8,224,256]{2,1,0:T(8,128)(2,1)}, u32[]{:S(2)}, u32[]{:S(2)}) %all-to-all-start.2) | async-done | bytes 917536 | tf_op jit(solution)/shard_map/all_to_all | solution.py:226
  105.9 1.3 reduce_sum.12
  107.2 0.0 reduce-scatter.2.cloned.1.call-done
  107.2 0.7 collective-permute-start.6
  107.9 0.9 copy-done.2
  108.8 0.9 dots.1
  109.8 8.7 %all-to-all-start.3 = ((f32[8,1,128]{2,1,0:T(1,128)}), f32[8,1,128]{2,1,0:T(1,128)S(1)}, u32[]{:S(2)}, u32[]{:S(2)}) async-start(f32[8,1,128]{2,1,0:T(1,128)} %get-tuple-element.21), calls=%async_computation.4 | async-start | bytes 8192 | tf_op jit(solution)/shard_map/all_to_all | solution.py:153
  118.5 4.8 %all-to-all-done.3.dots = f32[8,1,128]{2,1,0:T(1,128)S(1)} async-done(((f32[8,1,128]{2,1,0:T(1,128)}), f32[8,1,128]{2,1,0:T(1,128)S(1)}, u32[]{:S(2)}, u32[]{:S(2)}) %all-to-all-start.3) | async-done | bytes 4128 | tf_op jit(solution)/shard_map/all_to_all | solution.py:153
  123.3 1.5 %last.1 = (bf16[128,896]{1,0:T(8,128)(2,1)}, f32[224,896]{1,0:T(8,128)}, bf16[224,256]{1,0:T(8,128)(2,1)}) custom-call(f32[8,8,128]{2,1,0:T(8,128)S(1)} %all_to_all.20.ss, f32[8,1,128]{2,1,0:T(1,128)S(1)} %all-to-all-done.3.dots, bf16[128,896]{1,0:T(8,128)(2,1)S(1)} %get-tuple-element.22.grad, bf16[128,896]{1,0:T(8,128)(2,1)S(1)} %copy-done, ...), custom_call_target="tpu_custom_call" | custom-call | flops 917504 | bytes 6291456 | tf_op jit(solution)/shard_map/last/pallas_call | solution.py:234
  (18 shorter events, 0.1 us)
Async XLA Ops:
  7.2 55.0 %all-gather.4.cloned.1.call-start = ((), (), s32[]{:S(2)}) async-start(), calls=%async_computation.6 | async-start | bytes 2064384 | tf_op jit(solution)/shard_map/all_gather | solution.py:182
  7.9 15.6 %collective-permute-start = (bf16[224,256]{1,0:T(8,128)(2,1)}, bf16[224,256]{1,0:T(8,128)(2,1)S(1)}, u32[]{:S(2)}, u32[]{:S(2)}) collective-permute-start(bf16[224,256]{1,0:T(8,128)(2,1)} %bitcast.14), channel_id=1, source_target_pairs={{0,0},{2,2},{4,128},{6,130},{8,256},{10,258},{12,384},{14,386},{12... | collective-permute-start | bytes 344072 | tf_op jit(solution)/shard_map/ppermute | solution.py:183
  10.3 1.0 copy-start.1
  12.8 44.8 %all-to-all-start = ((bf16[4,224,896]{2,1,0:T(8,128)(2,1)}), bf16[4,224,896]{2,1,0:T(8,128)(2,1)S(1)}, u32[]{:S(2)}, u32[]{:S(2)}) async-start(bf16[4,224,896]{2,1,0:T(8,128)(2,1)} %scaled_weight.1), calls=%async_computation | async-start | bytes 3211264 | tf_op jit(solution)/shard_map/all_to_all | solution.py:188
  23.4 83.8 %reduce-scatter.2.cloned.1.call-start = ((), (), s32[]{:S(2)}) async-start(), calls=%async_computation.5 | async-start | bytes 2064384 | tf_op jit(solution)/shard_map/reduce_scatter | solution.py:202
  48.5 9.0 %collective-permute-start.1 = (bf16[8,224,256]{2,1,0:T(8,128)(2,1)S(1)}, bf16[8,224,256]{2,1,0:T(8,128)(2,1)S(1)}, u32[]{:S(2)}, u32[]{:S(2)}) collective-permute-start(bf16[8,224,256]{2,1,0:T(8,128)(2,1)S(1)} %bitcast.8), channel_id=1, source_target_pairs={{0,1},{1,0},{2,3},{3,2},{4,5},{5,4},{6,7},{7,6},{8,9},{9,8},{10,11... | collective-permute-start | bytes 2752520 | tf_op jit(solution)/shard_map/ppermute | solution.py:191
  61.5 0.7 copy-start.5
  62.2 1.5 %copy-start.3 = (bf16[1024,896]{1,0:T(8,128)(2,1)S(1)}, bf16[1024,896]{1,0:T(8,128)(2,1)}, u32[]{:S(2)}) copy-start(bf16[1024,896]{1,0:T(8,128)(2,1)} %all-gather.4.cloned.1.call-done) | copy-start | bytes 5505028
  66.5 9.8 %collective-permute-start.2 = (bf16[8,224,256]{2,1,0:T(8,128)(2,1)S(1)}, bf16[8,224,256]{2,1,0:T(8,128)(2,1)S(1)}, u32[]{:S(2)}, u32[]{:S(2)}) collective-permute-start(bf16[8,224,256]{2,1,0:T(8,128)(2,1)S(1)} %get-tuple-element.19), channel_id=1, source_target_pairs={{0,1},{1,0},{2,3},{3,2},{4,5},{5,4},{6,7},{7,6},{8,9},{9,8},{10,11... | collective-permute-start | bytes 2752520 | tf_op jit(solution)/shard_map/ppermute | solution.py:212
  77.4 28.4 %all-to-all-start.2 = ((bf16[8,224,256]{2,1,0:T(8,128)(2,1)}), bf16[8,224,256]{2,1,0:T(8,128)(2,1)}, u32[]{:S(2)}, u32[]{:S(2)}) async-start(bf16[8,224,256]{2,1,0:T(8,128)(2,1)} %scale.1), calls=%async_computation.3 | async-start | bytes 1835008 | tf_op jit(solution)/shard_map/all_to_all | solution.py:226
  81.7 1.5 %copy-start.4 = (bf16[1024,896]{1,0:T(8,128)(2,1)S(1)}, bf16[1024,896]{1,0:T(8,128)(2,1)}, u32[]{:S(2)}) copy-start(bf16[1024,896]{1,0:T(8,128)(2,1)} %all-gather.4.cloned.1.call-done) | copy-start | bytes 5505028
  83.2 24.7 %copy-start = (bf16[128,896]{1,0:T(8,128)(2,1)S(1)}, bf16[128,896]{1,0:T(8,128)(2,1)}, u32[]{:S(2)}) copy-start(bf16[128,896]{1,0:T(8,128)(2,1)} %joined.3) | copy-start | bytes 688132
  87.2 31.3 %collective-permute-start.3 = (bf16[224,896]{1,0:T(8,128)(2,1)}, bf16[224,896]{1,0:T(8,128)(2,1)S(1)}, u32[]{:S(2)}, u32[]{:S(2)}) collective-permute-start(bf16[224,896]{1,0:T(8,128)(2,1)} %get-tuple-element.24), channel_id=1, source_target_pairs={{0,128},{128,256},{256,384},{384,0},{1,129},{129,257},{257,385},{3... | collective-permute-start | bytes 1204232 | tf_op jit(solution)/shard_map/ppermute | solution.py:161
  89.9 28.6 %collective-permute-start.4 = (bf16[224,896]{1,0:T(8,128)(2,1)}, bf16[224,896]{1,0:T(8,128)(2,1)S(1)}, u32[]{:S(2)}, u32[]{:S(2)}) collective-permute-start(bf16[224,896]{1,0:T(8,128)(2,1)} %get-tuple-element.25), channel_id=1, source_target_pairs={{0,256},{128,384},{256,0},{384,128},{1,257},{129,385},{257,1},{385... | collective-permute-start | bytes 1204232 | tf_op jit(solution)/shard_map/ppermute | solution.py:161
  94.2 24.3 %collective-permute-start.5 = (bf16[224,896]{1,0:T(8,128)(2,1)}, bf16[224,896]{1,0:T(8,128)(2,1)S(1)}, u32[]{:S(2)}, u32[]{:S(2)}) collective-permute-start(bf16[224,896]{1,0:T(8,128)(2,1)} %get-tuple-element.26), channel_id=1, source_target_pairs={{0,384},{128,0},{256,128},{384,256},{1,385},{129,1},{257,129},{385... | collective-permute-start | bytes 1204232 | tf_op jit(solution)/shard_map/ppermute | solution.py:161
  107.2 16.1 %collective-permute-start.6 = (bf16[224,256]{1,0:T(8,128)(2,1)S(1)}, bf16[224,256]{1,0:T(8,128)(2,1)S(1)}, u32[]{:S(2)}, u32[]{:S(2)}) collective-permute-start(bf16[224,256]{1,0:T(8,128)(2,1)S(1)} %reduce_sum.12), channel_id=1, source_target_pairs={{0,0},{2,2},{4,128},{6,130},{8,256},{10,258},{12,384},{14,386},{12... | collective-permute-start | bytes 344072 | tf_op jit(solution)/shard_map/ppermute | solution.py:232
  107.9 0.9 copy-start.2
  109.8 13.5 %all-to-all-start.3 = ((f32[8,1,128]{2,1,0:T(1,128)}), f32[8,1,128]{2,1,0:T(1,128)S(1)}, u32[]{:S(2)}, u32[]{:S(2)}) async-start(f32[8,1,128]{2,1,0:T(1,128)} %get-tuple-element.21), calls=%async_computation.4 | async-start | bytes 8192 | tf_op jit(solution)/shard_map/all_to_all | solution.py:153
Sparse Core Ops, SparseCore 0:
  10.1 45.6 all-gather.3
  61.7 40.9 reduce-scatter.1

commit v7 on v6

--- a/solution.py
+++ b/solution.py
@@ -51,7 +51,7 @@
     return copies
 
 
-def input_grad_kernel(own, other, weight, grad, cot, sems):
+def input_grad_kernel(own, other, weight, gain, grad, cot, sems):
     wait_all(start_all(cot_copies(own, other, cot, sems)))
     for j in range(4):
         part = lax.dot_general(
@@ -196,9 +196,9 @@
         "input_grad",
         ((bricks, BF16),),
         flops,
-        [ANY, ANY, VMEM],
+        [ANY, ANY, VMEM, VMEM],
         scratch=[scratch[0], scratch[3]],
-    )(own, other, weight)
+    )(own, other, weight, gain)
     grad = lax.psum_scatter(grad, "z")
 
     keep, send, squares = kernel(

time: 133 us -> 133 us (level)
  waiting for transfers between devices: 16.1 us -> 18 us
    all_to_all x1, waiting for transfers between devices: 8.56 us -> 10.4 us  [per_device(): parts = lax.all_to_all(both, 'y', 0, 0)]
    all_to_all x1, starting transfers between devices: 8.73 us -> 6.84 us  [over_half(): return lax.all_to_all(copies, ('y', 'c'), 0, 0, axis_index_groups=groups)]
where the time goes in v7:
time: 133 us; the launch traced here: 132 us
  starting transfers between devices  43.9 us (33%)
  blocking collectives  32.6 us (25%)
  waiting for transfers between devices  18 us (14%)
  Pallas kernels  15.8 us (12%)
  between operations  14.2 us (11%)
  local copies, waits for them, and re-layouts  5.75 us (4%)
    all_gather x1, blocking collectives, per_device(): own = lax.all_gather(cot, 'y')  25 us
    all_to_all x1, starting transfers between devices, per_device(): weight = lax.all_to_all(weight, 'x', 0, 0).reshape(square)  10.8 us
    ppermute x3, starting transfers between devices, shifted(): return lax.ppermute(value, 'x', [(i, (i + k) % NX) for i in range(NX)])  10.5 us
    all_to_all x1, waiting for transfers between devices, per_device(): parts = lax.all_to_all(both, 'y', 0, 0)  10.4 us
    all_to_all x1, blocking collectives, over_half(): return lax.all_to_all(copies, ('y', 'c'), 0, 0, axis_index_groups=groups)  7.63 us
    ppermute x1, starting transfers between devices, per_device(): other = lax.ppermute(own, 'c', swap)  6.87 us
    all_to_all x1, starting transfers between devices, over_half(): return lax.all_to_all(copies, ('y', 'c'), 0, 0, axis_index_groups=groups)  6.84 us
    unnamed x13, local copies, waits for them, and re-layouts  5.75 us
  transfers between devices with their start and end apart: 12, of which 3 were waited for; matrix products, arithmetic and copies ran while one was open for 2% of the time, Pallas kernels for 11%

profile of v7, /device:TPU:1, one launch (start us, length us, event | category | flops | bytes accessed | tf_op | source)
XLA Modules:
  0.0 131.6 jit_solution(11677499231040851051)
XLA Ops:
  7.2 0.0 all-gather.4.cloned.1.call-start
  7.2 0.7 all-gather.4.cloned.1.call-update
  7.9 1.6 %collective-permute-start = (bf16[224,256]{1,0:T(8,128)(2,1)}, bf16[224,256]{1,0:T(8,128)(2,1)S(1)}, u32[]{:S(2)}, u32[]{:S(2)}) collective-permute-start(bf16[224,256]{1,0:T(8,128)(2,1)} %bitcast.14), channel_id=1, source_target_pairs={{0,0},{2,2},{4,128},{6,130},{8,256},{10,258},{12,384},{14,386},{12... | collective-permute-start | bytes 344072 | tf_op jit(solution)/shard_map/ppermute | solution.py:183
  9.5 0.8 copy.8.exponents
  10.3 1.0 copy-done.1
  11.3 1.5 %scaled_weight.1 = bf16[4,224,896]{2,1,0:T(8,128)(2,1)} custom-call(bf16[224,896]{1,0:T(8,128)(2,1)S(1)} %copy-done.1, s32[224,7]{1,0:T(8,128)S(1)} %copy.8.exponents), custom_call_target="tpu_custom_call" | custom-call | flops 802816 | bytes 6291456 | tf_op jit(solution)/shard_map/scaled_weight/pallas_call | solution.py:185
  12.8 10.8 %all-to-all-start = ((bf16[4,224,896]{2,1,0:T(8,128)(2,1)}), bf16[4,224,896]{2,1,0:T(8,128)(2,1)S(1)}, u32[]{:S(2)}, u32[]{:S(2)}) async-start(bf16[4,224,896]{2,1,0:T(8,128)(2,1)} %scaled_weight.1), calls=%async_computation | async-start | bytes 3211264 | tf_op jit(solution)/shard_map/all_to_all | solution.py:188
  23.6 25.0 %all-gather.1 = bf16[1792,256]{1,0:T(8,128)(2,1)S(1)} all-gather(bf16[224,256]{1,0:T(8,128)(2,1)S(1)} %collective-permute-done), channel_id=3, replica_groups=mesh['x'=4,'z'=8,'y'=8,'c'=2] {'y'}, dimensions={0}, use_global_device_ids=true | all-gather | bytes 1032192 | tf_op jit(solution)/shard_map/all_gather | solution.py:190
  48.5 6.9 %collective-permute-start.1 = (bf16[8,224,256]{2,1,0:T(8,128)(2,1)S(1)}, bf16[8,224,256]{2,1,0:T(8,128)(2,1)S(1)}, u32[]{:S(2)}, u32[]{:S(2)}) collective-permute-start(bf16[8,224,256]{2,1,0:T(8,128)(2,1)S(1)} %bitcast.8), channel_id=1, source_target_pairs={{0,1},{1,0},{2,3},{3,2},{4,5},{5,4},{6,7},{7,6},{8,9},{9,8},{10,11... | collective-permute-start | bytes 2752520 | tf_op jit(solution)/shard_map/ppermute | solution.py:191
  55.4 2.1 %collective-permute-done.1.other = bf16[8,224,256]{2,1,0:T(8,128)(2,1)S(1)} collective-permute-done((bf16[8,224,256]{2,1,0:T(8,128)(2,1)S(1)}, bf16[8,224,256]{2,1,0:T(8,128)(2,1)S(1)}, u32[]{:S(2)}, u32[]{:S(2)}) %collective-permute-start.1) | collective-permute-done | bytes 917536 | tf_op jit(solution)/shard_map/ppermute | solution.py:191
  57.5 4.0 %input_grad.1 = bf16[8,128,896]{2,1,0:T(8,128)(2,1)} custom-call(bf16[8,224,256]{2,1,0:T(8,128)(2,1)S(1)} %bitcast.9, bf16[8,224,256]{2,1,0:T(8,128)(2,1)S(1)} %collective-permute-done.1.other, bf16[896,896]{1,0:T(8,128)(2,1)S(1)} %bitcast.6, f32[1,896]{1,0:T(1,128)S(1)} %broadcast_in_dim.3.gain), custom_call_target="tpu_custom_call" | custom-call | flops 1644167168 | bytes 6291456 | tf_op jit(solution)/shard_map/input_grad/pallas_call | solution.py:194
  61.5 0.0 all-gather.4.cloned.1.call-done
  61.6 1.5 %copy-done.3 = bf16[1024,896]{1,0:T(8,128)(2,1)S(1)} copy-done((bf16[1024,896]{1,0:T(8,128)(2,1)S(1)}, bf16[1024,896]{1,0:T(8,128)(2,1)}, u32[]{:S(2)}) %copy-start.3) | copy-done | bytes 1835032
  63.1 2.8 %forward.1 = (bf16[8,224,256]{2,1,0:T(8,128)(2,1)S(1)}, bf16[8,224,256]{2,1,0:T(8,128)(2,1)S(1)}, f32[8,8,128]{2,1,0:T(8,128)S(1)}) custom-call(bf16[8,128,896]{2,1,0:T(8,128)(2,1)S(1)} %bitcast.12, f32[1,896]{1,0:T(1,128)S(1)} %broadcast_in_dim.3.gain, bf16[896,896]{1,0:T(8,128)(2,1)S(1)} %bitcast.7), custom_call_target="tpu_custom_call" | custom-call | flops 1644167168 | bytes 6291456 | tf_op jit(solution)/shard_map/forward/pallas_call | solution.py:204
  65.8 2.3 %collective-permute-start.2 = (bf16[8,224,256]{2,1,0:T(8,128)(2,1)S(1)}, bf16[8,224,256]{2,1,0:T(8,128)(2,1)S(1)}, u32[]{:S(2)}, u32[]{:S(2)}) collective-permute-start(bf16[8,224,256]{2,1,0:T(8,128)(2,1)S(1)} %get-tuple-element.19), channel_id=1, source_target_pairs={{0,1},{1,0},{2,3},{3,2},{4,5},{5,4},{6,7},{7,6},{8,9},{9,8},{10,11... | collective-permute-start | bytes 2752520 | tf_op jit(solution)/shard_map/ppermute | solution.py:212
  68.1 7.6 %all_to_all.20.ss = f32[8,8,128]{2,1,0:T(8,128)S(1)} all-to-all(f32[8,8,128]{2,1,0:T(8,128)S(1)} %get-tuple-element.17), channel_id=1, replica_groups={{0,1,2,3,4,5,6,7},{8,9,10,11,12,13,14,15},{16,17,18,19,20,21,22,23},{24..., dimensions={0} | all-to-all | bytes 65536 | tf_op jit(solution)/shard_map/all_to_all | solution.py:153
  75.7 1.2 scale.1
  77.0 4.3 %all-to-all-start.2 = ((bf16[8,224,256]{2,1,0:T(8,128)(2,1)}), bf16[8,224,256]{2,1,0:T(8,128)(2,1)}, u32[]{:S(2)}, u32[]{:S(2)}) async-start(bf16[8,224,256]{2,1,0:T(8,128)(2,1)} %scale.1), calls=%async_computation.3 | async-start | bytes 1835008 | tf_op jit(solution)/shard_map/all_to_all | solution.py:226
  81.3 1.5 %copy-done.4 = bf16[1024,896]{1,0:T(8,128)(2,1)S(1)} copy-done((bf16[1024,896]{1,0:T(8,128)(2,1)S(1)}, bf16[1024,896]{1,0:T(8,128)(2,1)}, u32[]{:S(2)}) %copy-start.4) | copy-done | bytes 1835032
  82.8 4.0 %weight_grad.1 = (f32[224,896]{1,0:T(8,128)S(1)}, bf16[224,896]{1,0:T(8,128)(2,1)}, bf16[224,896]{1,0:T(8,128)(2,1)}, bf16[224,896]{1,0:T(8,128)(2,1)}) custom-call(f32[8,8,128]{2,1,0:T(8,128)S(1)} %all_to_all.20.ss, f32[1,896]{1,0:T(1,128)S(1)} %broadcast_in_dim.3.gain, bf16[8,224,256]{2,1,0:T(8,128)(2,1)S(1)} %bitcast.10, ...), custom_call_target="tpu_custom_call" | custom-call | flops 1644167168 | bytes 6291456 | tf_op jit(solution)/shard_map/weight_grad/pallas_call | solution.py:215
  86.8 3.1 %collective-permute-start.3 = (bf16[224,896]{1,0:T(8,128)(2,1)}, bf16[224,896]{1,0:T(8,128)(2,1)S(1)}, u32[]{:S(2)}, u32[]{:S(2)}) collective-permute-start(bf16[224,896]{1,0:T(8,128)(2,1)} %get-tuple-element.24), channel_id=1, source_target_pairs={{0,128},{128,256},{256,384},{384,0},{1,129},{129,257},{257,385},{3... | collective-permute-start | bytes 1204232 | tf_op jit(solution)/shard_map/ppermute | solution.py:161
  89.9 4.3 %collective-permute-start.4 = (bf16[224,896]{1,0:T(8,128)(2,1)}, bf16[224,896]{1,0:T(8,128)(2,1)S(1)}, u32[]{:S(2)}, u32[]{:S(2)}) collective-permute-start(bf16[224,896]{1,0:T(8,128)(2,1)} %get-tuple-element.25), channel_id=1, source_target_pairs={{0,256},{128,384},{256,0},{384,128},{1,257},{129,385},{257,1},{385... | collective-permute-start | bytes 1204232 | tf_op jit(solution)/shard_map/ppermute | solution.py:161
  94.2 3.1 %collective-permute-start.5 = (bf16[224,896]{1,0:T(8,128)(2,1)}, bf16[224,896]{1,0:T(8,128)(2,1)S(1)}, u32[]{:S(2)}, u32[]{:S(2)}) collective-permute-start(bf16[224,896]{1,0:T(8,128)(2,1)} %get-tuple-element.26), channel_id=1, source_target_pairs={{0,384},{128,0},{256,128},{384,256},{1,385},{129,1},{257,129},{385... | collective-permute-start | bytes 1204232 | tf_op jit(solution)/shard_map/ppermute | solution.py:161
  97.3 10.4 %all-to-all-done.2 = bf16[8,224,256]{2,1,0:T(8,128)(2,1)} async-done(((bf16[8,224,256]{2,1,0:T(8,128)(2,1)}), bf16[8,224,256]{2,1,0:T(8,128)(2,1)}, u32[]{:S(2)}, u32[]{:S(2)}) %all-to-all-start.2) | async-done | bytes 917536 | tf_op jit(solution)/shard_map/all_to_all | solution.py:226
  107.8 1.3 reduce_sum.12
  109.1 0.0 reduce-scatter.2.cloned.1.call-done
  109.1 0.7 collective-permute-start.6
  109.8 0.9 copy-done.2
  110.7 0.9 dots.1
  111.7 6.8 %all-to-all-start.3 = ((f32[8,1,128]{2,1,0:T(1,128)}), f32[8,1,128]{2,1,0:T(1,128)S(1)}, u32[]{:S(2)}, u32[]{:S(2)}) async-start(f32[8,1,128]{2,1,0:T(1,128)} %get-tuple-element.21), calls=%async_computation.4 | async-start | bytes 8192 | tf_op jit(solution)/shard_map/all_to_all | solution.py:153
  118.5 4.8 %all-to-all-done.3.dots = f32[8,1,128]{2,1,0:T(1,128)S(1)} async-done(((f32[8,1,128]{2,1,0:T(1,128)}), f32[8,1,128]{2,1,0:T(1,128)S(1)}, u32[]{:S(2)}, u32[]{:S(2)}) %all-to-all-start.3) | async-done | bytes 4128 | tf_op jit(solution)/shard_map/all_to_all | solution.py:153
  123.3 1.5 %last.1 = (bf16[128,896]{1,0:T(8,128)(2,1)}, f32[224,896]{1,0:T(8,128)}, bf16[224,256]{1,0:T(8,128)(2,1)}) custom-call(f32[8,8,128]{2,1,0:T(8,128)S(1)} %all_to_all.20.ss, f32[8,1,128]{2,1,0:T(1,128)S(1)} %all-to-all-done.3.dots, bf16[128,896]{1,0:T(8,128)(2,1)S(1)} %get-tuple-element.22.grad, bf16[128,896]{1,0:T(8,128)(2,1)S(1)} %copy-done, ...), custom_call_target="tpu_custom_call" | custom-call | flops 917504 | bytes 6291456 | tf_op jit(solution)/shard_map/last/pallas_call | solution.py:234
  (18 shorter events, 0.1 us)
Async XLA Ops:
  7.2 54.4 %all-gather.4.cloned.1.call-start = ((), (), s32[]{:S(2)}) async-start(), calls=%async_computation.6 | async-start | bytes 2064384 | tf_op jit(solution)/shard_map/all_gather | solution.py:182
  7.9 15.7 %collective-permute-start = (bf16[224,256]{1,0:T(8,128)(2,1)}, bf16[224,256]{1,0:T(8,128)(2,1)S(1)}, u32[]{:S(2)}, u32[]{:S(2)}) collective-permute-start(bf16[224,256]{1,0:T(8,128)(2,1)} %bitcast.14), channel_id=1, source_target_pairs={{0,0},{2,2},{4,128},{6,130},{8,256},{10,258},{12,384},{14,386},{12... | collective-permute-start | bytes 344072 | tf_op jit(solution)/shard_map/ppermute | solution.py:183
  10.3 1.0 copy-start.1
  12.8 42.7 %copy-start.5 = (f32[896]{0:T(1024)S(1)}, f32[896]{0:T(1024)}, u32[]{:S(2)}) copy-start(f32[896]{0:T(1024)} %param.6) | copy-start | bytes 10756
  12.8 44.7 %all-to-all-start = ((bf16[4,224,896]{2,1,0:T(8,128)(2,1)}), bf16[4,224,896]{2,1,0:T(8,128)(2,1)S(1)}, u32[]{:S(2)}, u32[]{:S(2)}) async-start(bf16[4,224,896]{2,1,0:T(8,128)(2,1)} %scaled_weight.1), calls=%async_computation | async-start | bytes 3211264 | tf_op jit(solution)/shard_map/all_to_all | solution.py:188
  23.6 85.5 %reduce-scatter.2.cloned.1.call-start = ((), (), s32[]{:S(2)}) async-start(), calls=%async_computation.5 | async-start | bytes 2064384 | tf_op jit(solution)/shard_map/reduce_scatter | solution.py:202
  48.5 9.0 %collective-permute-start.1 = (bf16[8,224,256]{2,1,0:T(8,128)(2,1)S(1)}, bf16[8,224,256]{2,1,0:T(8,128)(2,1)S(1)}, u32[]{:S(2)}, u32[]{:S(2)}) collective-permute-start(bf16[8,224,256]{2,1,0:T(8,128)(2,1)S(1)} %bitcast.8), channel_id=1, source_target_pairs={{0,1},{1,0},{2,3},{3,2},{4,5},{5,4},{6,7},{7,6},{8,9},{9,8},{10,11... | collective-permute-start | bytes 2752520 | tf_op jit(solution)/shard_map/ppermute | solution.py:191
  61.6 1.5 %copy-start.3 = (bf16[1024,896]{1,0:T(8,128)(2,1)S(1)}, bf16[1024,896]{1,0:T(8,128)(2,1)}, u32[]{:S(2)}) copy-start(bf16[1024,896]{1,0:T(8,128)(2,1)} %all-gather.4.cloned.1.call-done) | copy-start | bytes 5505028
  65.8 9.9 %collective-permute-start.2 = (bf16[8,224,256]{2,1,0:T(8,128)(2,1)S(1)}, bf16[8,224,256]{2,1,0:T(8,128)(2,1)S(1)}, u32[]{:S(2)}, u32[]{:S(2)}) collective-permute-start(bf16[8,224,256]{2,1,0:T(8,128)(2,1)S(1)} %get-tuple-element.19), channel_id=1, source_target_pairs={{0,1},{1,0},{2,3},{3,2},{4,5},{5,4},{6,7},{7,6},{8,9},{9,8},{10,11... | collective-permute-start | bytes 2752520 | tf_op jit(solution)/shard_map/ppermute | solution.py:212
  77.0 30.8 %all-to-all-start.2 = ((bf16[8,224,256]{2,1,0:T(8,128)(2,1)}), bf16[8,224,256]{2,1,0:T(8,128)(2,1)}, u32[]{:S(2)}, u32[]{:S(2)}) async-start(bf16[8,224,256]{2,1,0:T(8,128)(2,1)} %scale.1), calls=%async_computation.3 | async-start | bytes 1835008 | tf_op jit(solution)/shard_map/all_to_all | solution.py:226
  81.3 1.5 %copy-start.4 = (bf16[1024,896]{1,0:T(8,128)(2,1)S(1)}, bf16[1024,896]{1,0:T(8,128)(2,1)}, u32[]{:S(2)}) copy-start(bf16[1024,896]{1,0:T(8,128)(2,1)} %all-gather.4.cloned.1.call-done) | copy-start | bytes 5505028
  82.8 27.0 %copy-start = (bf16[128,896]{1,0:T(8,128)(2,1)S(1)}, bf16[128,896]{1,0:T(8,128)(2,1)}, u32[]{:S(2)}) copy-start(bf16[128,896]{1,0:T(8,128)(2,1)} %joined.3) | copy-start | bytes 688132
  86.8 31.7 %collective-permute-start.3 = (bf16[224,896]{1,0:T(8,128)(2,1)}, bf16[224,896]{1,0:T(8,128)(2,1)S(1)}, u32[]{:S(2)}, u32[]{:S(2)}) collective-permute-start(bf16[224,896]{1,0:T(8,128)(2,1)} %get-tuple-element.24), channel_id=1, source_target_pairs={{0,128},{128,256},{256,384},{384,0},{1,129},{129,257},{257,385},{3... | collective-permute-start | bytes 1204232 | tf_op jit(solution)/shard_map/ppermute | solution.py:161
  89.9 28.6 %collective-permute-start.4 = (bf16[224,896]{1,0:T(8,128)(2,1)}, bf16[224,896]{1,0:T(8,128)(2,1)S(1)}, u32[]{:S(2)}, u32[]{:S(2)}) collective-permute-start(bf16[224,896]{1,0:T(8,128)(2,1)} %get-tuple-element.25), channel_id=1, source_target_pairs={{0,256},{128,384},{256,0},{384,128},{1,257},{129,385},{257,1},{385... | collective-permute-start | bytes 1204232 | tf_op jit(solution)/shard_map/ppermute | solution.py:161
  94.2 24.3 %collective-permute-start.5 = (bf16[224,896]{1,0:T(8,128)(2,1)}, bf16[224,896]{1,0:T(8,128)(2,1)S(1)}, u32[]{:S(2)}, u32[]{:S(2)}) collective-permute-start(bf16[224,896]{1,0:T(8,128)(2,1)} %get-tuple-element.26), channel_id=1, source_target_pairs={{0,384},{128,0},{256,128},{384,256},{1,385},{129,1},{257,129},{385... | collective-permute-start | bytes 1204232 | tf_op jit(solution)/shard_map/ppermute | solution.py:161
  109.1 14.2 %collective-permute-start.6 = (bf16[224,256]{1,0:T(8,128)(2,1)S(1)}, bf16[224,256]{1,0:T(8,128)(2,1)S(1)}, u32[]{:S(2)}, u32[]{:S(2)}) collective-permute-start(bf16[224,256]{1,0:T(8,128)(2,1)S(1)} %reduce_sum.12), channel_id=1, source_target_pairs={{0,0},{2,2},{4,128},{6,130},{8,256},{10,258},{12,384},{14,386},{12... | collective-permute-start | bytes 344072 | tf_op jit(solution)/shard_map/ppermute | solution.py:232
  109.8 0.9 copy-start.2
  111.7 11.6 %all-to-all-start.3 = ((f32[8,1,128]{2,1,0:T(1,128)}), f32[8,1,128]{2,1,0:T(1,128)S(1)}, u32[]{:S(2)}, u32[]{:S(2)}) async-start(f32[8,1,128]{2,1,0:T(1,128)} %get-tuple-element.21), calls=%async_computation.4 | async-start | bytes 8192 | tf_op jit(solution)/shard_map/all_to_all | solution.py:153
Sparse Core Ops, SparseCore 0:
  10.1 45.6 all-gather.3
  61.6 40.9 reduce-scatter.1
